TPU v7x, 128 devices: a whole 4x4x4 slice. The times are simulated.
128 devices in a mesh: dp: 32 (over y, z, core), expert: 4 (over x).
Axes of the slice: x: 4, y: 4, z: 4, core: 2. Of those that a mesh axis runs over, the one named last changes fastest.
Arguments:
- tokens: bfloat16 [32768, 7168], P(('dp', 'expert')), may hold values from -6 to 6
- routes: int32 [32768, 8], P(('dp', 'expert')), may hold values from 0 to 255, as said below
- slot_ids: int32 [32768, 8], P(('dp', 'expert')), may hold values from -1 to 15, as said below
- gate_weight: bfloat16 [4, 2048, 7168], P('expert', 'dp'), may hold values from -0.0625 to 0.0625
- up_weight: bfloat16 [4, 2048, 7168], P('expert', 'dp'), may hold values from -0.0625 to 0.0625
Outputs:
- input_hessian: float32 [4, 7168, 7168], P('expert', 'dp')
- down_hessian: float32 [4, 2048, 2048], P('expert', 'dp')
Inputs may be any that keep to these rules, and one draw needn't show every extreme that they name: `routes`: distinct ids in each row. On each device, no window expert is named by more than 16 tokens, and in every group of 4 consecutive devices along dp+expert (one index of dp) some window expert is named by exactly 16 tokens on every one of them. Every window expert is named on every device. `slot_ids`: for a choice of a window expert: on each device, the tokens naming that expert hold the slots 0 to n - 1, each once; for ids of 4 or more the slot is -1.
All inputs are finite; a program needn't handle non-finite values.
Results may differ from a plain program's by a relative error of at most 0.0038.
Values may be sent and summed in bfloat16 or wider, within the bound.
No kernel may reach another device: no remote copies, remote signals or barrier semaphores. Data moves between devices by JAX's collectives and lax.ppermute only.
A program may use at most 192 MiB of HBM per device.

v0:
```python
import jax
import jax.numpy as jnp
from jax import lax
from jax.sharding import PartitionSpec as P

CAP = 16


def expert_work(rows_in, gate_rows, up_rows, first_col, col_count):
    columns = lax.dynamic_slice_in_dim(rows_in, first_col, col_count, 1)
    gram = lax.dot_general(
        columns, rows_in, (((0,), (0,)), ((), ())), preferred_element_type=jnp.float32
    )
    gate = lax.dot_general(
        gate_rows, rows_in, (((1,), (1,)), ((), ())), preferred_element_type=jnp.float32
    )
    upward = lax.dot_general(
        up_rows, rows_in, (((1,), (1,)), ((), ())), preferred_element_type=jnp.float32
    )
    hidden_t = (jax.nn.silu(gate) * upward).astype(jnp.bfloat16)
    return (gram, hidden_t)


def local(tokens, routes, slot_ids, gate_weight, up_weight):
    width = tokens.shape[1]
    owners = lax.axis_size("expert")
    data_count = lax.axis_size("dp")
    expert_ids = jnp.arange(owners, dtype=jnp.int32)
    member = jnp.any(routes[:, :, None] == expert_ids[None, None, :], axis=1)
    local_counts = jnp.sum(member.astype(jnp.float32), axis=0)
    totals = lax.psum(local_counts, ("dp", "expert"))
    routed = jnp.take(totals, lax.axis_index("expert"))
    factor = 2.0 / routed
    slot_lanes = jnp.arange(owners * CAP, dtype=jnp.int32)
    matched = (routes[None, :, :] == (slot_lanes // CAP)[:, None, None]) & (
        slot_ids[None, :, :] == (slot_lanes % CAP)[:, None, None]
    )
    one_hot = jnp.any(matched, axis=2).astype(jnp.bfloat16)
    dispatched = jnp.dot(one_hot, tokens, preferred_element_type=jnp.float32).astype(jnp.bfloat16)
    dispatched = dispatched.reshape(owners, CAP, width)
    gate_rows = gate_weight[0]
    up_rows = up_weight[0]
    col_count = width // data_count
    first_col = lax.axis_index("dp") * col_count
    arrived = lax.all_to_all(dispatched, "expert", split_axis=0, concat_axis=1, tiled=True)[0]
    gathered = lax.all_gather(arrived, "dp", axis=0, tiled=True)
    gram, hidden_t = expert_work(gathered, gate_rows, up_rows, first_col, col_count)
    rows_t = lax.all_to_all(hidden_t, "dp", split_axis=1, concat_axis=0, tiled=True)
    down_block = lax.psum_scatter(
        lax.dot_general(
            rows_t, rows_t, (((1,), (1,)), ((), ())), preferred_element_type=jnp.float32
        ),
        "dp",
        scatter_dimension=0,
        tiled=True,
    )
    return ((gram * factor)[None], (down_block * factor)[None])


def solution(mesh):
    in_specs = (
        P(("dp", "expert"), None),
        P(("dp", "expert"), None),
        P(("dp", "expert"), None),
        P("expert", "dp", None),
        P("expert", "dp", None),
    )
    out_specs = (P("expert", "dp", None), P("expert", "dp", None))
    return jax.shard_map(local, mesh=mesh, in_specs=in_specs, out_specs=out_specs, check_vma=False)
```

profile of v0, /device:TPU:1, one launch (start us, length us, event | category | flops | bytes accessed | tf_op | source)
XLA Modules:
  0.0 307.4 jit_solution(8860785864224244251)
XLA Ops:
  7.2 0.0 copy-start
  7.2 0.0 copy-start.1
  7.2 0.0 all-gather.2.cloned.1.call-start
  7.2 1.1 and_reduce_fusion
  8.4 2.8 convolution_convert_fusion
  11.2 17.5 %all_to_all.28 = bf16[4,16,7168]{2,1,0:T(8,128)(2,1)} all-to-all(bf16[4,16,7168]{2,1,0:T(8,128)(2,1)S(1)} %bitcast.38), channel_id=1, replica_groups=mesh['dp'=32,'expert'=4] {'expert'}, dimensions={0} | all-to-all | bytes 1835008 | tf_op jit(solution)/shard_map/all_to_all | solution.py:45
  28.7 0.0 all-gather.2.cloned.1.call-update
  28.7 0.0 reduce-scatter.2.cloned.1.call-start
  28.8 105.3 %all-gather.2.cloned.1.call-done = bf16[2048,7168]{1,0:T(8,128)(2,1)} async-done(((bf16[64,7168]{1,0:T(8,128)(2,1)}), bf16[2048,7168]{1,0:T(8,128)(2,1)}) %all-gather.2.cloned.1.call-update) | async-done | bytes 29360144 | tf_op jit(solution)/shard_map/all_gather | solution.py:46
  134.0 0.0 copy-done
  134.1 14.3 %convolution_bitcast_fusion.1 = f32[64,2048]{1,0:T(8,128)S(1)} fusion(bf16[2048,7168]{1,0:T(8,128)(2,1)} %all-gather.2.cloned.1.call-done, bf16[1,64,7168]{2,1,0:T(8,128)(2,1)S(1)} %copy-done), kind=kOutput, calls=%fused_computation.4 | convolution fusion | flops 1879048192 | bytes 30801920 | tf_op jit(solution)/shard_map/dot_general | solution.py:14
  148.4 0.0 copy-done.1
  148.4 0.0 copy-start.2
  148.4 14.3 %fusion.2 = bf16[64,2048]{1,0:T(8,128)(2,1)S(1)} fusion(bf16[2048,7168]{1,0:T(8,128)(2,1)} %all-gather.2.cloned.1.call-done, bf16[1,64,7168]{2,1,0:T(8,128)(2,1)S(1)} %copy-done.1, f32[64,2048]{1,0:T(8,128)S(1)} %convolution_bitcast_fusion.1), kind=kOutput, calls=%fused_computation.6 | convolution fusion | flops 1879834624 | bytes 31064064 | tf_op jit(solution)/shard_map/dot_general | solution.py:17
  162.7 0.3 copy.21
  163.0 0.4 reshape.72
  163.4 14.1 %all_to_all.29 = bf16[32,2,2048]{2,1,0:T(2,128)(2,1)S(1)} all-to-all(bf16[32,2,2048]{2,1,0:T(2,128)(2,1)S(1)} %reshape.72), channel_id=1, replica_groups=mesh['dp'=32,'expert'=4] {'dp'}, dimensions={0} | all-to-all | bytes 524288 | tf_op jit(solution)/shard_map/all_to_all | solution.py:48
  177.5 0.4 reshape.73
  177.9 0.3 copy.20
  178.2 0.5 all_to_all.25
  178.7 8.1 %fusion.8 = f32[2048,2048]{1,0:T(8,128)} fusion(bf16[2048,64]{0,1:T(8,128)(2,1)S(1)} %all_to_all.25), kind=kOutput, calls=%fused_computation.22 | convolution fusion | flops 536870912 | bytes 17039360 | tf_op jit(solution)/shard_map/dot_general | solution.py:50
  186.8 0.0 reduce-scatter.2.cloned.1.call-update
  186.8 0.0 copy-done.2
  186.8 0.1 convert_reduce_fusion
  187.0 64.8 %psum.7 = f32[4]{0:T(128)S(1)} all-reduce(f32[4]{0:T(128)S(1)} %convert_reduce_fusion), channel_id=1, replica_groups=mesh['dp'=32,'expert'=4] {'dp','expert'}, use_global_device_ids=true, to_apply=%region_3.4 | all-reduce | flops 4 | bytes 32 | tf_op jit(solution)/shard_map/psum | solution.py:31
  251.8 0.6 dynamic-slice.2
  253.1 17.4 %fusion = f32[1,224,7168]{2,1,0:T(8,128)} fusion(bf16[2048,7168]{1,0:T(8,128)(2,1)} %all-gather.2.cloned.1.call-done, f32[]{:T(128)} %bitcast.3, s32[]{:T(128)S(6)} %select_n.33), kind=kOutput, calls=%fused_computation.1 | convolution fusion | flops 6578274304 | bytes 36831748 | tf_op jit(solution)/shard_map/dot_general | solution.py:11
  270.5 28.2 %reduce-scatter.2.cloned.1.call-done = f32[64,2048]{1,0:T(8,128)} async-done(((f32[2048,2048]{1,0:T(8,128)}), f32[64,2048]{1,0:T(8,128)}) %reduce-scatter.2.cloned.1.call-update) | async-done | bytes 524304 | tf_op jit(solution)/shard_map/reduce_scatter | solution.py:49
  298.7 1.9 multiply_bitcast_fusion
  (3 shorter events, 0.1 us)
Async XLA Ops:
  7.2 126.9 %copy-start = (bf16[1,64,7168]{2,1,0:T(8,128)(2,1)S(1)}, bf16[1,64,7168]{2,1,0:T(8,128)(2,1)}, u32[]{:S(2)}) copy-start(bf16[1,64,7168]{2,1,0:T(8,128)(2,1)} %param.8) | copy-start | bytes 2752516
  7.2 141.2 %copy-start.1 = (bf16[1,64,7168]{2,1,0:T(8,128)(2,1)S(1)}, bf16[1,64,7168]{2,1,0:T(8,128)(2,1)}, u32[]{:S(2)}) copy-start(bf16[1,64,7168]{2,1,0:T(8,128)(2,1)} %param.9) | copy-start | bytes 2752516
  7.2 126.9 %all-gather.2.cloned.1.call-start = ((), (), s32[]{:S(2)}) async-start(), calls=%async_computation.3 | async-start | bytes 30277632 | tf_op jit(solution)/shard_map/all_gather | solution.py:46
  28.7 270.0 %reduce-scatter.2.cloned.1.call-start = ((), (), s32[]{:S(2)}) async-start(), calls=%async_computation.4 | async-start | bytes 17301504 | tf_op jit(solution)/shard_map/reduce_scatter | solution.py:49
  148.4 38.4 %copy-start.2 = (s32[256,8]{0,1:T(8,128)S(1)}, s32[256,8]{0,1:T(8,128)}, u32[]{:S(2)}) copy-start(s32[256,8]{0,1:T(8,128)} %param.6) | copy-start | bytes 24580
Sparse Core Ops, SparseCore 0:
  28.8 105.1 all-gather.1
  186.9 111.6 reduce-scatter.1
where the time goes:
time: 308 us; the launch traced here: 307 us
  waiting for transfers between devices  134 us (44%)
  blocking collectives  96.4 us (31%)
  matrix products  57 us (19%)
  between operations  14.8 us (5%)
  other arithmetic  3.13 us (1%)
    all_gather x1, waiting for transfers between devices, local(): gathered = lax.all_gather(arrived, 'dp', axis=0, tiled=True)  105 us
    psum x1, blocking collectives, local(): totals = lax.psum(local_counts, ('dp', 'expert'))  64.8 us
    reduce_scatter x1, waiting for transfers between devices, local(): lax.psum_scatter(lax.dot_general(rows_t, rows_t, (((1,), (1,)), ((), ()))...  28.2 us
    all_to_all x1, blocking collectives, local(): lax.all_to_all(dispatched, 'expert', split_axis=0, concat_axis=1, tiled=T...  17.5 us
    dot_general x1, matrix products, expert_work(): lax.dot_general(columns, rows_in, (((0,), (0,)), ((), ())), preferred_ele...  17.4 us
    dot_general x1, matrix products, expert_work(): lax.dot_general(up_rows, rows_in, (((1,), (1,)), ((), ())), preferred_ele...  14.3 us
    dot_general x1, matrix products, expert_work(): lax.dot_general(gate_rows, rows_in, (((1,), (1,)), ((), ())), preferred_e...  14.3 us
    all_to_all x1, blocking collectives, local(): lax.all_to_all(hidden_t, 'dp', split_axis=1, concat_axis=0, tiled=True)  14.1 us
  transfers between devices with their start and end apart: 2, of which 2 were waited for; matrix products, arithmetic and copies ran while one was open for 6% of the time, Pallas kernels for 0%

commit v1 on v0

v1 whole, which is shorter than its diff:
```python
import functools

import jax
import jax.numpy as jnp
from jax import lax
from jax.experimental import pallas as pl
from jax.experimental.pallas import tpu as pltpu
from jax.sharding import PartitionSpec as P

CAP = 16
WIDTH = 7168
FLAG = 128
SENT = WIDTH + FLAG
FF = 2048
SIDE = 4
CHIPS = 16
GRAM_ROWS = 448
WINDOW = 512
F32 = jnp.float32
BF16 = jnp.bfloat16
ORIGIN = (0, -1, 1, 2)
VMEM = pl.BlockSpec(memory_space=pltpu.VMEM)
SMEM = pl.BlockSpec(memory_space=pltpu.SMEM)
PARAMS = pltpu.CompilerParams(vmem_limit_bytes=60 * 1024 * 1024)


def device(y, z, core):
    return ((y % SIDE) * SIDE + z % SIDE) * 2 + core


def steps(first, second):
    return [
        (device(y, z, core), device(y + move[0], z + move[1], core))
        for y in range(SIDE)
        for z in range(SIDE)
        for core, move in enumerate((first, second))
    ]


def major(value, step):
    return lax.ppermute(value, "dp", steps((step, 0), (0, step)))


def minor(value, step):
    return lax.ppermute(value, "dp", steps((0, step), (step, 0)))


def along_y(value, step):
    return lax.ppermute(value, "dp", steps((step, 0), (step, 0)))


def along_z(value, step):
    return lax.ppermute(value, "dp", steps((0, step), (0, step)))


def sibling(value):
    return lax.ppermute(value, "dp", [(i, i ^ 1) for i in range(2 * CHIPS)])


def ring(value, move):
    half = value.shape[0] // 2
    up = move(value, 1)
    down = move(value, -1)
    return (up, down, move(up[:half], 1), move(down[half:], -1))


def dispatch_kernel(where, routes, slots, tokens, *outs):
    wanted = jnp.where(routes[...] < 4, routes[...] * CAP + slots[...], -1)
    lane = lax.broadcasted_iota(jnp.int32, (4 * CAP, 1), 0)
    target = ((lane // CAP + where[0]) % 4) * CAP + lane % CAP
    hit = wanted[0:1, :] == target
    for k in range(1, 8):
        hit = hit | (wanted[k : k + 1, :] == target)
    one_hot = hit.astype(F32).astype(BF16)
    flag = jnp.max(hit.astype(F32), axis=1, keepdims=True)
    flag = jnp.broadcast_to(flag, (4 * CAP, FLAG)).astype(BF16)
    for start in range(0, WIDTH, 1024):
        rows = jnp.dot(
            one_hot, tokens[:, start : start + 1024], preferred_element_type=F32
        ).astype(BF16)
        for j, out in enumerate(outs):
            out[:, start : start + 1024] = rows[j * CAP : (j + 1) * CAP]
    for j, out in enumerate(outs):
        out[:, WIDTH:] = flag[j * CAP : (j + 1) * CAP]


def dispatch(where, routes, slots, tokens):
    return pl.pallas_call(
        dispatch_kernel,
        out_shape=[jax.ShapeDtypeStruct((CAP, SENT), BF16)] * 4,
        in_specs=[SMEM, VMEM, VMEM, VMEM],
        out_specs=[VMEM] * 4,
        compiler_params=PARAMS,
    )(where, routes.T, slots.T, tokens)


def hidden_kernel(where, p0, p1, p2, p3, p4, g, gs, u, us, hidden, window, count):
    pieces = (p0, p1, p2, p3, p4)
    base = pl.multiple_of(where[0], 128)
    total = jnp.zeros((256, 256), F32)
    for start in range(0, WIDTH, 1024):
        rows = jnp.concatenate([p[:, start : start + 1024] for p in pieces], 0)
        weights = jnp.concatenate([w[:, start : start + 1024] for w in (g, gs, u, us)], 0)
        total += lax.dot_general(
            rows, weights, (((1,), (1,)), ((), ())), preferred_element_type=F32
        )
    gate, upward = total[:, :128], total[:, 128:]
    value = gate / (1.0 + jnp.exp(-gate)) * upward
    value = jnp.where(where[1] == 1, pltpu.roll(value, 64, 1), value)
    hidden[...] = value.astype(BF16)
    window[...] = jnp.concatenate([p[:, pl.ds(base, WINDOW)] for p in pieces], 0)
    flags = jnp.concatenate([p[:, WIDTH:] for p in pieces], 0).astype(F32)
    count[...] = jnp.broadcast_to(jnp.sum(flags, axis=0, keepdims=True), (8, FLAG))


def hidden_work(where, pieces, weights):
    return pl.pallas_call(
        hidden_kernel,
        out_shape=[
            jax.ShapeDtypeStruct((256, 128), BF16),
            jax.ShapeDtypeStruct((256, WINDOW), BF16),
            jax.ShapeDtypeStruct((8, FLAG), F32),
        ],
        in_specs=[SMEM] + [VMEM] * 9,
        out_specs=[VMEM] * 3,
        compiler_params=PARAMS,
        cost_estimate=pl.CostEstimate(
            flops=2 * 256 * 256 * WIDTH, bytes_accessed=8 << 20, transcendentals=256 * 128
        ),
    )(where, *pieces, *weights)


def order_kernel(offsets, h0, h1, h2, h3, out):
    for i, h in enumerate((h0, h1, h2, h3)):
        for j in range(4):
            start = pl.multiple_of(offsets[4 * i + j], 64)
            out[pl.ds(start, 64), :] = h[64 * j : 64 * j + 64, :]


def order(offsets, parts):
    return pl.pallas_call(
        order_kernel,
        out_shape=jax.ShapeDtypeStruct((1024, 128), BF16),
        in_specs=[SMEM] + [VMEM] * 4,
        out_specs=VMEM,
        compiler_params=PARAMS,
    )(offsets, *parts)


def down_kernel(where, own, z0, z1, z2, z3, y0, y1, y2, y3, n0, n1, n2, n3, keep, send, tile):
    core = where[1]
    left = jnp.concatenate(
        [own[...], z0[...], z1[...], jnp.concatenate([z2[...], z3[...]], 0)], 1
    )
    right = jnp.concatenate(
        [own[...], y0[...], y1[...], jnp.concatenate([y2[...], y3[...]], 0)], 1
    )
    tile[...] = lax.dot_general(
        left, right, (((0,), (0,)), ((), ())), preferred_element_type=F32
    )
    for j in range(4):
        keep[64 * j : 64 * j + 64, :] = tile[pl.ds(pl.multiple_of(128 * j + 64 * core, 64), 64), :]
        send[64 * j : 64 * j + 64, :] = tile[
            pl.ds(pl.multiple_of(128 * j + 64 - 64 * core, 64), 64), :
        ]
    count = n0[...] + n1[...] + n2[...] + n3[...]
    count = jnp.concatenate([count] * 4, 1)
    keep[256:, :] = count
    send[256:, :] = count


def down_work(where, own, ring_z, ring_y, counts):
    return pl.pallas_call(
        down_kernel,
        out_shape=[jax.ShapeDtypeStruct((264, 512), F32)] * 2,
        in_specs=[SMEM] + [VMEM] * 13,
        out_specs=[VMEM] * 2,
        scratch_shapes=[pltpu.VMEM((512, 512), F32)],
        compiler_params=PARAMS,
        cost_estimate=pl.CostEstimate(
            flops=2 * 512 * 512 * 1024, bytes_accessed=4 << 20, transcendentals=0
        ),
    )(where, own, *ring_z, *ring_y, *counts)


def place_kernel(offsets, b0, b1, b2, b3, factor, out):
    for j, block in enumerate((b0, b1, b2, b3)):
        for i in range(4):
            start = pl.multiple_of(offsets[4 * j + i], 128)
            out[0, :, pl.ds(start, 128)] = block[:, 128 * i : 128 * i + 128] * factor[0, 0]


def place(offsets, blocks, factor):
    return pl.pallas_call(
        place_kernel,
        out_shape=jax.ShapeDtypeStruct((1, 64, FF), F32),
        in_specs=[SMEM] + [VMEM] * 4 + [SMEM],
        out_specs=VMEM,
        compiler_params=PARAMS,
    )(offsets, *blocks, factor)


def gram_kernel(first, count, where, w0, w1, w2, w3, *refs):
    pieces, (keep, send, left, tile) = refs[:20], refs[20:]
    core, shift = where[1], where[2]
    mine = pl.multiple_of(shift + core * 224, 32)
    other = pl.multiple_of(shift + 224 - core * 224, 32)
    for i, w in enumerate((w0, w1, w2, w3)):
        left[:, 256 * i : 256 * i + 256] = w[...].T

    @pl.loop(0, count // 512)
    def _(step):
        start = pl.multiple_of(step * 512, 512)
        here = pl.multiple_of(first + step * 512, 512)
        right = jnp.concatenate([p[:, pl.ds(here, 512)] for p in pieces], 0)
        tile[...] = jnp.dot(left[...], right, preferred_element_type=F32)
        keep[:, pl.ds(start, 512)] = tile[pl.ds(mine, 224), :]
        send[:, pl.ds(start, 512)] = tile[pl.ds(other, 224), :]


def gram_work(where, windows, pieces, first, count):
    return pl.pallas_call(
        functools.partial(gram_kernel, first, count),
        out_shape=[jax.ShapeDtypeStruct((224, count), F32)] * 2,
        in_specs=[SMEM] + [VMEM] * 24,
        out_specs=[VMEM] * 2,
        scratch_shapes=[pltpu.VMEM((WINDOW, 1024), BF16), pltpu.VMEM((WINDOW, 512), F32)],
        compiler_params=PARAMS,
        cost_estimate=pl.CostEstimate(
            flops=2 * 512 * count * 1024, bytes_accessed=8 << 20, transcendentals=0
        ),
    )(where, *windows, *pieces)


def local(tokens, routes, slot_ids, gate_weight, up_weight):
    place_dp = lax.axis_index("dp").astype(jnp.int32)
    place_x = lax.axis_index("expert").astype(jnp.int32)
    core = place_dp % 2
    chip = place_dp // 2
    z, y = chip % SIDE, chip // SIDE
    shift = (chip % 2) * 64
    where = jnp.stack([chip * GRAM_ROWS - shift, core, shift])
    minor_of = jnp.array(ORIGIN * 4, jnp.int32)
    major_of = jnp.repeat(jnp.array(ORIGIN, jnp.int32), 4)
    from_y = (y + jnp.where(core == 0, major_of, minor_of)) % SIDE
    from_z = (z + jnp.where(core == 0, minor_of, major_of)) % SIDE
    slots_at = (from_y * SIDE + from_z) * 64
    columns_at = (((y + minor_of) % SIDE) * SIDE + (z + major_of) % SIDE) * 128

    gate_own, up_own = gate_weight[0], up_weight[0]
    weights = (gate_own, sibling(gate_own), up_own, sibling(up_own))

    blocks = dispatch(place_x.reshape(1), routes, slot_ids, tokens)
    parts = [blocks[0]]
    for step in (1, 2, 3):
        parts.append(lax.ppermute(blocks[step], "expert", [(i, (i + step) % 4) for i in range(4)]))
    shard = jnp.concatenate(parts, 0)

    up, down, up2, down2 = ring(shard, major)
    groups = []
    for piece in (shard, up, down, jnp.concatenate([up2, down2], 0)):
        groups.append((piece,) + ring(piece, minor))

    hiddens, windows, counts = [], [], []
    for group in groups:
        h, w, n = hidden_work(where, group, weights)
        hiddens.append(h)
        windows.append(w)
        counts.append(n)

    hidden = order(slots_at, hiddens)
    ring_z = ring(hidden, along_z)
    ring_y = ring(hidden, along_y)
    pieces = [piece for group in groups for piece in group]
    halves = []
    for first in (0, WIDTH // 2):
        keep, send = gram_work(where, windows, pieces, first, WIDTH // 2)
        halves.append((keep, sibling(send)))

    down_keep, down_send = down_work(where, hidden, ring_z, ring_y, counts)
    summed = down_keep + sibling(down_send)
    factor = (2.0 / summed[256, 0]).reshape(1, 1)
    down_blocks = [
        summed[:64],
        along_z(summed[128:192], 1),
        along_z(summed[64:128], -1),
        along_z(summed[192:256], 2),
    ]
    down_rows = place(columns_at, down_blocks, factor)
    gram = jnp.concatenate([(keep + got) * factor for keep, got in halves], 1)
    return gram[None], down_rows


def solution(mesh):
    in_specs = (
        P(("dp", "expert"), None),
        P(("dp", "expert"), None),
        P(("dp", "expert"), None),
        P("expert", "dp", None),
        P("expert", "dp", None),
    )
    out_specs = (P("expert", "dp", None), P("expert", "dp", None))
    return jax.shard_map(local, mesh=mesh, in_specs=in_specs, out_specs=out_specs, check_vma=False)
```

time: 308 us -> 214 us (0.69)
  blocking collectives: 96.4 us -> 0 us
  waiting for transfers between devices: 134 us -> 65.7 us
  starting transfers between devices: 0.08 us -> 65 us
  Pallas kernels: 0 us -> 59.1 us
  matrix products: 57 us -> 0 us
  between operations: 14.8 us -> 1.72 us
  other arithmetic: 3.13 us -> 11.4 us
  local copies, waits for them, and re-layouts: 2.45 us -> 10.2 us
    all_gather x1 -> x0, waiting for transfers between devices: 105 us -> none  [local(): gathered = lax.all_gather(arrived, 'dp', axis=0, tiled=True)]
    ppermute x0 -> x39, waiting for transfers between devices: none -> 65.7 us  [the longest x4 21.7 us: major(): return lax.ppermute(value, 'dp', steps((step, 0), (0, step)))]
    ppermute x0 -> x39, starting transfers between devices: none -> 65 us  [the longest x16 26 us: minor(): return lax.ppermute(value, 'dp', steps((0, step), (step, 0)))]
    psum x1 -> x0, blocking collectives: 64.8 us -> none  [local(): totals = lax.psum(local_counts, ('dp', 'expert'))]
    pallas_call x0 -> x10, Pallas kernels: none -> 59.1 us  [the longest x2 28.1 us: gram_work(): pl.pallas_call(functools.partial(gram_kernel, first, count), out_shape=[j...]
    dot_general x5 -> x0, matrix products: 57 us -> none  [the longest x1 17.4 us: expert_work(): lax.dot_general(columns, rows_in, (((0,), (0,)), ((), ())), preferred_ele...]
    all_to_all x2 -> x0, blocking collectives: 31.6 us -> none  [the longest x1 17.5 us: local(): lax.all_to_all(dispatched, 'expert', split_axis=0, concat_axis=1, tiled=T...]
    reduce_scatter x1 -> x0, waiting for transfers between devices: 28.2 us -> none  [local(): lax.psum_scatter(lax.dot_general(rows_t, rows_t, (((1,), (1,)), ((), ()))...]
  transfers between devices with their start and end apart: 2 -> 39, of which waited for: 2 -> 16; matrix products, arithmetic and copies ran while one was open for 6% -> 6% of each run, Pallas kernels for 0% -> 17%
where the time goes in v1:
time: 214 us; the launch traced here: 213 us
  waiting for transfers between devices  65.7 us (31%)
  starting transfers between devices  65 us (30%)
  Pallas kernels  59.1 us (28%)
  other arithmetic  11.4 us (5%)
  local copies, waits for them, and re-layouts  10.2 us (5%)
    pallas_call x2, Pallas kernels, gram_work(): pl.pallas_call(functools.partial(gram_kernel, first, count), out_shape=[j...  28.1 us
    ppermute x16, starting transfers between devices, minor(): return lax.ppermute(value, 'dp', steps((0, step), (step, 0)))  26 us
    ppermute x4, waiting for transfers between devices, major(): return lax.ppermute(value, 'dp', steps((step, 0), (0, step)))  21.7 us
    pallas_call x4, Pallas kernels, hidden_work(): pl.pallas_call(hidden_kernel, out_shape=[jax.ShapeDtypeStruct((256, 128),...  20.2 us
    ppermute x5, starting transfers between devices, sibling(): return lax.ppermute(value, 'dp', [(i, i ^ 1) for i in range(2 * CHIPS)])  20.2 us
    ppermute x16, waiting for transfers between devices, minor(): return lax.ppermute(value, 'dp', steps((0, step), (step, 0)))  16 us
    ppermute x7, waiting for transfers between devices, along_z(): return lax.ppermute(value, 'dp', steps((0, step), (0, step)))  9.72 us
    ppermute x3, waiting for transfers between devices, local(): lax.ppermute(blocks[step], 'expert', [(i, (i + step) % 4) for i in range(...  8.17 us
  transfers between devices with their start and end apart: 39, of which 16 were waited for; matrix products, arithmetic and copies ran while one was open for 6% of the time, Pallas kernels for 17%

profile of v1, /device:TPU:1, one launch (start us, length us, event | category | flops | bytes accessed | tf_op | source)
XLA Modules:
  0.0 213.1 jit_solution(9467915042469314951)
XLA Ops:
  0.7 3.9 %shard_map.86 = (bf16[16,7296]{1,0:T(8,128)(2,1)}, bf16[16,7296]{1,0:T(8,128)(2,1)}, bf16[16,7296]{1,0:T(8,128)(2,1)}, bf16[16,7296]{1,0:T(8,128)(2,1)}) custom-call(s32[1]{0:T(128)} %bitcast.3.where, s32[8,256]{1,0:T(8,128)} %bitcast.21, s32[8,256]{1,0:T(8,128)} %bitcast.22, bf16[256,7168]{1,0:T(8,128)(2,1)} %tokens.1), custom_call_target="tpu_custom_call" | custom-call | tf_op jit(solution)/shard_map/pallas_call | solution.py:88
  13.0 6.3 %collective-permute-done.1 = bf16[16,7296]{1,0:T(8,128)(2,1)S(1)} collective-permute-done((bf16[16,7296]{1,0:T(8,128)(2,1)}, bf16[16,7296]{1,0:T(8,128)(2,1)S(1)}, u32[]{:S(2)}, u32[]{:S(2)}) %collective-permute-start.1) | collective-permute-done | bytes 233504 | tf_op jit(solution)/shard_map/ppermute | solution.py:256
  24.6 14.9 %collective-permute-done.9.p0.refs_5_ = bf16[64,7296]{1,0:T(8,128)(2,1)S(1)} collective-permute-done((bf16[64,7296]{1,0:T(8,128)(2,1)S(1)}, bf16[64,7296]{1,0:T(8,128)(2,1)S(1)}, u32[]{:S(2)}, u32[]{:S(2)}) %collective-permute-start.9) | collective-permute-done | bytes 933920 | tf_op jit(solution)/shard_map/ppermute | solution.py:41
  39.6 4.0 %collective-permute-start.4 = (bf16[64,7296]{1,0:T(8,128)(2,1)S(1)}, bf16[64,7296]{1,0:T(8,128)(2,1)S(1)}, u32[]{:S(2)}, u32[]{:S(2)}) collective-permute-start(bf16[64,7296]{1,0:T(8,128)(2,1)S(1)} %constant_dynamic-update-slice_fusion.p0.refs_0_), channel_id=1, source_target_pairs={{0,24},{4,100},{8,0},{12,108},{16,8},{20,116},{24,16},{28,124},{32... | collective-permute-start | bytes 2801672 | tf_op jit(solution)/shard_map/ppermute | solution.py:45
  43.6 6.2 %collective-permute-start.7 = (bf16[64,7168]{1,0:T(8,128)(2,1)S(1)}, bf16[64,7168]{1,0:T(8,128)(2,1)S(1)}, u32[]{:S(2)}, u32[]{:S(2)}) collective-permute-start(bf16[64,7168]{1,0:T(8,128)(2,1)S(1)} %bitcast.15), channel_id=1, source_target_pairs={{0,4},{4,0},{8,12},{12,8},{16,20},{20,16},{24,28},{28,24},{32,36},... | collective-permute-start | bytes 2752520 | tf_op jit(solution)/shard_map/ppermute | solution.py:57
  53.2 2.6 %collective-permute-start.16 = (bf16[64,7296]{1,0:T(8,128)(2,1)S(1)}, bf16[64,7296]{1,0:T(8,128)(2,1)S(1)}, u32[]{:S(2)}, u32[]{:S(2)}) collective-permute-start(bf16[64,7296]{1,0:T(8,128)(2,1)S(1)} %collective-permute-done.14.p0.refs_10_), channel_id=1, source_target_pairs={{0,24},{4,100},{8,0},{12,108},{16,8},{20,116},{24,16},{28,124},{32... | collective-permute-start | bytes 2801672 | tf_op jit(solution)/shard_map/ppermute | solution.py:45
  55.9 6.9 %collective-permute-done.20 = bf16[32,7296]{1,0:T(8,128)(2,1)S(1)} collective-permute-done((bf16[32,7296]{1,0:T(8,128)(2,1)S(1)}, bf16[32,7296]{1,0:T(8,128)(2,1)S(1)}, u32[]{:S(2)}, u32[]{:S(2)}) %collective-permute-start.20) | collective-permute-done | bytes 466976 | tf_op jit(solution)/shard_map/ppermute | solution.py:41
  62.8 2.6 %collective-permute-start.11 = (bf16[64,7296]{1,0:T(8,128)(2,1)S(1)}, bf16[64,7296]{1,0:T(8,128)(2,1)S(1)}, u32[]{:S(2)}, u32[]{:S(2)}) collective-permute-start(bf16[64,7296]{1,0:T(8,128)(2,1)S(1)} %collective-permute-done.9.p0.refs_5_), channel_id=1, source_target_pairs={{0,24},{4,100},{8,0},{12,108},{16,8},{20,116},{24,16},{28,124},{32... | collective-permute-start | bytes 2801672 | tf_op jit(solution)/shard_map/ppermute | solution.py:45
  65.5 3.7 %collective-permute-done.5.p3.refs_3_ = bf16[32,7296]{1,0:T(8,128)(2,1)S(1)} collective-permute-done((bf16[32,7296]{1,0:T(8,128)(2,1)S(1)}, bf16[32,7296]{1,0:T(8,128)(2,1)S(1)}, u32[]{:S(2)}, u32[]{:S(2)}) %collective-permute-start.5) | collective-permute-done | bytes 466976 | tf_op jit(solution)/shard_map/ppermute | solution.py:45
  69.3 2.6 %collective-permute-start.22 = (bf16[64,7296]{1,0:T(8,128)(2,1)S(1)}, bf16[64,7296]{1,0:T(8,128)(2,1)S(1)}, u32[]{:S(2)}, u32[]{:S(2)}) collective-permute-start(bf16[64,7296]{1,0:T(8,128)(2,1)S(1)} %constant_dynamic-update-slice_fusion.4.p0.refs_15_), channel_id=1, source_target_pairs={{0,24},{4,100},{8,0},{12,108},{16,8},{20,116},{24,16},{28,124},{32... | collective-permute-start | bytes 2801672 | tf_op jit(solution)/shard_map/ppermute | solution.py:45
  72.5 6.7 %collective-permute-done.10.p1.refs_6_ = bf16[64,7296]{1,0:T(8,128)(2,1)S(1)} collective-permute-done((bf16[64,7296]{1,0:T(8,128)(2,1)S(1)}, bf16[64,7296]{1,0:T(8,128)(2,1)S(1)}, u32[]{:S(2)}, u32[]{:S(2)}) %collective-permute-start.10) | collective-permute-done | bytes 933920 | tf_op jit(solution)/shard_map/ppermute | solution.py:45
  80.2 2.5 %collective-permute-start.18 = (bf16[32,7296]{1,0:T(8,128)(2,1)}, bf16[32,7296]{1,0:T(8,128)(2,1)}, u32[]{:S(2)}, u32[]{:S(2)}) collective-permute-start(bf16[32,7296]{1,0:T(8,128)(2,1)} %slice.81), channel_id=1, source_target_pairs={{0,24},{4,100},{8,0},{12,108},{16,8},{20,116},{24,16},{28,124},{32... | collective-permute-start | bytes 1400840 | tf_op jit(solution)/shard_map/ppermute | solution.py:45
  83.6 5.6 %collective-permute-done.21.p1.refs_16_ = bf16[64,7296]{1,0:T(8,128)(2,1)S(1)} collective-permute-done((bf16[64,7296]{1,0:T(8,128)(2,1)S(1)}, bf16[64,7296]{1,0:T(8,128)(2,1)S(1)}, u32[]{:S(2)}, u32[]{:S(2)}) %collective-permute-start.21) | collective-permute-done | bytes 933920 | tf_op jit(solution)/shard_map/ppermute | solution.py:45
  89.3 3.3 %collective-permute-start.13 = (bf16[32,7296]{1,0:T(8,128)(2,1)S(1)}, bf16[32,7296]{1,0:T(8,128)(2,1)}, u32[]{:S(2)}, u32[]{:S(2)}) collective-permute-start(bf16[32,7296]{1,0:T(8,128)(2,1)S(1)} %slice.79), channel_id=1, source_target_pairs={{0,24},{4,100},{8,0},{12,108},{16,8},{20,116},{24,16},{28,124},{32... | collective-permute-start | bytes 1400840 | tf_op jit(solution)/shard_map/ppermute | solution.py:45
  95.8 2.7 %collective-permute-start.24 = (bf16[32,7296]{1,0:T(8,128)(2,1)}, bf16[32,7296]{1,0:T(8,128)(2,1)S(1)}, u32[]{:S(2)}, u32[]{:S(2)}) collective-permute-start(bf16[32,7296]{1,0:T(8,128)(2,1)} %slice.85), channel_id=1, source_target_pairs={{0,24},{4,100},{8,0},{12,108},{16,8},{20,116},{24,16},{28,124},{32... | collective-permute-start | bytes 1400840 | tf_op jit(solution)/shard_map/ppermute | solution.py:45
  99.1 5.1 %shard_map.87 = (bf16[256,128]{1,0:T(8,128)(2,1)}, bf16[256,512]{1,0:T(8,128)(2,1)}, f32[8,128]{1,0:T(8,128)}) custom-call(s32[3]{0:T(128)} %pad_add_fusion.where, bf16[64,7296]{1,0:T(8,128)(2,1)} %copy-done.15, bf16[64,7296]{1,0:T(8,128)(2,1)} %copy-done.6, bf16[64,7296]{1,0:T(8,128)(2,1)} %copy-done.7, bf16[32,7296]{1,0:T(8,128)(2,1)} %copy-done.16, ...), custom_call_target="tpu_custom_call" | custom-call | flops 939524096 | bytes 8388608 | tf_op jit(solution)/shard_map/pallas_call | solution.py:117
  104.2 5.1 %shard_map.89 = (bf16[256,128]{1,0:T(8,128)(2,1)}, bf16[256,512]{1,0:T(8,128)(2,1)}, f32[8,128]{1,0:T(8,128)}) custom-call(s32[3]{0:T(128)} %pad_add_fusion.where, bf16[64,7296]{1,0:T(8,128)(2,1)} %copy-done.5, bf16[64,7296]{1,0:T(8,128)(2,1)} %copy-done.8, bf16[64,7296]{1,0:T(8,128)(2,1)} %copy-done.9, bf16[32,7296]{1,0:T(8,128)(2,1)} %copy-done.18, ...), custom_call_target="tpu_custom_call" | custom-call | flops 939524096 | bytes 8388608 | tf_op jit(solution)/shard_map/pallas_call | solution.py:117
  109.3 5.1 %shard_map.88 = (bf16[256,128]{1,0:T(8,128)(2,1)}, bf16[256,512]{1,0:T(8,128)(2,1)}, f32[8,128]{1,0:T(8,128)}) custom-call(s32[3]{0:T(128)} %pad_add_fusion.where, bf16[64,7296]{1,0:T(8,128)(2,1)} %copy-done.4, bf16[64,7296]{1,0:T(8,128)(2,1)} %copy-done.10, bf16[64,7296]{1,0:T(8,128)(2,1)} %copy-done.11, ...), custom_call_target="tpu_custom_call" | custom-call | flops 939524096 | bytes 8388608 | tf_op jit(solution)/shard_map/pallas_call | solution.py:117
  115.9 5.0 %shard_map.90 = (bf16[256,128]{1,0:T(8,128)(2,1)}, bf16[256,512]{1,0:T(8,128)(2,1)}, f32[8,128]{1,0:T(8,128)}) custom-call(s32[3]{0:T(128)} %pad_add_fusion.where, bf16[64,7296]{1,0:T(8,128)(2,1)} %copy-done.14, bf16[64,7296]{1,0:T(8,128)(2,1)} %copy-done.12, bf16[64,7296]{1,0:T(8,128)(2,1)} %copy-done.13, bf16[32,7296]{1,0:T(8,128)(2,1)} %copy-done.19, ...), custom_call_target="tpu_custom_call" | custom-call | flops 939524096 | bytes 8388608 | tf_op jit(solution)/shard_map/pallas_call | solution.py:117
  121.0 14.0 %shard_map.91 = (f32[224,3584]{1,0:T(8,128)}, f32[224,3584]{1,0:T(8,128)}) custom-call(s32[3]{0:T(128)} %pad_add_fusion.where, bf16[256,512]{1,0:T(8,128)(2,1)} %get-tuple-element.28.w0, bf16[256,512]{1,0:T(8,128)(2,1)} %get-tuple-element.29.w1, bf16[256,512]{1,0:T(8,128)(2,1)} %get-tuple-element.30.w2, bf16[256,512]{1,0:T(8,128)(2,1)} %get-tuple-element.31.w3, ...), custom_call_target="tpu_custom_call" | custom-call | flops 3758096384 | bytes 8388608 | tf_op jit(solution)/shard_map/pallas_call | solution.py:222
  134.9 10.4 %collective-permute-start.25 = (f32[224,3584]{1,0:T(8,128)}, f32[224,3584]{1,0:T(8,128)}, u32[]{:S(2)}, u32[]{:S(2)}) collective-permute-start(f32[224,3584]{1,0:T(8,128)} %get-tuple-element.33), channel_id=1, source_target_pairs={{0,4},{4,0},{8,12},{12,8},{16,20},{20,16},{24,28},{28,24},{32,36},... | collective-permute-start | bytes 9633800 | tf_op jit(solution)/shard_map/ppermute | solution.py:57
  145.3 14.2 %shard_map.94 = (f32[224,3584]{1,0:T(8,128)}, f32[224,3584]{1,0:T(8,128)}) custom-call(s32[3]{0:T(128)} %pad_add_fusion.where, bf16[256,512]{1,0:T(8,128)(2,1)} %get-tuple-element.28.w0, bf16[256,512]{1,0:T(8,128)(2,1)} %get-tuple-element.29.w1, bf16[256,512]{1,0:T(8,128)(2,1)} %get-tuple-element.30.w2, bf16[256,512]{1,0:T(8,128)(2,1)} %get-tuple-element.31.w3, ...), custom_call_target="tpu_custom_call" | custom-call | flops 3758096384 | bytes 8388608 | tf_op jit(solution)/shard_map/pallas_call | solution.py:222
  162.1 2.7 %collective-permute-start.27 = (bf16[1024,128]{1,0:T(8,128)(2,1)}, bf16[1024,128]{1,0:T(8,128)(2,1)S(1)}, u32[]{:S(2)}, u32[]{:S(2)}) collective-permute-start(bf16[1024,128]{1,0:T(8,128)(2,1)} %shard_map.92.own), channel_id=1, source_target_pairs={{0,24},{4,28},{8,0},{12,4},{16,8},{20,12},{24,16},{28,20},{32,56},... | collective-permute-start | bytes 786440 | tf_op jit(solution)/shard_map/ppermute | solution.py:53
  164.7 6.2 %collective-permute-done.26.z0 = bf16[1024,128]{1,0:T(8,128)(2,1)S(1)} collective-permute-done((bf16[1024,128]{1,0:T(8,128)(2,1)}, bf16[1024,128]{1,0:T(8,128)(2,1)S(1)}, u32[]{:S(2)}, u32[]{:S(2)}) %collective-permute-start.26) | collective-permute-done | bytes 262176 | tf_op jit(solution)/shard_map/ppermute | solution.py:53
  173.8 3.8 %collective-permute-done.31.y1 = bf16[1024,128]{1,0:T(8,128)(2,1)S(1)} collective-permute-done((bf16[1024,128]{1,0:T(8,128)(2,1)}, bf16[1024,128]{1,0:T(8,128)(2,1)S(1)}, u32[]{:S(2)}, u32[]{:S(2)}) %collective-permute-start.31) | collective-permute-done | bytes 262176 | tf_op jit(solution)/shard_map/ppermute | solution.py:49
  177.7 2.7 %collective-permute-start.33 = (bf16[512,128]{1,0:T(8,128)(2,1)S(1)}, bf16[512,128]{1,0:T(8,128)(2,1)S(1)}, u32[]{:S(2)}, u32[]{:S(2)}) collective-permute-start(bf16[512,128]{1,0:T(8,128)(2,1)S(1)} %slice.89), channel_id=1, source_target_pairs={{0,96},{4,100},{8,104},{12,108},{16,112},{20,116},{24,120},{28,124... | collective-permute-start | bytes 393224 | tf_op jit(solution)/shard_map/ppermute | solution.py:49
  183.4 3.2 %shard_map.93 = (f32[264,512]{1,0:T(8,128)}, f32[264,512]{1,0:T(8,128)}) custom-call(s32[3]{0:T(128)} %pad_add_fusion.where, bf16[1024,128]{1,0:T(8,128)(2,1)} %shard_map.92.own, bf16[1024,128]{1,0:T(8,128)(2,1)} %copy-done.26, bf16[1024,128]{1,0:T(8,128)(2,1)} %copy-done.27, bf16[512,128]{1,0:T(8,128)(2,1)} %copy-done.33, bf16[512,128]{1,0:T(8,128)(2,1)} %copy-done.34, ...), custom_call_target="tpu_custom_call" | custom-call | flops 536870912 | bytes 4194304 | tf_op jit(solution)/shard_map/pallas_call | solution.py:173
  186.7 3.3 %collective-permute-start.34 = (f32[264,512]{1,0:T(8,128)}, f32[264,512]{1,0:T(8,128)}, u32[]{:S(2)}, u32[]{:S(2)}) collective-permute-start(f32[264,512]{1,0:T(8,128)} %get-tuple-element.43), channel_id=1, source_target_pairs={{0,4},{4,0},{8,12},{12,8},{16,20},{20,16},{24,28},{28,24},{32,36},... | collective-permute-start | bytes 1622024 | tf_op jit(solution)/shard_map/ppermute | solution.py:57
  193.9 2.7 %collective-permute-start.37 = (f32[64,512]{1,0:T(8,128)S(1)}, f32[64,512]{1,0:T(8,128)S(1)}, u32[]{:S(2)}, u32[]{:S(2)}) collective-permute-start(f32[64,512]{1,0:T(8,128)S(1)} %get-tuple-element.47), channel_id=1, source_target_pairs={{0,24},{4,28},{8,0},{12,4},{16,8},{20,12},{24,16},{28,20},{32,56},... | collective-permute-start | bytes 393224 | tf_op jit(solution)/shard_map/ppermute | solution.py:53
  204.5 2.6 %add_multiply_fusion.1 = f32[224,3584]{1,0:T(8,128)S(1)} fusion(f32[224,3584]{1,0:T(8,128)S(1)} %copy-done.21, f32[224,3584]{1,0:T(8,128)} %collective-permute-done.25, f32[]{:T(128)} %bitcast.8), kind=kLoop, calls=%fused_computation.2 | loop fusion | flops 1605632 | bytes 9633796 | tf_op jit(solution)/shard_map/mul | solution.py:290
  207.4 2.5 %add_multiply_fusion = f32[224,3584]{1,0:T(8,128)S(1)} fusion(f32[224,3584]{1,0:T(8,128)S(1)} %copy-done.22, f32[224,3584]{1,0:T(8,128)} %collective-permute-done.35, f32[]{:T(128)} %bitcast.8), kind=kLoop, calls=%fused_computation.1 | loop fusion | flops 1605632 | bytes 9633796 | tf_op jit(solution)/shard_map/mul | solution.py:290
  209.8 3.3 %maximum_bitcast_fusion = f32[1,224,7168]{2,1,0:T(8,128)} fusion(f32[224,3584]{1,0:T(8,128)S(1)} %add_multiply_fusion, f32[224,3584]{1,0:T(8,128)S(1)} %add_multiply_fusion.1), kind=kLoop, calls=%fused_computation | loop fusion | flops 1605632 | bytes 12845056 | tf_op jit(solution)/shard_map/broadcast_in_dim | solution.py:291
  (165 shorter events, 45.3 us)
Async XLA Ops:
  4.5 8.5 %collective-permute-start = (bf16[16,7296]{1,0:T(8,128)(2,1)}, bf16[16,7296]{1,0:T(8,128)(2,1)S(1)}, u32[]{:S(2)}, u32[]{:S(2)}) collective-permute-start(bf16[16,7296]{1,0:T(8,128)(2,1)} %get-tuple-element.25), channel_id=1, source_target_pairs={{0,1},{1,2},{2,3},{3,0},{4,5},{5,6},{6,7},{7,4},{8,9},{9,10},{10,1... | collective-permute-start | bytes 700424 | tf_op jit(solution)/shard_map/ppermute | solution.py:256
  6.6 12.8 %collective-permute-start.1 = (bf16[16,7296]{1,0:T(8,128)(2,1)}, bf16[16,7296]{1,0:T(8,128)(2,1)S(1)}, u32[]{:S(2)}, u32[]{:S(2)}) collective-permute-start(bf16[16,7296]{1,0:T(8,128)(2,1)} %get-tuple-element.26), channel_id=1, source_target_pairs={{0,2},{1,3},{2,0},{3,1},{4,6},{5,7},{6,4},{7,5},{8,10},{9,11},{10,... | collective-permute-start | bytes 700424 | tf_op jit(solution)/shard_map/ppermute | solution.py:256
  9.0 10.3 %collective-permute-start.2 = (bf16[16,7296]{1,0:T(8,128)(2,1)}, bf16[16,7296]{1,0:T(8,128)(2,1)S(1)}, u32[]{:S(2)}, u32[]{:S(2)}) collective-permute-start(bf16[16,7296]{1,0:T(8,128)(2,1)} %get-tuple-element.27), channel_id=1, source_target_pairs={{0,3},{1,0},{2,1},{3,2},{4,7},{5,4},{6,5},{7,6},{8,11},{9,8},{10,9... | collective-permute-start | bytes 700424 | tf_op jit(solution)/shard_map/ppermute | solution.py:256
  19.4 20.1 %collective-permute-start.9 = (bf16[64,7296]{1,0:T(8,128)(2,1)S(1)}, bf16[64,7296]{1,0:T(8,128)(2,1)S(1)}, u32[]{:S(2)}, u32[]{:S(2)}) collective-permute-start(bf16[64,7296]{1,0:T(8,128)(2,1)S(1)} %constant_dynamic-update-slice_fusion.p0.refs_0_), channel_id=1, source_target_pairs={{0,32},{4,12},{8,40},{12,20},{16,48},{20,28},{24,56},{28,4},{32,64... | collective-permute-start | bytes 2801672 | tf_op jit(solution)/shard_map/ppermute | solution.py:41
  21.1 28.7 %collective-permute-start.14 = (bf16[64,7296]{1,0:T(8,128)(2,1)S(1)}, bf16[64,7296]{1,0:T(8,128)(2,1)S(1)}, u32[]{:S(2)}, u32[]{:S(2)}) collective-permute-start(bf16[64,7296]{1,0:T(8,128)(2,1)S(1)} %constant_dynamic-update-slice_fusion.p0.refs_0_), channel_id=1, source_target_pairs={{0,96},{4,28},{8,104},{12,4},{16,112},{20,12},{24,120},{28,20},{32... | collective-permute-start | bytes 2801672 | tf_op jit(solution)/shard_map/ppermute | solution.py:41
  23.3 26.6 %collective-permute-start.3 = (bf16[64,7296]{1,0:T(8,128)(2,1)S(1)}, bf16[64,7296]{1,0:T(8,128)(2,1)S(1)}, u32[]{:S(2)}, u32[]{:S(2)}) collective-permute-start(bf16[64,7296]{1,0:T(8,128)(2,1)S(1)} %constant_dynamic-update-slice_fusion.p0.refs_0_), channel_id=1, source_target_pairs={{0,8},{4,36},{8,16},{12,44},{16,24},{20,52},{24,0},{28,60},{32,40}... | collective-permute-start | bytes 2801672 | tf_op jit(solution)/shard_map/ppermute | solution.py:45
  39.5 10.7 %collective-permute-start.19 = (bf16[32,7296]{1,0:T(8,128)(2,1)S(1)}, bf16[32,7296]{1,0:T(8,128)(2,1)S(1)}, u32[]{:S(2)}, u32[]{:S(2)}) collective-permute-start(bf16[32,7296]{1,0:T(8,128)(2,1)S(1)} %slice.82), channel_id=1, source_target_pairs={{0,32},{4,12},{8,40},{12,20},{16,48},{20,28},{24,56},{28,4},{32,64... | collective-permute-start | bytes 1400840 | tf_op jit(solution)/shard_map/ppermute | solution.py:41
  39.6 16.3 %collective-permute-start.4 = (bf16[64,7296]{1,0:T(8,128)(2,1)S(1)}, bf16[64,7296]{1,0:T(8,128)(2,1)S(1)}, u32[]{:S(2)}, u32[]{:S(2)}) collective-permute-start(bf16[64,7296]{1,0:T(8,128)(2,1)S(1)} %constant_dynamic-update-slice_fusion.p0.refs_0_), channel_id=1, source_target_pairs={{0,24},{4,100},{8,0},{12,108},{16,8},{20,116},{24,16},{28,124},{32... | collective-permute-start | bytes 2801672 | tf_op jit(solution)/shard_map/ppermute | solution.py:45
  43.6 8.3 %collective-permute-start.7 = (bf16[64,7168]{1,0:T(8,128)(2,1)S(1)}, bf16[64,7168]{1,0:T(8,128)(2,1)S(1)}, u32[]{:S(2)}, u32[]{:S(2)}) collective-permute-start(bf16[64,7168]{1,0:T(8,128)(2,1)S(1)} %bitcast.15), channel_id=1, source_target_pairs={{0,4},{4,0},{8,12},{12,8},{16,20},{20,16},{24,28},{28,24},{32,36},... | collective-permute-start | bytes 2752520 | tf_op jit(solution)/shard_map/ppermute | solution.py:57
  49.9 12.8 %collective-permute-start.20 = (bf16[32,7296]{1,0:T(8,128)(2,1)S(1)}, bf16[32,7296]{1,0:T(8,128)(2,1)S(1)}, u32[]{:S(2)}, u32[]{:S(2)}) collective-permute-start(bf16[32,7296]{1,0:T(8,128)(2,1)S(1)} %slice.83), channel_id=1, source_target_pairs={{0,96},{4,28},{8,104},{12,4},{16,112},{20,12},{24,120},{28,20},{32... | collective-permute-start | bytes 1400840 | tf_op jit(solution)/shard_map/ppermute | solution.py:41
  50.2 19.1 %collective-permute-start.15 = (bf16[64,7296]{1,0:T(8,128)(2,1)S(1)}, bf16[64,7296]{1,0:T(8,128)(2,1)S(1)}, u32[]{:S(2)}, u32[]{:S(2)}) collective-permute-start(bf16[64,7296]{1,0:T(8,128)(2,1)S(1)} %collective-permute-done.14.p0.refs_10_), channel_id=1, source_target_pairs={{0,8},{4,36},{8,16},{12,44},{16,24},{20,52},{24,0},{28,60},{32,40}... | collective-permute-start | bytes 2801672 | tf_op jit(solution)/shard_map/ppermute | solution.py:45
  51.9 17.3 %collective-permute-start.5 = (bf16[32,7296]{1,0:T(8,128)(2,1)S(1)}, bf16[32,7296]{1,0:T(8,128)(2,1)S(1)}, u32[]{:S(2)}, u32[]{:S(2)}) collective-permute-start(bf16[32,7296]{1,0:T(8,128)(2,1)S(1)} %slice.76), channel_id=1, source_target_pairs={{0,8},{4,36},{8,16},{12,44},{16,24},{20,52},{24,0},{28,60},{32,40}... | collective-permute-start | bytes 1400840 | tf_op jit(solution)/shard_map/ppermute | solution.py:45
  53.2 18.8 %collective-permute-start.16 = (bf16[64,7296]{1,0:T(8,128)(2,1)S(1)}, bf16[64,7296]{1,0:T(8,128)(2,1)S(1)}, u32[]{:S(2)}, u32[]{:S(2)}) collective-permute-start(bf16[64,7296]{1,0:T(8,128)(2,1)S(1)} %collective-permute-done.14.p0.refs_10_), channel_id=1, source_target_pairs={{0,24},{4,100},{8,0},{12,108},{16,8},{20,116},{24,16},{28,124},{32... | collective-permute-start | bytes 2801672 | tf_op jit(solution)/shard_map/ppermute | solution.py:45
  55.8 23.3 %collective-permute-start.10 = (bf16[64,7296]{1,0:T(8,128)(2,1)S(1)}, bf16[64,7296]{1,0:T(8,128)(2,1)S(1)}, u32[]{:S(2)}, u32[]{:S(2)}) collective-permute-start(bf16[64,7296]{1,0:T(8,128)(2,1)S(1)} %collective-permute-done.9.p0.refs_5_), channel_id=1, source_target_pairs={{0,8},{4,36},{8,16},{12,44},{16,24},{20,52},{24,0},{28,60},{32,40}... | collective-permute-start | bytes 2801672 | tf_op jit(solution)/shard_map/ppermute | solution.py:45
  62.8 17.4 %collective-permute-start.11 = (bf16[64,7296]{1,0:T(8,128)(2,1)S(1)}, bf16[64,7296]{1,0:T(8,128)(2,1)S(1)}, u32[]{:S(2)}, u32[]{:S(2)}) collective-permute-start(bf16[64,7296]{1,0:T(8,128)(2,1)S(1)} %collective-permute-done.9.p0.refs_5_), channel_id=1, source_target_pairs={{0,24},{4,100},{8,0},{12,108},{16,8},{20,116},{24,16},{28,124},{32... | collective-permute-start | bytes 2801672 | tf_op jit(solution)/shard_map/ppermute | solution.py:45
  69.2 20.0 %collective-permute-start.21 = (bf16[64,7296]{1,0:T(8,128)(2,1)S(1)}, bf16[64,7296]{1,0:T(8,128)(2,1)S(1)}, u32[]{:S(2)}, u32[]{:S(2)}) collective-permute-start(bf16[64,7296]{1,0:T(8,128)(2,1)S(1)} %constant_dynamic-update-slice_fusion.4.p0.refs_15_), channel_id=1, source_target_pairs={{0,8},{4,36},{8,16},{12,44},{16,24},{20,52},{24,0},{28,60},{32,40}... | collective-permute-start | bytes 2801672 | tf_op jit(solution)/shard_map/ppermute | solution.py:45
  69.3 20.0 %collective-permute-start.22 = (bf16[64,7296]{1,0:T(8,128)(2,1)S(1)}, bf16[64,7296]{1,0:T(8,128)(2,1)S(1)}, u32[]{:S(2)}, u32[]{:S(2)}) collective-permute-start(bf16[64,7296]{1,0:T(8,128)(2,1)S(1)} %constant_dynamic-update-slice_fusion.4.p0.refs_15_), channel_id=1, source_target_pairs={{0,24},{4,100},{8,0},{12,108},{16,8},{20,116},{24,16},{28,124},{32... | collective-permute-start | bytes 2801672 | tf_op jit(solution)/shard_map/ppermute | solution.py:45
  72.0 22.2 %collective-permute-start.6 = (bf16[32,7296]{1,0:T(8,128)(2,1)S(1)}, bf16[32,7296]{1,0:T(8,128)(2,1)S(1)}, u32[]{:S(2)}, u32[]{:S(2)}) collective-permute-start(bf16[32,7296]{1,0:T(8,128)(2,1)S(1)} %slice.77), channel_id=1, source_target_pairs={{0,24},{4,100},{8,0},{12,108},{16,8},{20,116},{24,16},{28,124},{32... | collective-permute-start | bytes 1400840 | tf_op jit(solution)/shard_map/ppermute | solution.py:45
  79.2 15.8 %collective-permute-start.17 = (bf16[32,7296]{1,0:T(8,128)(2,1)S(1)}, bf16[32,7296]{1,0:T(8,128)(2,1)S(1)}, u32[]{:S(2)}, u32[]{:S(2)}) collective-permute-start(bf16[32,7296]{1,0:T(8,128)(2,1)S(1)} %slice.80), channel_id=1, source_target_pairs={{0,8},{4,36},{8,16},{12,44},{16,24},{20,52},{24,0},{28,60},{32,40}... | collective-permute-start | bytes 1400840 | tf_op jit(solution)/shard_map/ppermute | solution.py:45
  80.2 24.0 %collective-permute-start.18 = (bf16[32,7296]{1,0:T(8,128)(2,1)}, bf16[32,7296]{1,0:T(8,128)(2,1)}, u32[]{:S(2)}, u32[]{:S(2)}) collective-permute-start(bf16[32,7296]{1,0:T(8,128)(2,1)} %slice.81), channel_id=1, source_target_pairs={{0,24},{4,100},{8,0},{12,108},{16,8},{20,116},{24,16},{28,124},{32... | collective-permute-start | bytes 1400840 | tf_op jit(solution)/shard_map/ppermute | solution.py:45
  89.2 20.1 %collective-permute-start.12 = (bf16[32,7296]{1,0:T(8,128)(2,1)}, bf16[32,7296]{1,0:T(8,128)(2,1)}, u32[]{:S(2)}, u32[]{:S(2)}) collective-permute-start(bf16[32,7296]{1,0:T(8,128)(2,1)} %slice.78), channel_id=1, source_target_pairs={{0,8},{4,36},{8,16},{12,44},{16,24},{20,52},{24,0},{28,60},{32,40}... | collective-permute-start | bytes 1400840 | tf_op jit(solution)/shard_map/ppermute | solution.py:45
  89.3 20.0 %collective-permute-start.13 = (bf16[32,7296]{1,0:T(8,128)(2,1)S(1)}, bf16[32,7296]{1,0:T(8,128)(2,1)}, u32[]{:S(2)}, u32[]{:S(2)}) collective-permute-start(bf16[32,7296]{1,0:T(8,128)(2,1)S(1)} %slice.79), channel_id=1, source_target_pairs={{0,24},{4,100},{8,0},{12,108},{16,8},{20,116},{24,16},{28,124},{32... | collective-permute-start | bytes 1400840 | tf_op jit(solution)/shard_map/ppermute | solution.py:45
  94.2 20.2 %collective-permute-start.23 = (bf16[32,7296]{1,0:T(8,128)(2,1)}, bf16[32,7296]{1,0:T(8,128)(2,1)S(1)}, u32[]{:S(2)}, u32[]{:S(2)}) collective-permute-start(bf16[32,7296]{1,0:T(8,128)(2,1)} %slice.84), channel_id=1, source_target_pairs={{0,8},{4,36},{8,16},{12,44},{16,24},{20,52},{24,0},{28,60},{32,40}... | collective-permute-start | bytes 1400840 | tf_op jit(solution)/shard_map/ppermute | solution.py:45
  95.8 18.5 %collective-permute-start.24 = (bf16[32,7296]{1,0:T(8,128)(2,1)}, bf16[32,7296]{1,0:T(8,128)(2,1)S(1)}, u32[]{:S(2)}, u32[]{:S(2)}) collective-permute-start(bf16[32,7296]{1,0:T(8,128)(2,1)} %slice.85), channel_id=1, source_target_pairs={{0,24},{4,100},{8,0},{12,108},{16,8},{20,116},{24,16},{28,124},{32... | collective-permute-start | bytes 1400840 | tf_op jit(solution)/shard_map/ppermute | solution.py:45
  134.9 69.6 %collective-permute-start.25 = (f32[224,3584]{1,0:T(8,128)}, f32[224,3584]{1,0:T(8,128)}, u32[]{:S(2)}, u32[]{:S(2)}) collective-permute-start(f32[224,3584]{1,0:T(8,128)} %get-tuple-element.33), channel_id=1, source_target_pairs={{0,4},{4,0},{8,12},{12,8},{16,20},{20,16},{24,28},{28,24},{32,36},... | collective-permute-start | bytes 9633800 | tf_op jit(solution)/shard_map/ppermute | solution.py:57
  159.5 47.7 %collective-permute-start.35 = (f32[224,3584]{1,0:T(8,128)}, f32[224,3584]{1,0:T(8,128)}, u32[]{:S(2)}, u32[]{:S(2)}) collective-permute-start(f32[224,3584]{1,0:T(8,128)} %get-tuple-element.45), channel_id=1, source_target_pairs={{0,4},{4,0},{8,12},{12,8},{16,20},{20,16},{24,28},{28,24},{32,36},... | collective-permute-start | bytes 9633800 | tf_op jit(solution)/shard_map/ppermute | solution.py:57
  162.1 8.9 %collective-permute-start.26 = (bf16[1024,128]{1,0:T(8,128)(2,1)}, bf16[1024,128]{1,0:T(8,128)(2,1)S(1)}, u32[]{:S(2)}, u32[]{:S(2)}) collective-permute-start(bf16[1024,128]{1,0:T(8,128)(2,1)} %shard_map.92.own), channel_id=1, source_target_pairs={{0,8},{4,12},{8,16},{12,20},{16,24},{20,28},{24,0},{28,4},{32,40},... | collective-permute-start | bytes 786440 | tf_op jit(solution)/shard_map/ppermute | solution.py:53
  162.1 8.9 %collective-permute-start.27 = (bf16[1024,128]{1,0:T(8,128)(2,1)}, bf16[1024,128]{1,0:T(8,128)(2,1)S(1)}, u32[]{:S(2)}, u32[]{:S(2)}) collective-permute-start(bf16[1024,128]{1,0:T(8,128)(2,1)} %shard_map.92.own), channel_id=1, source_target_pairs={{0,24},{4,28},{8,0},{12,4},{16,8},{20,12},{24,16},{28,20},{32,56},... | collective-permute-start | bytes 786440 | tf_op jit(solution)/shard_map/ppermute | solution.py:53
  164.7 8.2 %collective-permute-start.30 = (bf16[1024,128]{1,0:T(8,128)(2,1)}, bf16[1024,128]{1,0:T(8,128)(2,1)S(1)}, u32[]{:S(2)}, u32[]{:S(2)}) collective-permute-start(bf16[1024,128]{1,0:T(8,128)(2,1)} %shard_map.92.own), channel_id=1, source_target_pairs={{0,32},{4,36},{8,40},{12,44},{16,48},{20,52},{24,56},{28,60},{32,6... | collective-permute-start | bytes 786440 | tf_op jit(solution)/shard_map/ppermute | solution.py:49
  170.9 6.7 %collective-permute-start.31 = (bf16[1024,128]{1,0:T(8,128)(2,1)}, bf16[1024,128]{1,0:T(8,128)(2,1)S(1)}, u32[]{:S(2)}, u32[]{:S(2)}) collective-permute-start(bf16[1024,128]{1,0:T(8,128)(2,1)} %shard_map.92.own), channel_id=1, source_target_pairs={{0,96},{4,100},{8,104},{12,108},{16,112},{20,116},{24,120},{28,124... | collective-permute-start | bytes 786440 | tf_op jit(solution)/shard_map/ppermute | solution.py:49
  173.0 7.5 %collective-permute-start.29 = (bf16[512,128]{1,0:T(8,128)(2,1)S(1)}, bf16[512,128]{1,0:T(8,128)(2,1)S(1)}, u32[]{:S(2)}, u32[]{:S(2)}) collective-permute-start(bf16[512,128]{1,0:T(8,128)(2,1)S(1)} %slice.87), channel_id=1, source_target_pairs={{0,24},{4,28},{8,0},{12,4},{16,8},{20,12},{24,16},{28,20},{32,56},... | collective-permute-start | bytes 393224 | tf_op jit(solution)/shard_map/ppermute | solution.py:53
  193.9 7.8 %collective-permute-start.37 = (f32[64,512]{1,0:T(8,128)S(1)}, f32[64,512]{1,0:T(8,128)S(1)}, u32[]{:S(2)}, u32[]{:S(2)}) collective-permute-start(f32[64,512]{1,0:T(8,128)S(1)} %get-tuple-element.47), channel_id=1, source_target_pairs={{0,24},{4,28},{8,0},{12,4},{16,8},{20,12},{24,16},{28,20},{32,56},... | collective-permute-start | bytes 393224 | tf_op jit(solution)/shard_map/ppermute | solution.py:53
  (44 other events, 700.9 us)

commit v2 on v1

v2 whole, which is shorter than its diff:
```python
import functools

import jax
import jax.numpy as jnp
from jax import lax
from jax.experimental import pallas as pl
from jax.experimental.pallas import tpu as pltpu
from jax.sharding import PartitionSpec as P

CAP = 16
WIDTH = 7168
FLAG = 128
SENT = WIDTH + FLAG
FF = 2048
SIDE = 4
CHIPS = 16
GRAM_ROWS = 448
WINDOW = 512
F32 = jnp.float32
BF16 = jnp.bfloat16
ORIGIN = (0, -1, 1, 2)
VMEM = pl.BlockSpec(memory_space=pltpu.VMEM)
SMEM = pl.BlockSpec(memory_space=pltpu.SMEM)
CHUNK = 1024


def params(mib):
    return pltpu.CompilerParams(vmem_limit_bytes=mib * 1024 * 1024)


def spot():
    here = lax.axis_index("dp")
    return here // 8, (here // 2) % SIDE, here % 2


def gram_start():
    y, z, _ = spot()
    chip = y * SIDE + z
    shift = (chip % 2) * 64
    return chip * GRAM_ROWS - shift, shift


def pinned(values):
    return [pltpu.with_memory_space_constraint(v, pltpu.VMEM) for v in values]


def device(y, z, core):
    return ((y % SIDE) * SIDE + z % SIDE) * 2 + core


def steps(first, second):
    return [
        (device(y, z, core), device(y + move[0], z + move[1], core))
        for y in range(SIDE)
        for z in range(SIDE)
        for core, move in enumerate((first, second))
    ]


def major(value, step):
    return lax.ppermute(value, "dp", steps((step, 0), (0, step)))


def minor(value, step):
    return lax.ppermute(value, "dp", steps((0, step), (step, 0)))


def along_y(value, step):
    return lax.ppermute(value, "dp", steps((step, 0), (step, 0)))


def along_z(value, step):
    return lax.ppermute(value, "dp", steps((0, step), (0, step)))


def sibling(value):
    return lax.ppermute(value, "dp", [(i, i ^ 1) for i in range(2 * CHIPS)])


def ring(value, move):
    half = value.shape[0] // 2
    up = move(value, 1)
    down = move(value, -1)
    return (up, down, move(up[:half], 1), move(down[half:], -1))


def direct_ring(value, move):
    return move(value, 1), move(value, -1), move(value, 2)


def dispatch_kernel(routes, slots, tokens, *outs):
    wanted = jnp.where(routes[...] < 4, routes[...] * CAP + slots[...], -1)
    lane = lax.broadcasted_iota(jnp.int32, (4 * CAP, 1), 0)
    target = ((lane // CAP + lax.axis_index("expert")) % 4) * CAP + lane % CAP
    hit = wanted[0:1, :] == target
    for k in range(1, 8):
        hit = hit | (wanted[k : k + 1, :] == target)
    one_hot = hit.astype(F32).astype(BF16)
    flag = jnp.max(hit.astype(F32), axis=1, keepdims=True)
    flag = jnp.broadcast_to(flag, (4 * CAP, FLAG)).astype(BF16)
    for start in range(0, WIDTH, 1024):
        rows = jnp.dot(
            one_hot, tokens[:, start : start + 1024], preferred_element_type=F32
        ).astype(BF16)
        for j, out in enumerate(outs):
            out[:, start : start + 1024] = rows[j * CAP : (j + 1) * CAP]
    for j, out in enumerate(outs):
        out[:, WIDTH:] = flag[j * CAP : (j + 1) * CAP]


def dispatch(routes, slots, tokens):
    return pl.pallas_call(
        dispatch_kernel,
        out_shape=[jax.ShapeDtypeStruct((CAP, SENT), BF16)] * 4,
        in_specs=[VMEM] * 3,
        out_specs=[VMEM] * 4,
        compiler_params=params(32),
    )(routes.T, slots.T, tokens)


def hidden_kernel(group, *refs):
    size = len(refs) - (8 if group else 7)
    pieces, (g, gs, u, us) = refs[:size], refs[size : size + 4]
    hidden, window, count = refs[-3:]
    y, z, core = spot()
    base, _ = gram_start()
    total = jnp.zeros((256, 256), F32)
    for start in range(0, WIDTH, CHUNK):
        rows = jnp.concatenate([p[:, start : start + CHUNK] for p in pieces], 0)
        weights = jnp.concatenate([w[:, start : start + CHUNK] for w in (g, gs, u, us)], 0)
        total += lax.dot_general(
            rows, weights, (((1,), (1,)), ((), ())), preferred_element_type=F32
        )
    gate, upward = total[:, :128], total[:, 128:]
    value = gate / (1.0 + jnp.exp(-gate)) * upward
    value = jnp.where(core == 1, pltpu.roll(value, 64, 1), value).astype(BF16)
    seen = jnp.concatenate([p[:, WIDTH:] for p in pieces], 0).astype(F32)
    count[...] = jnp.broadcast_to(jnp.sum(seen, axis=0, keepdims=True), (16, FLAG))
    if group:
        hidden[...] = refs[size + 4][...]
    for j in range(4):
        far = (jnp.where(core == 0, y, z) + ORIGIN[group] + SIDE) % SIDE
        near = (jnp.where(core == 0, z, y) + ORIGIN[j] + SIDE) % SIDE
        slot = jnp.where(core == 0, far * SIDE + near, near * SIDE + far)
        hidden[pl.ds(pl.multiple_of(slot * 64, 64), 64), :] = value[64 * j : 64 * j + 64]
    base = pl.multiple_of(base, 128)
    window[...] = jnp.concatenate([p[:, pl.ds(base, WINDOW)] for p in pieces], 0).T


def hidden_work(group, pieces, weights, before):
    return pl.pallas_call(
        functools.partial(hidden_kernel, group),
        out_shape=[
            jax.ShapeDtypeStruct((1024, 128), BF16),
            jax.ShapeDtypeStruct((WINDOW, 256), BF16),
            jax.ShapeDtypeStruct((16, FLAG), F32),
        ],
        in_specs=[VMEM] * (len(pieces) + 4 + len(before)),
        out_specs=[VMEM] * 3,
        compiler_params=params(12),
        cost_estimate=pl.CostEstimate(
            flops=2 * 256 * 256 * WIDTH, bytes_accessed=8 << 20, transcendentals=256 * 128
        ),
    )(*pinned(pieces), *pinned(weights), *pinned(before))


def down_kernel(own, z0, z1, z2, y0, y1, y2, n0, n1, n2, n3, keep, send, tile):
    core = spot()[2]
    left = jnp.concatenate([own[...], z0[...], z1[...], z2[...]], 1)
    right = jnp.concatenate([own[...], y0[...], y1[...], y2[...]], 1)
    tile[...] = lax.dot_general(
        left, right, (((0,), (0,)), ((), ())), preferred_element_type=F32
    )
    for j in range(4):
        mine = pl.multiple_of(128 * j + 64 * core, 64)
        other = pl.multiple_of(128 * j + 64 - 64 * core, 64)
        keep[64 * j : 64 * j + 64, :] = tile[pl.ds(mine, 64), :]
        send[64 * j : 64 * j + 64, :] = tile[pl.ds(other, 64), :].astype(BF16)
    counts = jnp.concatenate([n0[...], n1[...], n2[...], n3[...]], 1)
    keep[256:, :] = counts
    send[256:, :] = counts.astype(BF16)


def down_work(own, ring_z, ring_y, counts):
    return pl.pallas_call(
        down_kernel,
        out_shape=[
            jax.ShapeDtypeStruct((272, 512), F32),
            jax.ShapeDtypeStruct((272, 512), BF16),
        ],
        in_specs=[VMEM] * 11,
        out_specs=[VMEM] * 2,
        scratch_shapes=[pltpu.VMEM((512, 512), F32)],
        compiler_params=params(12),
        cost_estimate=pl.CostEstimate(
            flops=2 * 512 * 512 * 1024, bytes_accessed=4 << 20, transcendentals=0
        ),
    )(*pinned((own, *ring_z, *ring_y, *counts)))


def sum_kernel(keep, got, *outs):
    for j in range(4):
        rows = pl.ds(64 * j, 64)
        outs[j][...] = (keep[rows, :] + got[rows, :].astype(F32)).astype(outs[j].dtype)
    counts = keep[256:264, :] + got[256:, :].astype(F32)[:8]
    total = sum(counts[:, 128 * i : 128 * i + 128] for i in range(4))
    outs[4][...] = 2.0 / total


def sum_blocks(keep, got):
    return pl.pallas_call(
        sum_kernel,
        out_shape=[jax.ShapeDtypeStruct((64, 512), F32 if j == 0 else BF16) for j in range(4)]
        + [jax.ShapeDtypeStruct((8, 128), F32)],
        in_specs=[VMEM] * 2,
        out_specs=[VMEM] * 5,
        compiler_params=params(8),
    )(*pinned((keep, got)))


def place_kernel(b0, b1, b2, b3, factor, out):
    y, z, _ = spot()
    for j, block in enumerate((b0, b1, b2, b3)):
        for i in range(4):
            from_y = (y + ORIGIN[i] + SIDE) % SIDE
            from_z = (z + ORIGIN[j] + SIDE) % SIDE
            start = pl.multiple_of((from_y * SIDE + from_z) * 128, 128)
            part = block[:, 128 * i : 128 * i + 128].astype(F32)
            out[0, :, pl.ds(start, 128)] = part * factor[0:1, :]


def place(blocks, factor):
    return pl.pallas_call(
        place_kernel,
        out_shape=jax.ShapeDtypeStruct((1, 64, FF), F32),
        in_specs=[VMEM] * 5,
        out_specs=VMEM,
        compiler_params=params(8),
    )(*pinned((*blocks, factor)))


def gram_kernel(mine, *refs):
    size = len(refs) - (3 if mine else 1)
    windows, pieces, rest = refs[:4], refs[4:size], refs[size:]
    core = spot()[2]
    _, shift = gram_start()
    first = shift + core * 224 if mine else shift + 224 - core * 224
    first = pl.multiple_of(first, 32)
    left = jnp.concatenate([w[pl.ds(first, 224), :] for w in windows], 1)
    here = pl.ds(pl.multiple_of(pl.program_id(0) * CHUNK, CHUNK), CHUNK)
    right = jnp.concatenate([p[:, here] for p in pieces], 0)
    part = jnp.dot(left, right, preferred_element_type=F32)
    if mine:
        got, factor, out = rest
        out[0, :, :] = (part + got[:, here].astype(F32)) * factor[0:1, 0:1]
    else:
        rest[0][...] = part.astype(BF16)


def gram_work(windows, pieces, got=None, factor=None):
    mine = got is not None
    shape = (224, WIDTH)
    if mine:
        out_spec = pl.BlockSpec((1, 224, CHUNK), lambda n: (0, 0, n))
    else:
        out_spec = pl.BlockSpec((224, CHUNK), lambda n: (0, n))
    return pl.pallas_call(
        functools.partial(gram_kernel, mine),
        grid=(WIDTH // CHUNK,),
        out_shape=jax.ShapeDtypeStruct((1,) + shape, F32) if mine else jax.ShapeDtypeStruct(shape, BF16),
        in_specs=[VMEM] * (4 + len(pieces)) + ([VMEM] * 2 if mine else []),
        out_specs=out_spec,
        compiler_params=params(10),
        cost_estimate=pl.CostEstimate(
            flops=2 * 224 * WIDTH * 1024, bytes_accessed=24 << 20, transcendentals=0
        ),
    )(*pinned(windows), *pinned(pieces), *(pinned((got, factor)) if mine else ()))


def after(value, done):
    return lax.optimization_barrier((value, done))


def local(tokens, routes, slot_ids, gate_weight, up_weight):
    gate_own, up_own = gate_weight[0], up_weight[0]
    weights = (gate_own, sibling(gate_own), up_own, sibling(up_own))

    blocks = dispatch(routes, slot_ids, tokens)
    parts = [blocks[0]]
    for step in (1, 2, 3):
        parts.append(lax.ppermute(blocks[step], "expert", [(i, (i + step) % 4) for i in range(4)]))
    shard = jnp.concatenate(parts, 0)

    up, down, up2, down2 = ring(shard, major)
    groups = []
    for piece in (shard, up, down, jnp.concatenate([up2, down2], 0)):
        groups.append((piece,) + ring(piece, minor))
    windows, counts, before = [], [], ()
    for index, group in enumerate(groups):
        hidden, window, count = hidden_work(index, group, weights, before)
        before = (hidden,)
        windows.append(window)
        counts.append(count)

    ring_z = direct_ring(hidden, along_z)
    ring_y = direct_ring(hidden, along_y)
    pieces = [piece for group in groups for piece in group]
    send, _ = after(gram_work(windows, pieces), (ring_z[:2], ring_y[:2]))
    got = sibling(send)

    down_keep, down_send = down_work(hidden, ring_z, ring_y, counts)
    *sums, factor = sum_blocks(down_keep, sibling(down_send))
    down_blocks = [
        sums[0],
        along_z(sums[2], 1),
        along_z(sums[1], -1),
        along_z(sums[3], 2),
    ]
    gram = gram_work(windows, pieces, got, factor)
    factor, gram = after(factor, gram)
    return gram, place(down_blocks, factor)


def solution(mesh):
    in_specs = (
        P(("dp", "expert"), None),
        P(("dp", "expert"), None),
        P(("dp", "expert"), None),
        P("expert", "dp", None),
        P("expert", "dp", None),
    )
    out_specs = (P("expert", "dp", None), P("expert", "dp", None))
    return jax.shard_map(local, mesh=mesh, in_specs=in_specs, out_specs=out_specs, check_vma=False)
```

time: 214 us -> 146 us (0.68)
  Pallas kernels: 59.1 us -> 18.6 us
  starting transfers between devices: 65 us -> 53.3 us
  other arithmetic: 11.4 us -> 0 us
  local copies, waits for them, and re-layouts: 10.2 us -> 4.04 us
  waiting for transfers between devices: 65.7 us -> 69.2 us
    pallas_call x8, Pallas kernels: 53.2 us -> 16.9 us  [the longest x2 11.1 us: gram_work(): pl.pallas_call(functools.partial(gram_kernel, mine), grid=(WIDTH // CHUNK...]
    ppermute x16, waiting for transfers between devices: 16 us -> 36.7 us  [minor(): return lax.ppermute(value, 'dp', steps((0, step), (step, 0)))]
    ppermute x4, waiting for transfers between devices: 21.7 us -> 11 us  [major(): return lax.ppermute(value, 'dp', steps((step, 0), (0, step)))]
    ppermute x5 -> x4, starting transfers between devices: 20.2 us -> 12 us  [sibling(): return lax.ppermute(value, 'dp', [(i, i ^ 1) for i in range(2 * CHIPS)])]
    ppermute x7 -> x6, waiting for transfers between devices: 9.72 us -> 2.83 us  [along_z(): return lax.ppermute(value, 'dp', steps((0, step), (0, step)))]
    mul x4 -> x0, other arithmetic: 6.17 us -> none  [the longest x2 5.06 us: local(): gram = jnp.concatenate([(keep + got) * factor for keep, got in halves], 1)]
    ppermute x16, starting transfers between devices: 26 us -> 21.6 us  [minor(): return lax.ppermute(value, 'dp', steps((0, step), (step, 0)))]
    slice x14 -> x10, local copies, waits for them, and re-layouts: 3.58 us -> 0.32 us  [ring(): return (up, down, move(up[:half], 1), move(down[half:], -1))]
  transfers between devices with their start and end apart: 39 -> 36, of which waited for: 16 -> 19; matrix products, arithmetic and copies ran while one was open for 6% -> 0% of each run, Pallas kernels for 17% -> 11%
where the time goes in v2:
time: 146 us
  waiting for transfers between devices  69.2 us (47%)
  starting transfers between devices  53.3 us (37%)
  Pallas kernels  18.6 us (13%)
  local copies, waits for them, and re-layouts  4.04 us (3%)
    ppermute x16, waiting for transfers between devices, minor(): return lax.ppermute(value, 'dp', steps((0, step), (step, 0)))  36.7 us
    ppermute x16, starting transfers between devices, minor(): return lax.ppermute(value, 'dp', steps((0, step), (step, 0)))  21.6 us
    ppermute x4, starting transfers between devices, sibling(): return lax.ppermute(value, 'dp', [(i, i ^ 1) for i in range(2 * CHIPS)])  12 us
    pallas_call x2, Pallas kernels, gram_work(): pl.pallas_call(functools.partial(gram_kernel, mine), grid=(WIDTH // CHUNK...  11.1 us
    ppermute x4, waiting for transfers between devices, major(): return lax.ppermute(value, 'dp', steps((step, 0), (0, step)))  11 us
    ppermute x3, waiting for transfers between devices, local(): lax.ppermute(blocks[step], 'expert', [(i, (i + step) % 4) for i in range(...  8.9 us
    ppermute x3, waiting for transfers between devices, along_y(): return lax.ppermute(value, 'dp', steps((step, 0), (step, 0)))  8.51 us
    ppermute x4, starting transfers between devices, major(): return lax.ppermute(value, 'dp', steps((step, 0), (0, step)))  6.48 us
  transfers between devices with their start and end apart: 36, of which 19 were waited for; matrix products, arithmetic and copies ran while one was open for 0% of the time, Pallas kernels for 11%

profile of v2, /device:TPU:1, one launch (start us, length us, event | category | flops | bytes accessed | tf_op | source)
XLA Modules:
  0.0 146.0 jit_solution(15220718545472043666)
XLA Ops:
  0.7 2.2 %copy-done.2 = bf16[256,7168]{1,0:T(8,128)(2,1)S(1)} copy-done((bf16[256,7168]{1,0:T(8,128)(2,1)S(1)}, bf16[256,7168]{1,0:T(8,128)(2,1)}, u32[]{:S(2)}) %copy-start.2) | copy-done | bytes 3670040
  5.0 2.1 %collective-permute-start = (bf16[16,7296]{1,0:T(8,128)(2,1)S(1)}, bf16[16,7296]{1,0:T(8,128)(2,1)S(1)}, u32[]{:S(2)}, u32[]{:S(2)}) collective-permute-start(bf16[16,7296]{1,0:T(8,128)(2,1)S(1)} %get-tuple-element.29), channel_id=1, source_target_pairs={{0,1},{1,2},{2,3},{3,0},{4,5},{5,6},{6,7},{7,4},{8,9},{9,10},{10,1... | collective-permute-start | bytes 700424 | tf_op jit(solution)/shard_map/ppermute | solution.py:291
  7.1 2.5 %collective-permute-start.1 = (bf16[16,7296]{1,0:T(8,128)(2,1)S(1)}, bf16[16,7296]{1,0:T(8,128)(2,1)S(1)}, u32[]{:S(2)}, u32[]{:S(2)}) collective-permute-start(bf16[16,7296]{1,0:T(8,128)(2,1)S(1)} %get-tuple-element.30), channel_id=1, source_target_pairs={{0,2},{1,3},{2,0},{3,1},{4,6},{5,7},{6,4},{7,5},{8,10},{9,11},{10,... | collective-permute-start | bytes 700424 | tf_op jit(solution)/shard_map/ppermute | solution.py:291
  10.7 2.6 %collective-permute-done = bf16[16,7296]{1,0:T(8,128)(2,1)S(1)} collective-permute-done((bf16[16,7296]{1,0:T(8,128)(2,1)S(1)}, bf16[16,7296]{1,0:T(8,128)(2,1)S(1)}, u32[]{:S(2)}, u32[]{:S(2)}) %collective-permute-start) | collective-permute-done | bytes 233504 | tf_op jit(solution)/shard_map/ppermute | solution.py:291
  13.4 6.3 %collective-permute-done.1 = bf16[16,7296]{1,0:T(8,128)(2,1)S(1)} collective-permute-done((bf16[16,7296]{1,0:T(8,128)(2,1)S(1)}, bf16[16,7296]{1,0:T(8,128)(2,1)S(1)}, u32[]{:S(2)}, u32[]{:S(2)}) %collective-permute-start.1) | collective-permute-done | bytes 233504 | tf_op jit(solution)/shard_map/ppermute | solution.py:291
  19.7 1.7 %collective-permute-start.3 = (bf16[64,7296]{1,0:T(8,128)(2,1)S(1)}, bf16[64,7296]{1,0:T(8,128)(2,1)S(1)}, u32[]{:S(2)}, u32[]{:S(2)}) collective-permute-start(bf16[64,7296]{1,0:T(8,128)(2,1)S(1)} %constant_dynamic-update-slice_fusion.refs_0_.refs_4_), channel_id=1, source_target_pairs={{0,32},{4,12},{8,40},{12,20},{16,48},{20,28},{24,56},{28,4},{32,64... | collective-permute-start | bytes 2801672 | tf_op jit(solution)/shard_map/ppermute | solution.py:61
  21.4 2.2 %collective-permute-start.5 = (bf16[64,7296]{1,0:T(8,128)(2,1)S(1)}, bf16[64,7296]{1,0:T(8,128)(2,1)S(1)}, u32[]{:S(2)}, u32[]{:S(2)}) collective-permute-start(bf16[64,7296]{1,0:T(8,128)(2,1)S(1)} %constant_dynamic-update-slice_fusion.refs_0_.refs_4_), channel_id=1, source_target_pairs={{0,96},{4,28},{8,104},{12,4},{16,112},{20,12},{24,120},{28,20},{32... | collective-permute-start | bytes 2801672 | tf_op jit(solution)/shard_map/ppermute | solution.py:61
  23.6 2.7 %collective-permute-start.22 = (bf16[64,7296]{1,0:T(8,128)(2,1)S(1)}, bf16[64,7296]{1,0:T(8,128)(2,1)S(1)}, u32[]{:S(2)}, u32[]{:S(2)}) collective-permute-start(bf16[64,7296]{1,0:T(8,128)(2,1)S(1)} %constant_dynamic-update-slice_fusion.refs_0_.refs_4_), channel_id=1, source_target_pairs={{0,24},{4,100},{8,0},{12,108},{16,8},{20,116},{24,16},{28,124},{32... | collective-permute-start | bytes 2801672 | tf_op jit(solution)/shard_map/ppermute | solution.py:65
  26.3 8.4 %collective-permute-done.3.refs_0_.refs_9_ = bf16[64,7296]{1,0:T(8,128)(2,1)S(1)} collective-permute-done((bf16[64,7296]{1,0:T(8,128)(2,1)S(1)}, bf16[64,7296]{1,0:T(8,128)(2,1)S(1)}, u32[]{:S(2)}, u32[]{:S(2)}) %collective-permute-start.3) | collective-permute-done | bytes 933920 | tf_op jit(solution)/shard_map/ppermute | solution.py:61
  36.0 2.5 %collective-permute-start.11 = (bf16[64,7168]{1,0:T(8,128)(2,1)S(1)}, bf16[64,7168]{1,0:T(8,128)(2,1)S(1)}, u32[]{:S(2)}, u32[]{:S(2)}) collective-permute-start(bf16[64,7168]{1,0:T(8,128)(2,1)S(1)} %bitcast.4), channel_id=1, source_target_pairs={{0,4},{4,0},{8,12},{12,8},{16,20},{20,16},{24,28},{28,24},{32,36},... | collective-permute-start | bytes 2752520 | tf_op jit(solution)/shard_map/ppermute | solution.py:77
  38.5 2.3 %collective-permute-done.5.refs_0_.refs_14_ = bf16[64,7296]{1,0:T(8,128)(2,1)S(1)} collective-permute-done((bf16[64,7296]{1,0:T(8,128)(2,1)S(1)}, bf16[64,7296]{1,0:T(8,128)(2,1)S(1)}, u32[]{:S(2)}, u32[]{:S(2)}) %collective-permute-start.5) | collective-permute-done | bytes 933920 | tf_op jit(solution)/shard_map/ppermute | solution.py:61
  40.8 5.4 %collective-permute-start.12 = (bf16[64,7168]{1,0:T(8,128)(2,1)S(1)}, bf16[64,7168]{1,0:T(8,128)(2,1)S(1)}, u32[]{:S(2)}, u32[]{:S(2)}) collective-permute-start(bf16[64,7168]{1,0:T(8,128)(2,1)S(1)} %bitcast.9), channel_id=1, source_target_pairs={{0,4},{4,0},{8,12},{12,8},{16,20},{20,16},{24,28},{28,24},{32,36},... | collective-permute-start | bytes 2752520 | tf_op jit(solution)/shard_map/ppermute | solution.py:77
  46.3 2.5 %collective-permute-start.6 = (bf16[32,7296]{1,0:T(8,128)(2,1)S(1)}, bf16[32,7296]{1,0:T(8,128)(2,1)S(1)}, u32[]{:S(2)}, u32[]{:S(2)}) collective-permute-start(bf16[32,7296]{1,0:T(8,128)(2,1)S(1)} %slice.41), channel_id=1, source_target_pairs={{0,96},{4,28},{8,104},{12,4},{16,112},{20,12},{24,120},{28,20},{32... | collective-permute-start | bytes 1400840 | tf_op jit(solution)/shard_map/ppermute | solution.py:61
  48.8 3.5 %collective-permute-start.18 = (bf16[64,7296]{1,0:T(8,128)(2,1)S(1)}, bf16[64,7296]{1,0:T(8,128)(2,1)S(1)}, u32[]{:S(2)}, u32[]{:S(2)}) collective-permute-start(bf16[64,7296]{1,0:T(8,128)(2,1)S(1)} %collective-permute-done.3.refs_0_.refs_9_), channel_id=1, source_target_pairs={{0,24},{4,100},{8,0},{12,108},{16,8},{20,116},{24,16},{28,124},{32... | collective-permute-start | bytes 2801672 | tf_op jit(solution)/shard_map/ppermute | solution.py:65
  52.5 1.3 collective-permute-done.21.refs_1_.refs_5_
  54.3 3.3 %collective-permute-start.17 = (bf16[64,7296]{1,0:T(8,128)(2,1)S(1)}, bf16[64,7296]{1,0:T(8,128)(2,1)S(1)}, u32[]{:S(2)}, u32[]{:S(2)}) collective-permute-start(bf16[64,7296]{1,0:T(8,128)(2,1)S(1)} %collective-permute-done.3.refs_0_.refs_9_), channel_id=1, source_target_pairs={{0,8},{4,36},{8,16},{12,44},{16,24},{20,52},{24,0},{28,60},{32,40}... | collective-permute-start | bytes 2801672 | tf_op jit(solution)/shard_map/ppermute | solution.py:65
  57.6 11.9 %collective-permute-done.24.refs_4_.refs_8_ = bf16[32,7296]{1,0:T(8,128)(2,1)S(1)} collective-permute-done((bf16[32,7296]{1,0:T(8,128)(2,1)S(1)}, bf16[32,7296]{1,0:T(8,128)(2,1)S(1)}, u32[]{:S(2)}, u32[]{:S(2)}) %collective-permute-start.24) | collective-permute-done | bytes 466976 | tf_op jit(solution)/shard_map/ppermute | solution.py:65
  69.5 2.4 %collective-permute-start.8 = (bf16[64,7296]{1,0:T(8,128)(2,1)S(1)}, bf16[64,7296]{1,0:T(8,128)(2,1)S(1)}, u32[]{:S(2)}, u32[]{:S(2)}) collective-permute-start(bf16[64,7296]{1,0:T(8,128)(2,1)S(1)} %constant_dynamic-update-slice_fusion.4.refs_0_.refs_19_), channel_id=1, source_target_pairs={{0,24},{4,100},{8,0},{12,108},{16,8},{20,116},{24,16},{28,124},{32... | collective-permute-start | bytes 2801672 | tf_op jit(solution)/shard_map/ppermute | solution.py:65
  72.0 7.5 %collective-permute-done.14.refs_2_.refs_16_ = bf16[64,7296]{1,0:T(8,128)(2,1)S(1)} collective-permute-done((bf16[64,7296]{1,0:T(8,128)(2,1)S(1)}, bf16[64,7296]{1,0:T(8,128)(2,1)S(1)}, u32[]{:S(2)}, u32[]{:S(2)}) %collective-permute-start.14) | collective-permute-done | bytes 933920 | tf_op jit(solution)/shard_map/ppermute | solution.py:65
  80.8 1.4 collective-permute-start.20
  82.5 7.1 %collective-permute-done.8.refs_2_.refs_21_ = bf16[64,7296]{1,0:T(8,128)(2,1)S(1)} collective-permute-done((bf16[64,7296]{1,0:T(8,128)(2,1)S(1)}, bf16[64,7296]{1,0:T(8,128)(2,1)S(1)}, u32[]{:S(2)}, u32[]{:S(2)}) %collective-permute-start.8) | collective-permute-done | bytes 933920 | tf_op jit(solution)/shard_map/ppermute | solution.py:65
  89.5 2.4 %collective-permute-start.16 = (bf16[32,7296]{1,0:T(8,128)(2,1)S(1)}, bf16[32,7296]{1,0:T(8,128)(2,1)S(1)}, u32[]{:S(2)}, u32[]{:S(2)}) collective-permute-start(bf16[32,7296]{1,0:T(8,128)(2,1)S(1)} %slice.45), channel_id=1, source_target_pairs={{0,24},{4,100},{8,0},{12,108},{16,8},{20,116},{24,16},{28,124},{32... | collective-permute-start | bytes 1400840 | tf_op jit(solution)/shard_map/ppermute | solution.py:65
  92.8 2.0 %collective-permute-start.10 = (bf16[32,7296]{1,0:T(8,128)(2,1)S(1)}, bf16[32,7296]{1,0:T(8,128)(2,1)S(1)}, u32[]{:S(2)}, u32[]{:S(2)}) collective-permute-start(bf16[32,7296]{1,0:T(8,128)(2,1)S(1)} %slice.43), channel_id=1, source_target_pairs={{0,24},{4,100},{8,0},{12,108},{16,8},{20,116},{24,16},{28,124},{32... | collective-permute-start | bytes 1400840 | tf_op jit(solution)/shard_map/ppermute | solution.py:65
  99.5 3.2 %collective-permute-done.15.refs_3_.refs_17_ = bf16[32,7296]{1,0:T(8,128)(2,1)S(1)} collective-permute-done((bf16[32,7296]{1,0:T(8,128)(2,1)S(1)}, bf16[32,7296]{1,0:T(8,128)(2,1)S(1)}, u32[]{:S(2)}, u32[]{:S(2)}) %collective-permute-start.15) | collective-permute-done | bytes 466976 | tf_op jit(solution)/shard_map/ppermute | solution.py:65
  104.5 3.2 %collective-permute-done.9.refs_3_.refs_22_ = bf16[32,7296]{1,0:T(8,128)(2,1)S(1)} collective-permute-done((bf16[32,7296]{1,0:T(8,128)(2,1)S(1)}, bf16[32,7296]{1,0:T(8,128)(2,1)S(1)}, u32[]{:S(2)}, u32[]{:S(2)}) %collective-permute-start.9) | collective-permute-done | bytes 466976 | tf_op jit(solution)/shard_map/ppermute | solution.py:65
  110.6 2.2 %collective-permute-start.26 = (bf16[1024,128]{1,0:T(8,128)(2,1)S(1)}, bf16[1024,128]{1,0:T(8,128)(2,1)S(1)}, u32[]{:S(2)}, u32[]{:S(2)}) collective-permute-start(bf16[1024,128]{1,0:T(8,128)(2,1)S(1)} %get-tuple-element.35.own), channel_id=1, source_target_pairs={{0,24},{4,28},{8,0},{12,4},{16,8},{20,12},{24,16},{28,20},{32,56},... | collective-permute-start | bytes 786440 | tf_op jit(solution)/shard_map/ppermute | solution.py:73
  112.8 4.8 %shard_map.75 = bf16[224,7168]{1,0:T(8,128)(2,1)S(1)} custom-call(bf16[512,256]{1,0:T(8,128)(2,1)S(1)} %get-tuple-element.43.refs_0_, bf16[512,256]{1,0:T(8,128)(2,1)S(1)} %get-tuple-element.44.refs_1_, bf16[512,256]{1,0:T(8,128)(2,1)S(1)} %get-tuple-element.45.refs_2_, bf16[512,256]{1,0:T(8,128)(2,1)S(1)} %get-tuple-element.46.refs_3_, ...), custom_call_target="tpu_custom_call" | custom-call | flops 3288334336 | bytes 25165824 | tf_op jit(solution)/shard_map/pallas_call | solution.py:267
  117.6 2.2 %collective-permute-done.25.z0 = bf16[1024,128]{1,0:T(8,128)(2,1)S(1)} collective-permute-done((bf16[1024,128]{1,0:T(8,128)(2,1)S(1)}, bf16[1024,128]{1,0:T(8,128)(2,1)S(1)}, u32[]{:S(2)}, u32[]{:S(2)}) %collective-permute-start.25) | collective-permute-done | bytes 262176 | tf_op jit(solution)/shard_map/ppermute | solution.py:73
  119.8 2.9 %collective-permute-start.32 = (bf16[224,7168]{1,0:T(8,128)(2,1)S(1)}, bf16[224,7168]{1,0:T(8,128)(2,1)S(1)}, u32[]{:S(2)}, u32[]{:S(2)}) collective-permute-start(bf16[224,7168]{1,0:T(8,128)(2,1)S(1)} %shard_map.75), channel_id=1, source_target_pairs={{0,4},{4,0},{8,12},{12,8},{16,20},{20,16},{24,28},{28,24},{32,36},... | collective-permute-start | bytes 9633800 | tf_op jit(solution)/shard_map/ppermute | solution.py:77
  123.7 8.5 %collective-permute-done.30.y2 = bf16[1024,128]{1,0:T(8,128)(2,1)S(1)} collective-permute-done((bf16[1024,128]{1,0:T(8,128)(2,1)S(1)}, bf16[1024,128]{1,0:T(8,128)(2,1)S(1)}, u32[]{:S(2)}, u32[]{:S(2)}) %collective-permute-start.30) | collective-permute-done | bytes 262176 | tf_op jit(solution)/shard_map/ppermute | solution.py:69
  136.1 2.7 %collective-permute-start.34 = (bf16[64,512]{1,0:T(8,128)(2,1)S(1)}, bf16[64,512]{1,0:T(8,128)(2,1)S(1)}, u32[]{:S(2)}, u32[]{:S(2)}) collective-permute-start(bf16[64,512]{1,0:T(8,128)(2,1)S(1)} %get-tuple-element.51), channel_id=1, source_target_pairs={{0,24},{4,28},{8,0},{12,4},{16,8},{20,12},{24,16},{28,20},{32,56},... | collective-permute-start | bytes 196616 | tf_op jit(solution)/shard_map/ppermute | solution.py:73
  138.8 6.3 %shard_map.76 = f32[1,224,7168]{2,1,0:T(8,128)} custom-call(bf16[512,256]{1,0:T(8,128)(2,1)S(1)} %get-tuple-element.43.refs_0_, bf16[512,256]{1,0:T(8,128)(2,1)S(1)} %get-tuple-element.44.refs_1_, bf16[512,256]{1,0:T(8,128)(2,1)S(1)} %get-tuple-element.45.refs_2_, bf16[512,256]{1,0:T(8,128)(2,1)S(1)} %get-tuple-element.46.refs_3_, ...), custom_call_target="tpu_custom_call" | custom-call | flops 3288334336 | bytes 25165824 | tf_op jit(solution)/shard_map/pallas_call | solution.py:267
  (76 shorter events, 22.9 us)
Async XLA Ops:
  5.0 8.3 %collective-permute-start = (bf16[16,7296]{1,0:T(8,128)(2,1)S(1)}, bf16[16,7296]{1,0:T(8,128)(2,1)S(1)}, u32[]{:S(2)}, u32[]{:S(2)}) collective-permute-start(bf16[16,7296]{1,0:T(8,128)(2,1)S(1)} %get-tuple-element.29), channel_id=1, source_target_pairs={{0,1},{1,2},{2,3},{3,0},{4,5},{5,6},{6,7},{7,4},{8,9},{9,10},{10,1... | collective-permute-start | bytes 700424 | tf_op jit(solution)/shard_map/ppermute | solution.py:291
  7.1 12.5 %collective-permute-start.1 = (bf16[16,7296]{1,0:T(8,128)(2,1)S(1)}, bf16[16,7296]{1,0:T(8,128)(2,1)S(1)}, u32[]{:S(2)}, u32[]{:S(2)}) collective-permute-start(bf16[16,7296]{1,0:T(8,128)(2,1)S(1)} %get-tuple-element.30), channel_id=1, source_target_pairs={{0,2},{1,3},{2,0},{3,1},{4,6},{5,7},{6,4},{7,5},{8,10},{9,11},{10,... | collective-permute-start | bytes 700424 | tf_op jit(solution)/shard_map/ppermute | solution.py:291
  9.5 10.1 %collective-permute-start.2 = (bf16[16,7296]{1,0:T(8,128)(2,1)S(1)}, bf16[16,7296]{1,0:T(8,128)(2,1)S(1)}, u32[]{:S(2)}, u32[]{:S(2)}) collective-permute-start(bf16[16,7296]{1,0:T(8,128)(2,1)S(1)} %get-tuple-element.31), channel_id=1, source_target_pairs={{0,3},{1,0},{2,1},{3,2},{4,7},{5,4},{6,5},{7,6},{8,11},{9,8},{10,9... | collective-permute-start | bytes 700424 | tf_op jit(solution)/shard_map/ppermute | solution.py:291
  19.7 15.1 %collective-permute-start.3 = (bf16[64,7296]{1,0:T(8,128)(2,1)S(1)}, bf16[64,7296]{1,0:T(8,128)(2,1)S(1)}, u32[]{:S(2)}, u32[]{:S(2)}) collective-permute-start(bf16[64,7296]{1,0:T(8,128)(2,1)S(1)} %constant_dynamic-update-slice_fusion.refs_0_.refs_4_), channel_id=1, source_target_pairs={{0,32},{4,12},{8,40},{12,20},{16,48},{20,28},{24,56},{28,4},{32,64... | collective-permute-start | bytes 2801672 | tf_op jit(solution)/shard_map/ppermute | solution.py:61
  21.4 19.4 %collective-permute-start.5 = (bf16[64,7296]{1,0:T(8,128)(2,1)S(1)}, bf16[64,7296]{1,0:T(8,128)(2,1)S(1)}, u32[]{:S(2)}, u32[]{:S(2)}) collective-permute-start(bf16[64,7296]{1,0:T(8,128)(2,1)S(1)} %constant_dynamic-update-slice_fusion.refs_0_.refs_4_), channel_id=1, source_target_pairs={{0,96},{4,28},{8,104},{12,4},{16,112},{20,12},{24,120},{28,20},{32... | collective-permute-start | bytes 2801672 | tf_op jit(solution)/shard_map/ppermute | solution.py:61
  23.6 22.6 %collective-permute-start.22 = (bf16[64,7296]{1,0:T(8,128)(2,1)S(1)}, bf16[64,7296]{1,0:T(8,128)(2,1)S(1)}, u32[]{:S(2)}, u32[]{:S(2)}) collective-permute-start(bf16[64,7296]{1,0:T(8,128)(2,1)S(1)} %constant_dynamic-update-slice_fusion.refs_0_.refs_4_), channel_id=1, source_target_pairs={{0,24},{4,100},{8,0},{12,108},{16,8},{20,116},{24,16},{28,124},{32... | collective-permute-start | bytes 2801672 | tf_op jit(solution)/shard_map/ppermute | solution.py:65
  34.8 14.0 %collective-permute-start.4 = (bf16[32,7296]{1,0:T(8,128)(2,1)S(1)}, bf16[32,7296]{1,0:T(8,128)(2,1)S(1)}, u32[]{:S(2)}, u32[]{:S(2)}) collective-permute-start(bf16[32,7296]{1,0:T(8,128)(2,1)S(1)} %slice.40), channel_id=1, source_target_pairs={{0,32},{4,12},{8,40},{12,20},{16,48},{20,28},{24,56},{28,4},{32,64... | collective-permute-start | bytes 1400840 | tf_op jit(solution)/shard_map/ppermute | solution.py:61
  34.9 18.9 %collective-permute-start.21 = (bf16[64,7296]{1,0:T(8,128)(2,1)S(1)}, bf16[64,7296]{1,0:T(8,128)(2,1)S(1)}, u32[]{:S(2)}, u32[]{:S(2)}) collective-permute-start(bf16[64,7296]{1,0:T(8,128)(2,1)S(1)} %constant_dynamic-update-slice_fusion.refs_0_.refs_4_), channel_id=1, source_target_pairs={{0,8},{4,36},{8,16},{12,44},{16,24},{20,52},{24,0},{28,60},{32,40}... | collective-permute-start | bytes 2801672 | tf_op jit(solution)/shard_map/ppermute | solution.py:65
  36.0 16.4 %collective-permute-start.11 = (bf16[64,7168]{1,0:T(8,128)(2,1)S(1)}, bf16[64,7168]{1,0:T(8,128)(2,1)S(1)}, u32[]{:S(2)}, u32[]{:S(2)}) collective-permute-start(bf16[64,7168]{1,0:T(8,128)(2,1)S(1)} %bitcast.4), channel_id=1, source_target_pairs={{0,4},{4,0},{8,12},{12,8},{16,20},{20,16},{24,28},{28,24},{32,36},... | collective-permute-start | bytes 2752520 | tf_op jit(solution)/shard_map/ppermute | solution.py:77
  40.8 11.6 %collective-permute-start.12 = (bf16[64,7168]{1,0:T(8,128)(2,1)S(1)}, bf16[64,7168]{1,0:T(8,128)(2,1)S(1)}, u32[]{:S(2)}, u32[]{:S(2)}) collective-permute-start(bf16[64,7168]{1,0:T(8,128)(2,1)S(1)} %bitcast.9), channel_id=1, source_target_pairs={{0,4},{4,0},{8,12},{12,8},{16,20},{20,16},{24,28},{28,24},{32,36},... | collective-permute-start | bytes 2752520 | tf_op jit(solution)/shard_map/ppermute | solution.py:77
  46.3 8.0 %collective-permute-start.6 = (bf16[32,7296]{1,0:T(8,128)(2,1)S(1)}, bf16[32,7296]{1,0:T(8,128)(2,1)S(1)}, u32[]{:S(2)}, u32[]{:S(2)}) collective-permute-start(bf16[32,7296]{1,0:T(8,128)(2,1)S(1)} %slice.41), channel_id=1, source_target_pairs={{0,96},{4,28},{8,104},{12,4},{16,112},{20,12},{24,120},{28,20},{32... | collective-permute-start | bytes 1400840 | tf_op jit(solution)/shard_map/ppermute | solution.py:61
  48.8 23.1 %collective-permute-start.18 = (bf16[64,7296]{1,0:T(8,128)(2,1)S(1)}, bf16[64,7296]{1,0:T(8,128)(2,1)S(1)}, u32[]{:S(2)}, u32[]{:S(2)}) collective-permute-start(bf16[64,7296]{1,0:T(8,128)(2,1)S(1)} %collective-permute-done.3.refs_0_.refs_9_), channel_id=1, source_target_pairs={{0,24},{4,100},{8,0},{12,108},{16,8},{20,116},{24,16},{28,124},{32... | collective-permute-start | bytes 2801672 | tf_op jit(solution)/shard_map/ppermute | solution.py:65
  52.3 17.2 %collective-permute-start.24 = (bf16[32,7296]{1,0:T(8,128)(2,1)S(1)}, bf16[32,7296]{1,0:T(8,128)(2,1)S(1)}, u32[]{:S(2)}, u32[]{:S(2)}) collective-permute-start(bf16[32,7296]{1,0:T(8,128)(2,1)S(1)} %slice.49), channel_id=1, source_target_pairs={{0,24},{4,100},{8,0},{12,108},{16,8},{20,116},{24,16},{28,124},{32... | collective-permute-start | bytes 1400840 | tf_op jit(solution)/shard_map/ppermute | solution.py:65
  52.4 27.1 %collective-permute-start.14 = (bf16[64,7296]{1,0:T(8,128)(2,1)S(1)}, bf16[64,7296]{1,0:T(8,128)(2,1)S(1)}, u32[]{:S(2)}, u32[]{:S(2)}) collective-permute-start(bf16[64,7296]{1,0:T(8,128)(2,1)S(1)} %collective-permute-done.5.refs_0_.refs_14_), channel_id=1, source_target_pairs={{0,24},{4,100},{8,0},{12,108},{16,8},{20,116},{24,16},{28,124},{32... | collective-permute-start | bytes 2801672 | tf_op jit(solution)/shard_map/ppermute | solution.py:65
  53.8 28.4 %collective-permute-start.13 = (bf16[64,7296]{1,0:T(8,128)(2,1)S(1)}, bf16[64,7296]{1,0:T(8,128)(2,1)S(1)}, u32[]{:S(2)}, u32[]{:S(2)}) collective-permute-start(bf16[64,7296]{1,0:T(8,128)(2,1)S(1)} %collective-permute-done.5.refs_0_.refs_14_), channel_id=1, source_target_pairs={{0,8},{4,36},{8,16},{12,44},{16,24},{20,52},{24,0},{28,60},{32,40}... | collective-permute-start | bytes 2801672 | tf_op jit(solution)/shard_map/ppermute | solution.py:65
  54.3 26.5 %collective-permute-start.17 = (bf16[64,7296]{1,0:T(8,128)(2,1)S(1)}, bf16[64,7296]{1,0:T(8,128)(2,1)S(1)}, u32[]{:S(2)}, u32[]{:S(2)}) collective-permute-start(bf16[64,7296]{1,0:T(8,128)(2,1)S(1)} %collective-permute-done.3.refs_0_.refs_9_), channel_id=1, source_target_pairs={{0,8},{4,36},{8,16},{12,44},{16,24},{20,52},{24,0},{28,60},{32,40}... | collective-permute-start | bytes 2801672 | tf_op jit(solution)/shard_map/ppermute | solution.py:65
  69.5 20.0 %collective-permute-start.8 = (bf16[64,7296]{1,0:T(8,128)(2,1)S(1)}, bf16[64,7296]{1,0:T(8,128)(2,1)S(1)}, u32[]{:S(2)}, u32[]{:S(2)}) collective-permute-start(bf16[64,7296]{1,0:T(8,128)(2,1)S(1)} %constant_dynamic-update-slice_fusion.4.refs_0_.refs_19_), channel_id=1, source_target_pairs={{0,24},{4,100},{8,0},{12,108},{16,8},{20,116},{24,16},{28,124},{32... | collective-permute-start | bytes 2801672 | tf_op jit(solution)/shard_map/ppermute | solution.py:65
  71.9 20.0 %collective-permute-start.7 = (bf16[64,7296]{1,0:T(8,128)(2,1)S(1)}, bf16[64,7296]{1,0:T(8,128)(2,1)S(1)}, u32[]{:S(2)}, u32[]{:S(2)}) collective-permute-start(bf16[64,7296]{1,0:T(8,128)(2,1)S(1)} %constant_dynamic-update-slice_fusion.4.refs_0_.refs_19_), channel_id=1, source_target_pairs={{0,8},{4,36},{8,16},{12,44},{16,24},{20,52},{24,0},{28,60},{32,40}... | collective-permute-start | bytes 2801672 | tf_op jit(solution)/shard_map/ppermute | solution.py:65
  79.5 13.2 %collective-permute-start.23 = (bf16[32,7296]{1,0:T(8,128)(2,1)S(1)}, bf16[32,7296]{1,0:T(8,128)(2,1)S(1)}, u32[]{:S(2)}, u32[]{:S(2)}) collective-permute-start(bf16[32,7296]{1,0:T(8,128)(2,1)S(1)} %slice.48), channel_id=1, source_target_pairs={{0,8},{4,36},{8,16},{12,44},{16,24},{20,52},{24,0},{28,60},{32,40}... | collective-permute-start | bytes 1400840 | tf_op jit(solution)/shard_map/ppermute | solution.py:65
  80.8 13.9 %collective-permute-start.20 = (bf16[32,7296]{1,0:T(8,128)(2,1)S(1)}, bf16[32,7296]{1,0:T(8,128)(2,1)S(1)}, u32[]{:S(2)}, u32[]{:S(2)}) collective-permute-start(bf16[32,7296]{1,0:T(8,128)(2,1)S(1)} %slice.47), channel_id=1, source_target_pairs={{0,24},{4,100},{8,0},{12,108},{16,8},{20,116},{24,16},{28,124},{32... | collective-permute-start | bytes 1400840 | tf_op jit(solution)/shard_map/ppermute | solution.py:65
  82.2 15.5 %collective-permute-start.19 = (bf16[32,7296]{1,0:T(8,128)(2,1)S(1)}, bf16[32,7296]{1,0:T(8,128)(2,1)S(1)}, u32[]{:S(2)}, u32[]{:S(2)}) collective-permute-start(bf16[32,7296]{1,0:T(8,128)(2,1)S(1)} %slice.46), channel_id=1, source_target_pairs={{0,8},{4,36},{8,16},{12,44},{16,24},{20,52},{24,0},{28,60},{32,40}... | collective-permute-start | bytes 1400840 | tf_op jit(solution)/shard_map/ppermute | solution.py:65
  89.5 10.0 %collective-permute-start.16 = (bf16[32,7296]{1,0:T(8,128)(2,1)S(1)}, bf16[32,7296]{1,0:T(8,128)(2,1)S(1)}, u32[]{:S(2)}, u32[]{:S(2)}) collective-permute-start(bf16[32,7296]{1,0:T(8,128)(2,1)S(1)} %slice.45), channel_id=1, source_target_pairs={{0,24},{4,100},{8,0},{12,108},{16,8},{20,116},{24,16},{28,124},{32... | collective-permute-start | bytes 1400840 | tf_op jit(solution)/shard_map/ppermute | solution.py:65
  91.9 10.9 %collective-permute-start.15 = (bf16[32,7296]{1,0:T(8,128)(2,1)S(1)}, bf16[32,7296]{1,0:T(8,128)(2,1)S(1)}, u32[]{:S(2)}, u32[]{:S(2)}) collective-permute-start(bf16[32,7296]{1,0:T(8,128)(2,1)S(1)} %slice.44), channel_id=1, source_target_pairs={{0,8},{4,36},{8,16},{12,44},{16,24},{20,52},{24,0},{28,60},{32,40}... | collective-permute-start | bytes 1400840 | tf_op jit(solution)/shard_map/ppermute | solution.py:65
  92.8 11.8 %collective-permute-start.10 = (bf16[32,7296]{1,0:T(8,128)(2,1)S(1)}, bf16[32,7296]{1,0:T(8,128)(2,1)S(1)}, u32[]{:S(2)}, u32[]{:S(2)}) collective-permute-start(bf16[32,7296]{1,0:T(8,128)(2,1)S(1)} %slice.43), channel_id=1, source_target_pairs={{0,24},{4,100},{8,0},{12,108},{16,8},{20,116},{24,16},{28,124},{32... | collective-permute-start | bytes 1400840 | tf_op jit(solution)/shard_map/ppermute | solution.py:65
  94.7 13.0 %collective-permute-start.9 = (bf16[32,7296]{1,0:T(8,128)(2,1)S(1)}, bf16[32,7296]{1,0:T(8,128)(2,1)S(1)}, u32[]{:S(2)}, u32[]{:S(2)}) collective-permute-start(bf16[32,7296]{1,0:T(8,128)(2,1)S(1)} %slice.42), channel_id=1, source_target_pairs={{0,8},{4,36},{8,16},{12,44},{16,24},{20,52},{24,0},{28,60},{32,40}... | collective-permute-start | bytes 1400840 | tf_op jit(solution)/shard_map/ppermute | solution.py:65
  109.0 8.5 %collective-permute-start.29 = (bf16[1024,128]{1,0:T(8,128)(2,1)S(1)}, bf16[1024,128]{1,0:T(8,128)(2,1)S(1)}, u32[]{:S(2)}, u32[]{:S(2)}) collective-permute-start(bf16[1024,128]{1,0:T(8,128)(2,1)S(1)} %get-tuple-element.35.own), channel_id=1, source_target_pairs={{0,96},{4,100},{8,104},{12,108},{16,112},{20,116},{24,120},{28,124... | collective-permute-start | bytes 786440 | tf_op jit(solution)/shard_map/ppermute | solution.py:69
  109.5 8.1 %collective-permute-start.28 = (bf16[1024,128]{1,0:T(8,128)(2,1)S(1)}, bf16[1024,128]{1,0:T(8,128)(2,1)S(1)}, u32[]{:S(2)}, u32[]{:S(2)}) collective-permute-start(bf16[1024,128]{1,0:T(8,128)(2,1)S(1)} %get-tuple-element.35.own), channel_id=1, source_target_pairs={{0,32},{4,36},{8,40},{12,44},{16,48},{20,52},{24,56},{28,60},{32,6... | collective-permute-start | bytes 786440 | tf_op jit(solution)/shard_map/ppermute | solution.py:69
  119.8 19.0 %collective-permute-start.32 = (bf16[224,7168]{1,0:T(8,128)(2,1)S(1)}, bf16[224,7168]{1,0:T(8,128)(2,1)S(1)}, u32[]{:S(2)}, u32[]{:S(2)}) collective-permute-start(bf16[224,7168]{1,0:T(8,128)(2,1)S(1)} %shard_map.75), channel_id=1, source_target_pairs={{0,4},{4,0},{8,12},{12,8},{16,20},{20,16},{24,28},{28,24},{32,36},... | collective-permute-start | bytes 9633800 | tf_op jit(solution)/shard_map/ppermute | solution.py:77
  122.7 9.4 %collective-permute-start.30 = (bf16[1024,128]{1,0:T(8,128)(2,1)S(1)}, bf16[1024,128]{1,0:T(8,128)(2,1)S(1)}, u32[]{:S(2)}, u32[]{:S(2)}) collective-permute-start(bf16[1024,128]{1,0:T(8,128)(2,1)S(1)} %get-tuple-element.35.own), channel_id=1, source_target_pairs={{0,64},{4,68},{8,72},{12,76},{16,80},{20,84},{24,88},{28,92},{32,9... | collective-permute-start | bytes 786440 | tf_op jit(solution)/shard_map/ppermute | solution.py:69
  123.7 9.1 %collective-permute-start.27 = (bf16[1024,128]{1,0:T(8,128)(2,1)S(1)}, bf16[1024,128]{1,0:T(8,128)(2,1)S(1)}, u32[]{:S(2)}, u32[]{:S(2)}) collective-permute-start(bf16[1024,128]{1,0:T(8,128)(2,1)S(1)} %get-tuple-element.35.own), channel_id=1, source_target_pairs={{0,16},{4,20},{8,24},{12,28},{16,0},{20,4},{24,8},{28,12},{32,48},... | collective-permute-start | bytes 786440 | tf_op jit(solution)/shard_map/ppermute | solution.py:73
  136.0 9.1 %collective-permute-start.33 = (bf16[64,512]{1,0:T(8,128)(2,1)S(1)}, bf16[64,512]{1,0:T(8,128)(2,1)S(1)}, u32[]{:S(2)}, u32[]{:S(2)}) collective-permute-start(bf16[64,512]{1,0:T(8,128)(2,1)S(1)} %get-tuple-element.50), channel_id=1, source_target_pairs={{0,8},{4,12},{8,16},{12,20},{16,24},{20,28},{24,0},{28,4},{32,40},... | collective-permute-start | bytes 196616 | tf_op jit(solution)/shard_map/ppermute | solution.py:73
  136.1 9.0 %collective-permute-start.34 = (bf16[64,512]{1,0:T(8,128)(2,1)S(1)}, bf16[64,512]{1,0:T(8,128)(2,1)S(1)}, u32[]{:S(2)}, u32[]{:S(2)}) collective-permute-start(bf16[64,512]{1,0:T(8,128)(2,1)S(1)} %get-tuple-element.51), channel_id=1, source_target_pairs={{0,24},{4,28},{8,0},{12,4},{16,8},{20,12},{24,16},{28,20},{32,56},... | collective-permute-start | bytes 196616 | tf_op jit(solution)/shard_map/ppermute | solution.py:73
  (9 other events, 101.8 us)

commit v3 on v2

--- a/solution.py
+++ b/solution.py
@@ -82,10 +82,6 @@
     up = move(value, 1)
     down = move(value, -1)
     return (up, down, move(up[:half], 1), move(down[half:], -1))
-
-
-def direct_ring(value, move):
-    return move(value, 1), move(value, -1), move(value, 2)
 
 
 def dispatch_kernel(routes, slots, tokens, *outs):
@@ -109,22 +105,24 @@
 
 
 def dispatch(routes, slots, tokens):
+    in_hbm = [pltpu.with_memory_space_constraint(v.T, pltpu.HBM) for v in (routes, slots)]
     return pl.pallas_call(
         dispatch_kernel,
         out_shape=[jax.ShapeDtypeStruct((CAP, SENT), BF16)] * 4,
         in_specs=[VMEM] * 3,
         out_specs=[VMEM] * 4,
         compiler_params=params(32),
-    )(routes.T, slots.T, tokens)
-
-
-def hidden_kernel(group, *refs):
-    size = len(refs) - (8 if group else 7)
+    )(*in_hbm, *pinned([tokens]))
+
+
+def hidden_kernel(spots, first, *refs):
+    size = len(refs) - (7 if first else 8)
+    height = 64 * len(spots)
     pieces, (g, gs, u, us) = refs[:size], refs[size : size + 4]
     hidden, window, count = refs[-3:]
     y, z, core = spot()
     base, _ = gram_start()
-    total = jnp.zeros((256, 256), F32)
+    total = jnp.zeros((height, 256), F32)
     for start in range(0, WIDTH, CHUNK):
         rows = jnp.concatenate([p[:, start : start + CHUNK] for p in pieces], 0)
         weights = jnp.concatenate([w[:, start : start + CHUNK] for w in (g, gs, u, us)], 0)
@@ -135,36 +133,42 @@
     value = gate / (1.0 + jnp.exp(-gate)) * upward
     value = jnp.where(core == 1, pltpu.roll(value, 64, 1), value).astype(BF16)
     seen = jnp.concatenate([p[:, WIDTH:] for p in pieces], 0).astype(F32)
-    count[...] = jnp.broadcast_to(jnp.sum(seen, axis=0, keepdims=True), (16, FLAG))
-    if group:
+    for part in range(height // 256):
+        total_seen = jnp.sum(seen[256 * part : 256 * part + 256], axis=0, keepdims=True)
+        count[:, FLAG * part : FLAG * part + FLAG] = jnp.broadcast_to(total_seen, (16, FLAG))
+    if not first:
         hidden[...] = refs[size + 4][...]
-    for j in range(4):
-        far = (jnp.where(core == 0, y, z) + ORIGIN[group] + SIDE) % SIDE
-        near = (jnp.where(core == 0, z, y) + ORIGIN[j] + SIDE) % SIDE
+    for j, (far, near) in enumerate(spots):
+        far = (jnp.where(core == 0, y, z) + far + SIDE) % SIDE
+        near = (jnp.where(core == 0, z, y) + near + SIDE) % SIDE
         slot = jnp.where(core == 0, far * SIDE + near, near * SIDE + far)
         hidden[pl.ds(pl.multiple_of(slot * 64, 64), 64), :] = value[64 * j : 64 * j + 64]
     base = pl.multiple_of(base, 128)
     window[...] = jnp.concatenate([p[:, pl.ds(base, WINDOW)] for p in pieces], 0).T
 
 
-def hidden_work(group, pieces, weights, before):
-    return pl.pallas_call(
-        functools.partial(hidden_kernel, group),
+def hidden_work(spots, pieces, weights, before):
+    height = 64 * len(spots)
+    return pl.pallas_call(
+        functools.partial(hidden_kernel, spots, not before),
         out_shape=[
             jax.ShapeDtypeStruct((1024, 128), BF16),
-            jax.ShapeDtypeStruct((WINDOW, 256), BF16),
-            jax.ShapeDtypeStruct((16, FLAG), F32),
+            jax.ShapeDtypeStruct((WINDOW, height), BF16),
+            jax.ShapeDtypeStruct((16, height // 256 * FLAG), F32),
         ],
         in_specs=[VMEM] * (len(pieces) + 4 + len(before)),
         out_specs=[VMEM] * 3,
         compiler_params=params(12),
         cost_estimate=pl.CostEstimate(
-            flops=2 * 256 * 256 * WIDTH, bytes_accessed=8 << 20, transcendentals=256 * 128
+            flops=2 * height * 256 * WIDTH,
+            bytes_accessed=8 << 20,
+            transcendentals=height * 128,
         ),
     )(*pinned(pieces), *pinned(weights), *pinned(before))
 
 
-def down_kernel(own, z0, z1, z2, y0, y1, y2, n0, n1, n2, n3, keep, send, tile):
+def down_kernel(own, z0, z1, z2, y0, y1, y2, *refs):
+    counts, (keep, send, tile) = refs[:-3], refs[-3:]
     core = spot()[2]
     left = jnp.concatenate([own[...], z0[...], z1[...], z2[...]], 1)
     right = jnp.concatenate([own[...], y0[...], y1[...], y2[...]], 1)
@@ -176,7 +180,7 @@
         other = pl.multiple_of(128 * j + 64 - 64 * core, 64)
         keep[64 * j : 64 * j + 64, :] = tile[pl.ds(mine, 64), :]
         send[64 * j : 64 * j + 64, :] = tile[pl.ds(other, 64), :].astype(BF16)
-    counts = jnp.concatenate([n0[...], n1[...], n2[...], n3[...]], 1)
+    counts = jnp.concatenate([n[...] for n in counts], 1)
     keep[256:, :] = counts
     send[256:, :] = counts.astype(BF16)
 
@@ -188,7 +192,7 @@
             jax.ShapeDtypeStruct((272, 512), F32),
             jax.ShapeDtypeStruct((272, 512), BF16),
         ],
-        in_specs=[VMEM] * 11,
+        in_specs=[VMEM] * (7 + len(counts)),
         out_specs=[VMEM] * 2,
         scratch_shapes=[pltpu.VMEM((512, 512), F32)],
         compiler_params=params(12),
@@ -201,7 +205,7 @@
 def sum_kernel(keep, got, *outs):
     for j in range(4):
         rows = pl.ds(64 * j, 64)
-        outs[j][...] = (keep[rows, :] + got[rows, :].astype(F32)).astype(outs[j].dtype)
+        outs[j][...] = keep[rows, :] + got[rows, :].astype(F32)
     counts = keep[256:264, :] + got[256:, :].astype(F32)[:8]
     total = sum(counts[:, 128 * i : 128 * i + 128] for i in range(4))
     outs[4][...] = 2.0 / total
@@ -210,7 +214,7 @@
 def sum_blocks(keep, got):
     return pl.pallas_call(
         sum_kernel,
-        out_shape=[jax.ShapeDtypeStruct((64, 512), F32 if j == 0 else BF16) for j in range(4)]
+        out_shape=[jax.ShapeDtypeStruct((64, 512), F32)] * 4
         + [jax.ShapeDtypeStruct((8, 128), F32)],
         in_specs=[VMEM] * 2,
         out_specs=[VMEM] * 5,
@@ -225,7 +229,7 @@
             from_y = (y + ORIGIN[i] + SIDE) % SIDE
             from_z = (z + ORIGIN[j] + SIDE) % SIDE
             start = pl.multiple_of((from_y * SIDE + from_z) * 128, 128)
-            part = block[:, 128 * i : 128 * i + 128].astype(F32)
+            part = block[:, 128 * i : 128 * i + 128]
             out[0, :, pl.ds(start, 128)] = part * factor[0:1, :]
 
 
@@ -239,9 +243,9 @@
     )(*pinned((*blocks, factor)))
 
 
-def gram_kernel(mine, *refs):
+def gram_kernel(mine, groups, *refs):
     size = len(refs) - (3 if mine else 1)
-    windows, pieces, rest = refs[:4], refs[4:size], refs[size:]
+    windows, pieces, rest = refs[:groups], refs[groups:size], refs[size:]
     core = spot()[2]
     _, shift = gram_start()
     first = shift + core * 224 if mine else shift + 224 - core * 224
@@ -259,22 +263,24 @@
 
 def gram_work(windows, pieces, got=None, factor=None):
     mine = got is not None
-    shape = (224, WIDTH)
     if mine:
+        out_shape = jax.ShapeDtypeStruct((1, 224, WIDTH), F32)
         out_spec = pl.BlockSpec((1, 224, CHUNK), lambda n: (0, 0, n))
     else:
+        out_shape = jax.ShapeDtypeStruct((224, WIDTH), BF16)
         out_spec = pl.BlockSpec((224, CHUNK), lambda n: (0, n))
-    return pl.pallas_call(
-        functools.partial(gram_kernel, mine),
+    operands = (*windows, *pieces) + ((got, factor) if mine else ())
+    return pl.pallas_call(
+        functools.partial(gram_kernel, mine, len(windows)),
         grid=(WIDTH // CHUNK,),
-        out_shape=jax.ShapeDtypeStruct((1,) + shape, F32) if mine else jax.ShapeDtypeStruct(shape, BF16),
-        in_specs=[VMEM] * (4 + len(pieces)) + ([VMEM] * 2 if mine else []),
+        out_shape=out_shape,
+        in_specs=[VMEM] * len(operands),
         out_specs=out_spec,
         compiler_params=params(10),
         cost_estimate=pl.CostEstimate(
             flops=2 * 224 * WIDTH * 1024, bytes_accessed=24 << 20, transcendentals=0
         ),
-    )(*pinned(windows), *pinned(pieces), *(pinned((got, factor)) if mine else ()))
+    )(*pinned(operands))
 
 
 def after(value, done):
@@ -292,24 +298,30 @@
     shard = jnp.concatenate(parts, 0)
 
     up, down, up2, down2 = ring(shard, major)
+    far = jnp.concatenate([up2, down2], 0)
     groups = []
-    for piece in (shard, up, down, jnp.concatenate([up2, down2], 0)):
-        groups.append((piece,) + ring(piece, minor))
+    for origin, piece in zip(ORIGIN, (shard, up, down, far)):
+        groups.append(((origin,), (piece,) + ring(piece, minor)))
     windows, counts, before = [], [], ()
-    for index, group in enumerate(groups):
-        hidden, window, count = hidden_work(index, group, weights, before)
+    for origins, pieces in groups:
+        spots = [(far, near) for near in ORIGIN for far in origins]
+        hidden, window, count = hidden_work(spots, pieces, weights, before)
         before = (hidden,)
         windows.append(window)
         counts.append(count)
 
-    ring_z = direct_ring(hidden, along_z)
-    ring_y = direct_ring(hidden, along_y)
-    pieces = [piece for group in groups for piece in group]
-    send, _ = after(gram_work(windows, pieces), (ring_z[:2], ring_y[:2]))
+    z_down, y_down = along_z(hidden, -1), along_y(hidden, -1)
+    y_up, z_far, y_far = along_y(hidden, 1), along_z(hidden, 2), along_y(hidden, 2)
+    z_up = along_z(hidden, 1)
+    hops = (z_up, z_down, z_far, y_up, y_down, y_far)
+    pieces = [piece for _, group in groups for piece in group]
+    send = gram_work(windows, pieces)
+    hops, send = after(hops, send)
+    down_keep, down_send = down_work(hidden, hops[:3], hops[3:], counts)
+    down_got = sibling(down_send)
+    send, down_got = after(send, down_got)
     got = sibling(send)
-
-    down_keep, down_send = down_work(hidden, ring_z, ring_y, counts)
-    *sums, factor = sum_blocks(down_keep, sibling(down_send))
+    *sums, factor = sum_blocks(down_keep, down_got)
     down_blocks = [
         sums[0],
         along_z(sums[2], 1),

time: 146 us -> 144 us (0.986)
  waiting for transfers between devices: 69.2 us -> 66 us
  starting transfers between devices: 53.3 us -> 55.3 us
    ppermute x3, waiting for transfers between devices: 8.51 us -> 3.31 us  [along_y(): return lax.ppermute(value, 'dp', steps((step, 0), (step, 0)))]
    ppermute x4, waiting for transfers between devices: 1.19 us -> 3.77 us  [sibling(): return lax.ppermute(value, 'dp', [(i, i ^ 1) for i in range(2 * CHIPS)])]
    unnamed x14 -> x10, local copies, waits for them, and re-layouts: 3.66 us -> 2.26 us
  transfers between devices with their start and end apart: 36 -> 36, of which waited for: 19 -> 21; matrix products, arithmetic and copies ran while one was open for 0% -> 0% of each run, Pallas kernels for 11% -> 10%
where the time goes in v3:
time: 144 us
  waiting for transfers between devices  66 us (46%)
  starting transfers between devices  55.3 us (38%)
  Pallas kernels  19.3 us (13%)
  local copies, waits for them, and re-layouts  2.64 us (2%)
    ppermute x16, waiting for transfers between devices, minor(): return lax.ppermute(value, 'dp', steps((0, step), (step, 0)))  36.7 us
    ppermute x16, starting transfers between devices, minor(): return lax.ppermute(value, 'dp', steps((0, step), (step, 0)))  21.6 us
    ppermute x4, starting transfers between devices, sibling(): return lax.ppermute(value, 'dp', [(i, i ^ 1) for i in range(2 * CHIPS)])  12.9 us
    ppermute x4, waiting for transfers between devices, major(): return lax.ppermute(value, 'dp', steps((step, 0), (0, step)))  11.1 us
    pallas_call x2, Pallas kernels, gram_work(): pl.pallas_call(functools.partial(gram_kernel, mine, len(windows)), grid=(...  11.1 us
    ppermute x3, waiting for transfers between devices, local(): lax.ppermute(blocks[step], 'expert', [(i, (i + step) % 4) for i in range(...  8.9 us
    ppermute x4, starting transfers between devices, major(): return lax.ppermute(value, 'dp', steps((step, 0), (0, step)))  6.48 us
    ppermute x6, starting transfers between devices, along_z(): return lax.ppermute(value, 'dp', steps((0, step), (0, step)))  6.42 us
  transfers between devices with their start and end apart: 36, of which 21 were waited for; matrix products, arithmetic and copies ran while one was open for 0% of the time, Pallas kernels for 10%

profile of v3, /device:TPU:1, one launch (start us, length us, event | category | flops | bytes accessed | tf_op | source)
XLA Modules:
  0.0 144.2 jit_solution(13063823082044937094)
XLA Ops:
  0.7 2.2 %copy-done.2 = bf16[256,7168]{1,0:T(8,128)(2,1)S(1)} copy-done((bf16[256,7168]{1,0:T(8,128)(2,1)S(1)}, bf16[256,7168]{1,0:T(8,128)(2,1)}, u32[]{:S(2)}) %copy-start.2) | copy-done | bytes 3670040
  4.3 2.1 %collective-permute-start = (bf16[16,7296]{1,0:T(8,128)(2,1)S(1)}, bf16[16,7296]{1,0:T(8,128)(2,1)S(1)}, u32[]{:S(2)}, u32[]{:S(2)}) collective-permute-start(bf16[16,7296]{1,0:T(8,128)(2,1)S(1)} %get-tuple-element.37), channel_id=1, source_target_pairs={{0,1},{1,2},{2,3},{3,0},{4,5},{5,6},{6,7},{7,4},{8,9},{9,10},{10,1... | collective-permute-start | bytes 700424 | tf_op jit(solution)/shard_map/ppermute | solution.py:297
  6.4 2.5 %collective-permute-start.1 = (bf16[16,7296]{1,0:T(8,128)(2,1)S(1)}, bf16[16,7296]{1,0:T(8,128)(2,1)S(1)}, u32[]{:S(2)}, u32[]{:S(2)}) collective-permute-start(bf16[16,7296]{1,0:T(8,128)(2,1)S(1)} %get-tuple-element.38), channel_id=1, source_target_pairs={{0,2},{1,3},{2,0},{3,1},{4,6},{5,7},{6,4},{7,5},{8,10},{9,11},{10,... | collective-permute-start | bytes 700424 | tf_op jit(solution)/shard_map/ppermute | solution.py:297
  10.0 2.6 %collective-permute-done = bf16[16,7296]{1,0:T(8,128)(2,1)S(1)} collective-permute-done((bf16[16,7296]{1,0:T(8,128)(2,1)S(1)}, bf16[16,7296]{1,0:T(8,128)(2,1)S(1)}, u32[]{:S(2)}, u32[]{:S(2)}) %collective-permute-start) | collective-permute-done | bytes 233504 | tf_op jit(solution)/shard_map/ppermute | solution.py:297
  12.7 6.3 %collective-permute-done.1 = bf16[16,7296]{1,0:T(8,128)(2,1)S(1)} collective-permute-done((bf16[16,7296]{1,0:T(8,128)(2,1)S(1)}, bf16[16,7296]{1,0:T(8,128)(2,1)S(1)}, u32[]{:S(2)}, u32[]{:S(2)}) %collective-permute-start.1) | collective-permute-done | bytes 233504 | tf_op jit(solution)/shard_map/ppermute | solution.py:297
  19.0 1.7 %collective-permute-start.3 = (bf16[64,7296]{1,0:T(8,128)(2,1)S(1)}, bf16[64,7296]{1,0:T(8,128)(2,1)S(1)}, u32[]{:S(2)}, u32[]{:S(2)}) collective-permute-start(bf16[64,7296]{1,0:T(8,128)(2,1)S(1)} %constant_dynamic-update-slice_fusion.refs_0_.refs_4_), channel_id=1, source_target_pairs={{0,32},{4,12},{8,40},{12,20},{16,48},{20,28},{24,56},{28,4},{32,64... | collective-permute-start | bytes 2801672 | tf_op jit(solution)/shard_map/ppermute | solution.py:61
  20.7 2.2 %collective-permute-start.5 = (bf16[64,7296]{1,0:T(8,128)(2,1)S(1)}, bf16[64,7296]{1,0:T(8,128)(2,1)S(1)}, u32[]{:S(2)}, u32[]{:S(2)}) collective-permute-start(bf16[64,7296]{1,0:T(8,128)(2,1)S(1)} %constant_dynamic-update-slice_fusion.refs_0_.refs_4_), channel_id=1, source_target_pairs={{0,96},{4,28},{8,104},{12,4},{16,112},{20,12},{24,120},{28,20},{32... | collective-permute-start | bytes 2801672 | tf_op jit(solution)/shard_map/ppermute | solution.py:61
  22.9 2.7 %collective-permute-start.22 = (bf16[64,7296]{1,0:T(8,128)(2,1)S(1)}, bf16[64,7296]{1,0:T(8,128)(2,1)S(1)}, u32[]{:S(2)}, u32[]{:S(2)}) collective-permute-start(bf16[64,7296]{1,0:T(8,128)(2,1)S(1)} %constant_dynamic-update-slice_fusion.refs_0_.refs_4_), channel_id=1, source_target_pairs={{0,24},{4,100},{8,0},{12,108},{16,8},{20,116},{24,16},{28,124},{32... | collective-permute-start | bytes 2801672 | tf_op jit(solution)/shard_map/ppermute | solution.py:65
  25.7 8.4 %collective-permute-done.3.refs_0_.refs_9_ = bf16[64,7296]{1,0:T(8,128)(2,1)S(1)} collective-permute-done((bf16[64,7296]{1,0:T(8,128)(2,1)S(1)}, bf16[64,7296]{1,0:T(8,128)(2,1)S(1)}, u32[]{:S(2)}, u32[]{:S(2)}) %collective-permute-start.3) | collective-permute-done | bytes 933920 | tf_op jit(solution)/shard_map/ppermute | solution.py:61
  35.3 2.5 %collective-permute-start.11 = (bf16[64,7168]{1,0:T(8,128)(2,1)S(1)}, bf16[64,7168]{1,0:T(8,128)(2,1)S(1)}, u32[]{:S(2)}, u32[]{:S(2)}) collective-permute-start(bf16[64,7168]{1,0:T(8,128)(2,1)S(1)} %bitcast.4), channel_id=1, source_target_pairs={{0,4},{4,0},{8,12},{12,8},{16,20},{20,16},{24,28},{28,24},{32,36},... | collective-permute-start | bytes 2752520 | tf_op jit(solution)/shard_map/ppermute | solution.py:77
  37.8 2.3 %collective-permute-done.5.refs_0_.refs_14_ = bf16[64,7296]{1,0:T(8,128)(2,1)S(1)} collective-permute-done((bf16[64,7296]{1,0:T(8,128)(2,1)S(1)}, bf16[64,7296]{1,0:T(8,128)(2,1)S(1)}, u32[]{:S(2)}, u32[]{:S(2)}) %collective-permute-start.5) | collective-permute-done | bytes 933920 | tf_op jit(solution)/shard_map/ppermute | solution.py:61
  40.1 5.4 %collective-permute-start.12 = (bf16[64,7168]{1,0:T(8,128)(2,1)S(1)}, bf16[64,7168]{1,0:T(8,128)(2,1)S(1)}, u32[]{:S(2)}, u32[]{:S(2)}) collective-permute-start(bf16[64,7168]{1,0:T(8,128)(2,1)S(1)} %bitcast.9), channel_id=1, source_target_pairs={{0,4},{4,0},{8,12},{12,8},{16,20},{20,16},{24,28},{28,24},{32,36},... | collective-permute-start | bytes 2752520 | tf_op jit(solution)/shard_map/ppermute | solution.py:77
  45.6 2.5 %collective-permute-start.6 = (bf16[32,7296]{1,0:T(8,128)(2,1)S(1)}, bf16[32,7296]{1,0:T(8,128)(2,1)S(1)}, u32[]{:S(2)}, u32[]{:S(2)}) collective-permute-start(bf16[32,7296]{1,0:T(8,128)(2,1)S(1)} %slice.41), channel_id=1, source_target_pairs={{0,96},{4,28},{8,104},{12,4},{16,112},{20,12},{24,120},{28,20},{32... | collective-permute-start | bytes 1400840 | tf_op jit(solution)/shard_map/ppermute | solution.py:61
  48.1 3.5 %collective-permute-start.18 = (bf16[64,7296]{1,0:T(8,128)(2,1)S(1)}, bf16[64,7296]{1,0:T(8,128)(2,1)S(1)}, u32[]{:S(2)}, u32[]{:S(2)}) collective-permute-start(bf16[64,7296]{1,0:T(8,128)(2,1)S(1)} %collective-permute-done.3.refs_0_.refs_9_), channel_id=1, source_target_pairs={{0,24},{4,100},{8,0},{12,108},{16,8},{20,116},{24,16},{28,124},{32... | collective-permute-start | bytes 2801672 | tf_op jit(solution)/shard_map/ppermute | solution.py:65
  53.6 3.4 %collective-permute-start.17 = (bf16[64,7296]{1,0:T(8,128)(2,1)S(1)}, bf16[64,7296]{1,0:T(8,128)(2,1)S(1)}, u32[]{:S(2)}, u32[]{:S(2)}) collective-permute-start(bf16[64,7296]{1,0:T(8,128)(2,1)S(1)} %collective-permute-done.3.refs_0_.refs_9_), channel_id=1, source_target_pairs={{0,8},{4,36},{8,16},{12,44},{16,24},{20,52},{24,0},{28,60},{32,40}... | collective-permute-start | bytes 2801672 | tf_op jit(solution)/shard_map/ppermute | solution.py:65
  57.0 11.8 %collective-permute-done.24.refs_4_.refs_8_ = bf16[32,7296]{1,0:T(8,128)(2,1)S(1)} collective-permute-done((bf16[32,7296]{1,0:T(8,128)(2,1)S(1)}, bf16[32,7296]{1,0:T(8,128)(2,1)S(1)}, u32[]{:S(2)}, u32[]{:S(2)}) %collective-permute-start.24) | collective-permute-done | bytes 466976 | tf_op jit(solution)/shard_map/ppermute | solution.py:65
  68.8 2.4 %collective-permute-start.8 = (bf16[64,7296]{1,0:T(8,128)(2,1)S(1)}, bf16[64,7296]{1,0:T(8,128)(2,1)S(1)}, u32[]{:S(2)}, u32[]{:S(2)}) collective-permute-start(bf16[64,7296]{1,0:T(8,128)(2,1)S(1)} %constant_dynamic-update-slice_fusion.4.refs_0_.refs_19_), channel_id=1, source_target_pairs={{0,24},{4,100},{8,0},{12,108},{16,8},{20,116},{24,16},{28,124},{32... | collective-permute-start | bytes 2801672 | tf_op jit(solution)/shard_map/ppermute | solution.py:65
  71.3 7.5 %collective-permute-done.14.refs_2_.refs_16_ = bf16[64,7296]{1,0:T(8,128)(2,1)S(1)} collective-permute-done((bf16[64,7296]{1,0:T(8,128)(2,1)S(1)}, bf16[64,7296]{1,0:T(8,128)(2,1)S(1)}, u32[]{:S(2)}, u32[]{:S(2)}) %collective-permute-start.14) | collective-permute-done | bytes 933920 | tf_op jit(solution)/shard_map/ppermute | solution.py:65
  81.8 7.0 %collective-permute-done.8.refs_2_.refs_21_ = bf16[64,7296]{1,0:T(8,128)(2,1)S(1)} collective-permute-done((bf16[64,7296]{1,0:T(8,128)(2,1)S(1)}, bf16[64,7296]{1,0:T(8,128)(2,1)S(1)}, u32[]{:S(2)}, u32[]{:S(2)}) %collective-permute-start.8) | collective-permute-done | bytes 933920 | tf_op jit(solution)/shard_map/ppermute | solution.py:65
  88.8 2.4 %collective-permute-start.16 = (bf16[32,7296]{1,0:T(8,128)(2,1)S(1)}, bf16[32,7296]{1,0:T(8,128)(2,1)S(1)}, u32[]{:S(2)}, u32[]{:S(2)}) collective-permute-start(bf16[32,7296]{1,0:T(8,128)(2,1)S(1)} %slice.45), channel_id=1, source_target_pairs={{0,24},{4,100},{8,0},{12,108},{16,8},{20,116},{24,16},{28,124},{32... | collective-permute-start | bytes 1400840 | tf_op jit(solution)/shard_map/ppermute | solution.py:65
  92.1 2.0 %collective-permute-start.10 = (bf16[32,7296]{1,0:T(8,128)(2,1)S(1)}, bf16[32,7296]{1,0:T(8,128)(2,1)S(1)}, u32[]{:S(2)}, u32[]{:S(2)}) collective-permute-start(bf16[32,7296]{1,0:T(8,128)(2,1)S(1)} %slice.43), channel_id=1, source_target_pairs={{0,24},{4,100},{8,0},{12,108},{16,8},{20,116},{24,16},{28,124},{32... | collective-permute-start | bytes 1400840 | tf_op jit(solution)/shard_map/ppermute | solution.py:65
  98.8 3.2 %collective-permute-done.15.refs_3_.refs_17_ = bf16[32,7296]{1,0:T(8,128)(2,1)S(1)} collective-permute-done((bf16[32,7296]{1,0:T(8,128)(2,1)S(1)}, bf16[32,7296]{1,0:T(8,128)(2,1)S(1)}, u32[]{:S(2)}, u32[]{:S(2)}) %collective-permute-start.15) | collective-permute-done | bytes 466976 | tf_op jit(solution)/shard_map/ppermute | solution.py:65
  103.8 3.2 %collective-permute-done.9.refs_3_.refs_22_ = bf16[32,7296]{1,0:T(8,128)(2,1)S(1)} collective-permute-done((bf16[32,7296]{1,0:T(8,128)(2,1)S(1)}, bf16[32,7296]{1,0:T(8,128)(2,1)S(1)}, u32[]{:S(2)}, u32[]{:S(2)}) %collective-permute-start.9) | collective-permute-done | bytes 466976 | tf_op jit(solution)/shard_map/ppermute | solution.py:65
  110.5 2.5 %collective-permute-start.27 = (bf16[1024,128]{1,0:T(8,128)(2,1)S(1)}, bf16[1024,128]{1,0:T(8,128)(2,1)S(1)}, u32[]{:S(2)}, u32[]{:S(2)}) collective-permute-start(bf16[1024,128]{1,0:T(8,128)(2,1)S(1)} %get-tuple-element.43.own), channel_id=1, source_target_pairs={{0,16},{4,20},{8,24},{12,28},{16,0},{20,4},{24,8},{28,12},{32,48},... | collective-permute-start | bytes 786440 | tf_op jit(solution)/shard_map/ppermute | solution.py:73
  113.7 1.5 %collective-permute-done.30.y2 = bf16[1024,128]{1,0:T(8,128)(2,1)S(1)} collective-permute-done((bf16[1024,128]{1,0:T(8,128)(2,1)S(1)}, bf16[1024,128]{1,0:T(8,128)(2,1)S(1)}, u32[]{:S(2)}, u32[]{:S(2)}) %collective-permute-start.30) | collective-permute-done | bytes 262176 | tf_op jit(solution)/shard_map/ppermute | solution.py:69
  115.7 4.8 %shard_map.73 = bf16[224,7168]{1,0:T(8,128)(2,1)S(1)} custom-call(bf16[512,256]{1,0:T(8,128)(2,1)S(1)} %get-tuple-element.44.refs_0_, bf16[512,256]{1,0:T(8,128)(2,1)S(1)} %get-tuple-element.45.refs_1_, bf16[512,256]{1,0:T(8,128)(2,1)S(1)} %get-tuple-element.46.refs_2_, bf16[512,256]{1,0:T(8,128)(2,1)S(1)} %get-tuple-element.47.refs_3_, ...), custom_call_target="tpu_custom_call" | custom-call | flops 3288334336 | bytes 25165824 | tf_op jit(solution)/shard_map/pallas_call | solution.py:273
  120.5 1.8 %collective-permute-done.28.y0 = bf16[1024,128]{1,0:T(8,128)(2,1)S(1)} collective-permute-done((bf16[1024,128]{1,0:T(8,128)(2,1)S(1)}, bf16[1024,128]{1,0:T(8,128)(2,1)S(1)}, u32[]{:S(2)}, u32[]{:S(2)}) %collective-permute-start.28) | collective-permute-done | bytes 262176 | tf_op jit(solution)/shard_map/ppermute | solution.py:69
  122.3 1.8 %collective-permute-done.26.z1 = bf16[1024,128]{1,0:T(8,128)(2,1)S(1)} collective-permute-done((bf16[1024,128]{1,0:T(8,128)(2,1)S(1)}, bf16[1024,128]{1,0:T(8,128)(2,1)S(1)}, u32[]{:S(2)}, u32[]{:S(2)}) %collective-permute-start.26) | collective-permute-done | bytes 262176 | tf_op jit(solution)/shard_map/ppermute | solution.py:73
  125.4 4.6 %collective-permute-start.31 = (bf16[272,512]{1,0:T(8,128)(2,1)S(1)}, bf16[272,512]{1,0:T(8,128)(2,1)S(1)}, u32[]{:S(2)}, u32[]{:S(2)}) collective-permute-start(bf16[272,512]{1,0:T(8,128)(2,1)S(1)} %get-tuple-element.60), channel_id=1, source_target_pairs={{0,4},{4,0},{8,12},{12,8},{16,20},{20,16},{24,28},{28,24},{32,36},... | collective-permute-start | bytes 835592 | tf_op jit(solution)/shard_map/ppermute | solution.py:77
  131.7 2.7 %collective-permute-start.34 = (f32[64,512]{1,0:T(8,128)S(1)}, f32[64,512]{1,0:T(8,128)S(1)}, u32[]{:S(2)}, u32[]{:S(2)}) collective-permute-start(f32[64,512]{1,0:T(8,128)S(1)} %get-tuple-element.67), channel_id=1, source_target_pairs={{0,24},{4,28},{8,0},{12,4},{16,8},{20,12},{24,16},{28,20},{32,56},... | collective-permute-start | bytes 393224 | tf_op jit(solution)/shard_map/ppermute | solution.py:73
  134.4 2.6 %collective-permute-done.32.refs_24_ = bf16[224,7168]{1,0:T(8,128)(2,1)S(1)} collective-permute-done((bf16[224,7168]{1,0:T(8,128)(2,1)S(1)}, bf16[224,7168]{1,0:T(8,128)(2,1)S(1)}, u32[]{:S(2)}, u32[]{:S(2)}) %collective-permute-start.32) | collective-permute-done | bytes 3211296 | tf_op jit(solution)/shard_map/ppermute | solution.py:77
  137.0 6.3 %shard_map.76 = f32[1,224,7168]{2,1,0:T(8,128)} custom-call(bf16[512,256]{1,0:T(8,128)(2,1)S(1)} %get-tuple-element.44.refs_0_, bf16[512,256]{1,0:T(8,128)(2,1)S(1)} %get-tuple-element.45.refs_1_, bf16[512,256]{1,0:T(8,128)(2,1)S(1)} %get-tuple-element.46.refs_2_, bf16[512,256]{1,0:T(8,128)(2,1)S(1)} %get-tuple-element.47.refs_3_, ...), custom_call_target="tpu_custom_call" | custom-call | flops 3288334336 | bytes 25165824 | tf_op jit(solution)/shard_map/pallas_call | solution.py:273
  (72 shorter events, 24.9 us)
Async XLA Ops:
  4.3 8.3 %collective-permute-start = (bf16[16,7296]{1,0:T(8,128)(2,1)S(1)}, bf16[16,7296]{1,0:T(8,128)(2,1)S(1)}, u32[]{:S(2)}, u32[]{:S(2)}) collective-permute-start(bf16[16,7296]{1,0:T(8,128)(2,1)S(1)} %get-tuple-element.37), channel_id=1, source_target_pairs={{0,1},{1,2},{2,3},{3,0},{4,5},{5,6},{6,7},{7,4},{8,9},{9,10},{10,1... | collective-permute-start | bytes 700424 | tf_op jit(solution)/shard_map/ppermute | solution.py:297
  6.4 12.5 %collective-permute-start.1 = (bf16[16,7296]{1,0:T(8,128)(2,1)S(1)}, bf16[16,7296]{1,0:T(8,128)(2,1)S(1)}, u32[]{:S(2)}, u32[]{:S(2)}) collective-permute-start(bf16[16,7296]{1,0:T(8,128)(2,1)S(1)} %get-tuple-element.38), channel_id=1, source_target_pairs={{0,2},{1,3},{2,0},{3,1},{4,6},{5,7},{6,4},{7,5},{8,10},{9,11},{10,... | collective-permute-start | bytes 700424 | tf_op jit(solution)/shard_map/ppermute | solution.py:297
  8.9 10.1 %collective-permute-start.2 = (bf16[16,7296]{1,0:T(8,128)(2,1)S(1)}, bf16[16,7296]{1,0:T(8,128)(2,1)S(1)}, u32[]{:S(2)}, u32[]{:S(2)}) collective-permute-start(bf16[16,7296]{1,0:T(8,128)(2,1)S(1)} %get-tuple-element.39), channel_id=1, source_target_pairs={{0,3},{1,0},{2,1},{3,2},{4,7},{5,4},{6,5},{7,6},{8,11},{9,8},{10,9... | collective-permute-start | bytes 700424 | tf_op jit(solution)/shard_map/ppermute | solution.py:297
  19.0 15.1 %collective-permute-start.3 = (bf16[64,7296]{1,0:T(8,128)(2,1)S(1)}, bf16[64,7296]{1,0:T(8,128)(2,1)S(1)}, u32[]{:S(2)}, u32[]{:S(2)}) collective-permute-start(bf16[64,7296]{1,0:T(8,128)(2,1)S(1)} %constant_dynamic-update-slice_fusion.refs_0_.refs_4_), channel_id=1, source_target_pairs={{0,32},{4,12},{8,40},{12,20},{16,48},{20,28},{24,56},{28,4},{32,64... | collective-permute-start | bytes 2801672 | tf_op jit(solution)/shard_map/ppermute | solution.py:61
  20.7 19.4 %collective-permute-start.5 = (bf16[64,7296]{1,0:T(8,128)(2,1)S(1)}, bf16[64,7296]{1,0:T(8,128)(2,1)S(1)}, u32[]{:S(2)}, u32[]{:S(2)}) collective-permute-start(bf16[64,7296]{1,0:T(8,128)(2,1)S(1)} %constant_dynamic-update-slice_fusion.refs_0_.refs_4_), channel_id=1, source_target_pairs={{0,96},{4,28},{8,104},{12,4},{16,112},{20,12},{24,120},{28,20},{32... | collective-permute-start | bytes 2801672 | tf_op jit(solution)/shard_map/ppermute | solution.py:61
  22.9 22.6 %collective-permute-start.22 = (bf16[64,7296]{1,0:T(8,128)(2,1)S(1)}, bf16[64,7296]{1,0:T(8,128)(2,1)S(1)}, u32[]{:S(2)}, u32[]{:S(2)}) collective-permute-start(bf16[64,7296]{1,0:T(8,128)(2,1)S(1)} %constant_dynamic-update-slice_fusion.refs_0_.refs_4_), channel_id=1, source_target_pairs={{0,24},{4,100},{8,0},{12,108},{16,8},{20,116},{24,16},{28,124},{32... | collective-permute-start | bytes 2801672 | tf_op jit(solution)/shard_map/ppermute | solution.py:65
  34.1 14.0 %collective-permute-start.4 = (bf16[32,7296]{1,0:T(8,128)(2,1)S(1)}, bf16[32,7296]{1,0:T(8,128)(2,1)S(1)}, u32[]{:S(2)}, u32[]{:S(2)}) collective-permute-start(bf16[32,7296]{1,0:T(8,128)(2,1)S(1)} %slice.40), channel_id=1, source_target_pairs={{0,32},{4,12},{8,40},{12,20},{16,48},{20,28},{24,56},{28,4},{32,64... | collective-permute-start | bytes 1400840 | tf_op jit(solution)/shard_map/ppermute | solution.py:61
  34.2 18.9 %collective-permute-start.21 = (bf16[64,7296]{1,0:T(8,128)(2,1)S(1)}, bf16[64,7296]{1,0:T(8,128)(2,1)S(1)}, u32[]{:S(2)}, u32[]{:S(2)}) collective-permute-start(bf16[64,7296]{1,0:T(8,128)(2,1)S(1)} %constant_dynamic-update-slice_fusion.refs_0_.refs_4_), channel_id=1, source_target_pairs={{0,8},{4,36},{8,16},{12,44},{16,24},{20,52},{24,0},{28,60},{32,40}... | collective-permute-start | bytes 2801672 | tf_op jit(solution)/shard_map/ppermute | solution.py:65
  35.3 16.4 %collective-permute-start.11 = (bf16[64,7168]{1,0:T(8,128)(2,1)S(1)}, bf16[64,7168]{1,0:T(8,128)(2,1)S(1)}, u32[]{:S(2)}, u32[]{:S(2)}) collective-permute-start(bf16[64,7168]{1,0:T(8,128)(2,1)S(1)} %bitcast.4), channel_id=1, source_target_pairs={{0,4},{4,0},{8,12},{12,8},{16,20},{20,16},{24,28},{28,24},{32,36},... | collective-permute-start | bytes 2752520 | tf_op jit(solution)/shard_map/ppermute | solution.py:77
  40.1 11.6 %collective-permute-start.12 = (bf16[64,7168]{1,0:T(8,128)(2,1)S(1)}, bf16[64,7168]{1,0:T(8,128)(2,1)S(1)}, u32[]{:S(2)}, u32[]{:S(2)}) collective-permute-start(bf16[64,7168]{1,0:T(8,128)(2,1)S(1)} %bitcast.9), channel_id=1, source_target_pairs={{0,4},{4,0},{8,12},{12,8},{16,20},{20,16},{24,28},{28,24},{32,36},... | collective-permute-start | bytes 2752520 | tf_op jit(solution)/shard_map/ppermute | solution.py:77
  48.1 23.1 %collective-permute-start.18 = (bf16[64,7296]{1,0:T(8,128)(2,1)S(1)}, bf16[64,7296]{1,0:T(8,128)(2,1)S(1)}, u32[]{:S(2)}, u32[]{:S(2)}) collective-permute-start(bf16[64,7296]{1,0:T(8,128)(2,1)S(1)} %collective-permute-done.3.refs_0_.refs_9_), channel_id=1, source_target_pairs={{0,24},{4,100},{8,0},{12,108},{16,8},{20,116},{24,16},{28,124},{32... | collective-permute-start | bytes 2801672 | tf_op jit(solution)/shard_map/ppermute | solution.py:65
  51.6 17.2 %collective-permute-start.24 = (bf16[32,7296]{1,0:T(8,128)(2,1)S(1)}, bf16[32,7296]{1,0:T(8,128)(2,1)S(1)}, u32[]{:S(2)}, u32[]{:S(2)}) collective-permute-start(bf16[32,7296]{1,0:T(8,128)(2,1)S(1)} %slice.49), channel_id=1, source_target_pairs={{0,24},{4,100},{8,0},{12,108},{16,8},{20,116},{24,16},{28,124},{32... | collective-permute-start | bytes 1400840 | tf_op jit(solution)/shard_map/ppermute | solution.py:65
  51.7 27.1 %collective-permute-start.14 = (bf16[64,7296]{1,0:T(8,128)(2,1)S(1)}, bf16[64,7296]{1,0:T(8,128)(2,1)S(1)}, u32[]{:S(2)}, u32[]{:S(2)}) collective-permute-start(bf16[64,7296]{1,0:T(8,128)(2,1)S(1)} %collective-permute-done.5.refs_0_.refs_14_), channel_id=1, source_target_pairs={{0,24},{4,100},{8,0},{12,108},{16,8},{20,116},{24,16},{28,124},{32... | collective-permute-start | bytes 2801672 | tf_op jit(solution)/shard_map/ppermute | solution.py:65
  53.1 28.4 %collective-permute-start.13 = (bf16[64,7296]{1,0:T(8,128)(2,1)S(1)}, bf16[64,7296]{1,0:T(8,128)(2,1)S(1)}, u32[]{:S(2)}, u32[]{:S(2)}) collective-permute-start(bf16[64,7296]{1,0:T(8,128)(2,1)S(1)} %collective-permute-done.5.refs_0_.refs_14_), channel_id=1, source_target_pairs={{0,8},{4,36},{8,16},{12,44},{16,24},{20,52},{24,0},{28,60},{32,40}... | collective-permute-start | bytes 2801672 | tf_op jit(solution)/shard_map/ppermute | solution.py:65
  53.6 26.6 %collective-permute-start.17 = (bf16[64,7296]{1,0:T(8,128)(2,1)S(1)}, bf16[64,7296]{1,0:T(8,128)(2,1)S(1)}, u32[]{:S(2)}, u32[]{:S(2)}) collective-permute-start(bf16[64,7296]{1,0:T(8,128)(2,1)S(1)} %collective-permute-done.3.refs_0_.refs_9_), channel_id=1, source_target_pairs={{0,8},{4,36},{8,16},{12,44},{16,24},{20,52},{24,0},{28,60},{32,40}... | collective-permute-start | bytes 2801672 | tf_op jit(solution)/shard_map/ppermute | solution.py:65
  68.8 20.0 %collective-permute-start.8 = (bf16[64,7296]{1,0:T(8,128)(2,1)S(1)}, bf16[64,7296]{1,0:T(8,128)(2,1)S(1)}, u32[]{:S(2)}, u32[]{:S(2)}) collective-permute-start(bf16[64,7296]{1,0:T(8,128)(2,1)S(1)} %constant_dynamic-update-slice_fusion.4.refs_0_.refs_19_), channel_id=1, source_target_pairs={{0,24},{4,100},{8,0},{12,108},{16,8},{20,116},{24,16},{28,124},{32... | collective-permute-start | bytes 2801672 | tf_op jit(solution)/shard_map/ppermute | solution.py:65
  71.2 20.0 %collective-permute-start.7 = (bf16[64,7296]{1,0:T(8,128)(2,1)S(1)}, bf16[64,7296]{1,0:T(8,128)(2,1)S(1)}, u32[]{:S(2)}, u32[]{:S(2)}) collective-permute-start(bf16[64,7296]{1,0:T(8,128)(2,1)S(1)} %constant_dynamic-update-slice_fusion.4.refs_0_.refs_19_), channel_id=1, source_target_pairs={{0,8},{4,36},{8,16},{12,44},{16,24},{20,52},{24,0},{28,60},{32,40}... | collective-permute-start | bytes 2801672 | tf_op jit(solution)/shard_map/ppermute | solution.py:65
  78.8 13.2 %collective-permute-start.23 = (bf16[32,7296]{1,0:T(8,128)(2,1)S(1)}, bf16[32,7296]{1,0:T(8,128)(2,1)S(1)}, u32[]{:S(2)}, u32[]{:S(2)}) collective-permute-start(bf16[32,7296]{1,0:T(8,128)(2,1)S(1)} %slice.48), channel_id=1, source_target_pairs={{0,8},{4,36},{8,16},{12,44},{16,24},{20,52},{24,0},{28,60},{32,40}... | collective-permute-start | bytes 1400840 | tf_op jit(solution)/shard_map/ppermute | solution.py:65
  80.1 13.9 %collective-permute-start.20 = (bf16[32,7296]{1,0:T(8,128)(2,1)S(1)}, bf16[32,7296]{1,0:T(8,128)(2,1)S(1)}, u32[]{:S(2)}, u32[]{:S(2)}) collective-permute-start(bf16[32,7296]{1,0:T(8,128)(2,1)S(1)} %slice.47), channel_id=1, source_target_pairs={{0,24},{4,100},{8,0},{12,108},{16,8},{20,116},{24,16},{28,124},{32... | collective-permute-start | bytes 1400840 | tf_op jit(solution)/shard_map/ppermute | solution.py:65
  81.6 15.5 %collective-permute-start.19 = (bf16[32,7296]{1,0:T(8,128)(2,1)S(1)}, bf16[32,7296]{1,0:T(8,128)(2,1)S(1)}, u32[]{:S(2)}, u32[]{:S(2)}) collective-permute-start(bf16[32,7296]{1,0:T(8,128)(2,1)S(1)} %slice.46), channel_id=1, source_target_pairs={{0,8},{4,36},{8,16},{12,44},{16,24},{20,52},{24,0},{28,60},{32,40}... | collective-permute-start | bytes 1400840 | tf_op jit(solution)/shard_map/ppermute | solution.py:65
  88.8 10.0 %collective-permute-start.16 = (bf16[32,7296]{1,0:T(8,128)(2,1)S(1)}, bf16[32,7296]{1,0:T(8,128)(2,1)S(1)}, u32[]{:S(2)}, u32[]{:S(2)}) collective-permute-start(bf16[32,7296]{1,0:T(8,128)(2,1)S(1)} %slice.45), channel_id=1, source_target_pairs={{0,24},{4,100},{8,0},{12,108},{16,8},{20,116},{24,16},{28,124},{32... | collective-permute-start | bytes 1400840 | tf_op jit(solution)/shard_map/ppermute | solution.py:65
  91.2 10.9 %collective-permute-start.15 = (bf16[32,7296]{1,0:T(8,128)(2,1)S(1)}, bf16[32,7296]{1,0:T(8,128)(2,1)S(1)}, u32[]{:S(2)}, u32[]{:S(2)}) collective-permute-start(bf16[32,7296]{1,0:T(8,128)(2,1)S(1)} %slice.44), channel_id=1, source_target_pairs={{0,8},{4,36},{8,16},{12,44},{16,24},{20,52},{24,0},{28,60},{32,40}... | collective-permute-start | bytes 1400840 | tf_op jit(solution)/shard_map/ppermute | solution.py:65
  92.1 11.8 %collective-permute-start.10 = (bf16[32,7296]{1,0:T(8,128)(2,1)S(1)}, bf16[32,7296]{1,0:T(8,128)(2,1)S(1)}, u32[]{:S(2)}, u32[]{:S(2)}) collective-permute-start(bf16[32,7296]{1,0:T(8,128)(2,1)S(1)} %slice.43), channel_id=1, source_target_pairs={{0,24},{4,100},{8,0},{12,108},{16,8},{20,116},{24,16},{28,124},{32... | collective-permute-start | bytes 1400840 | tf_op jit(solution)/shard_map/ppermute | solution.py:65
  94.1 13.0 %collective-permute-start.9 = (bf16[32,7296]{1,0:T(8,128)(2,1)S(1)}, bf16[32,7296]{1,0:T(8,128)(2,1)S(1)}, u32[]{:S(2)}, u32[]{:S(2)}) collective-permute-start(bf16[32,7296]{1,0:T(8,128)(2,1)S(1)} %slice.42), channel_id=1, source_target_pairs={{0,8},{4,36},{8,16},{12,44},{16,24},{20,52},{24,0},{28,60},{32,40}... | collective-permute-start | bytes 1400840 | tf_op jit(solution)/shard_map/ppermute | solution.py:65
  109.1 11.4 %collective-permute-start.29 = (bf16[1024,128]{1,0:T(8,128)(2,1)S(1)}, bf16[1024,128]{1,0:T(8,128)(2,1)S(1)}, u32[]{:S(2)}, u32[]{:S(2)}) collective-permute-start(bf16[1024,128]{1,0:T(8,128)(2,1)S(1)} %get-tuple-element.43.own), channel_id=1, source_target_pairs={{0,96},{4,100},{8,104},{12,108},{16,112},{20,116},{24,120},{28,124... | collective-permute-start | bytes 786440 | tf_op jit(solution)/shard_map/ppermute | solution.py:69
  109.7 12.5 %collective-permute-start.28 = (bf16[1024,128]{1,0:T(8,128)(2,1)S(1)}, bf16[1024,128]{1,0:T(8,128)(2,1)S(1)}, u32[]{:S(2)}, u32[]{:S(2)}) collective-permute-start(bf16[1024,128]{1,0:T(8,128)(2,1)S(1)} %get-tuple-element.43.own), channel_id=1, source_target_pairs={{0,32},{4,36},{8,40},{12,44},{16,48},{20,52},{24,56},{28,60},{32,6... | collective-permute-start | bytes 786440 | tf_op jit(solution)/shard_map/ppermute | solution.py:69
  110.5 11.8 %collective-permute-start.27 = (bf16[1024,128]{1,0:T(8,128)(2,1)S(1)}, bf16[1024,128]{1,0:T(8,128)(2,1)S(1)}, u32[]{:S(2)}, u32[]{:S(2)}) collective-permute-start(bf16[1024,128]{1,0:T(8,128)(2,1)S(1)} %get-tuple-element.43.own), channel_id=1, source_target_pairs={{0,16},{4,20},{8,24},{12,28},{16,0},{20,4},{24,8},{28,12},{32,48},... | collective-permute-start | bytes 786440 | tf_op jit(solution)/shard_map/ppermute | solution.py:73
  113.0 11.1 %collective-permute-start.26 = (bf16[1024,128]{1,0:T(8,128)(2,1)S(1)}, bf16[1024,128]{1,0:T(8,128)(2,1)S(1)}, u32[]{:S(2)}, u32[]{:S(2)}) collective-permute-start(bf16[1024,128]{1,0:T(8,128)(2,1)S(1)} %get-tuple-element.43.own), channel_id=1, source_target_pairs={{0,24},{4,28},{8,0},{12,4},{16,8},{20,12},{24,16},{28,20},{32,56},... | collective-permute-start | bytes 786440 | tf_op jit(solution)/shard_map/ppermute | solution.py:73
  115.2 9.3 %collective-permute-start.25 = (bf16[1024,128]{1,0:T(8,128)(2,1)S(1)}, bf16[1024,128]{1,0:T(8,128)(2,1)S(1)}, u32[]{:S(2)}, u32[]{:S(2)}) collective-permute-start(bf16[1024,128]{1,0:T(8,128)(2,1)S(1)} %get-tuple-element.43.own), channel_id=1, source_target_pairs={{0,8},{4,12},{8,16},{12,20},{16,24},{20,28},{24,0},{28,4},{32,40},... | collective-permute-start | bytes 786440 | tf_op jit(solution)/shard_map/ppermute | solution.py:73
  131.6 11.6 %collective-permute-start.33 = (f32[64,512]{1,0:T(8,128)S(1)}, f32[64,512]{1,0:T(8,128)S(1)}, u32[]{:S(2)}, u32[]{:S(2)}) collective-permute-start(f32[64,512]{1,0:T(8,128)S(1)} %get-tuple-element.66), channel_id=1, source_target_pairs={{0,8},{4,12},{8,16},{12,20},{16,24},{20,28},{24,0},{28,4},{32,40},... | collective-permute-start | bytes 393224 | tf_op jit(solution)/shard_map/ppermute | solution.py:73
  131.7 11.6 %collective-permute-start.34 = (f32[64,512]{1,0:T(8,128)S(1)}, f32[64,512]{1,0:T(8,128)S(1)}, u32[]{:S(2)}, u32[]{:S(2)}) collective-permute-start(f32[64,512]{1,0:T(8,128)S(1)} %get-tuple-element.67), channel_id=1, source_target_pairs={{0,24},{4,28},{8,0},{12,4},{16,8},{20,12},{24,16},{28,20},{32,56},... | collective-permute-start | bytes 393224 | tf_op jit(solution)/shard_map/ppermute | solution.py:73
  134.4 8.9 %collective-permute-start.35 = (f32[64,512]{1,0:T(8,128)S(1)}, f32[64,512]{1,0:T(8,128)S(1)}, u32[]{:S(2)}, u32[]{:S(2)}) collective-permute-start(f32[64,512]{1,0:T(8,128)S(1)} %get-tuple-element.68), channel_id=1, source_target_pairs={{0,16},{4,20},{8,24},{12,28},{16,0},{20,4},{24,8},{28,12},{32,48},... | collective-permute-start | bytes 393224 | tf_op jit(solution)/shard_map/ppermute | solution.py:73
  (7 other events, 102.8 us)

commit v4 on v3

--- a/solution.py
+++ b/solution.py
@@ -133,9 +133,7 @@
     value = gate / (1.0 + jnp.exp(-gate)) * upward
     value = jnp.where(core == 1, pltpu.roll(value, 64, 1), value).astype(BF16)
     seen = jnp.concatenate([p[:, WIDTH:] for p in pieces], 0).astype(F32)
-    for part in range(height // 256):
-        total_seen = jnp.sum(seen[256 * part : 256 * part + 256], axis=0, keepdims=True)
-        count[:, FLAG * part : FLAG * part + FLAG] = jnp.broadcast_to(total_seen, (16, FLAG))
+    count[...] = jnp.broadcast_to(jnp.sum(seen, axis=0, keepdims=True), (16, FLAG))
     if not first:
         hidden[...] = refs[size + 4][...]
     for j, (far, near) in enumerate(spots):
@@ -154,7 +152,7 @@
         out_shape=[
             jax.ShapeDtypeStruct((1024, 128), BF16),
             jax.ShapeDtypeStruct((WINDOW, height), BF16),
-            jax.ShapeDtypeStruct((16, height // 256 * FLAG), F32),
+            jax.ShapeDtypeStruct((16, FLAG), F32),
         ],
         in_specs=[VMEM] * (len(pieces) + 4 + len(before)),
         out_specs=[VMEM] * 3,
@@ -180,7 +178,10 @@
         other = pl.multiple_of(128 * j + 64 - 64 * core, 64)
         keep[64 * j : 64 * j + 64, :] = tile[pl.ds(mine, 64), :]
         send[64 * j : 64 * j + 64, :] = tile[pl.ds(other, 64), :].astype(BF16)
-    counts = jnp.concatenate([n[...] for n in counts], 1)
+    total = sum(n[...] for n in counts)
+    high = jnp.floor(total * (1.0 / 32.0)) * 32.0
+    zero = jnp.zeros_like(total)
+    counts = jnp.concatenate([high, total - high, zero, zero], 1)
     keep[256:, :] = counts
     send[256:, :] = counts.astype(BF16)
 
@@ -243,42 +244,57 @@
     )(*pinned((*blocks, factor)))
 
 
-def gram_kernel(mine, groups, *refs):
-    size = len(refs) - (3 if mine else 1)
-    windows, pieces, rest = refs[:groups], refs[groups:size], refs[size:]
-    core = spot()[2]
-    _, shift = gram_start()
-    first = shift + core * 224 if mine else shift + 224 - core * 224
+def gram_part(windows, pieces, first):
     first = pl.multiple_of(first, 32)
     left = jnp.concatenate([w[pl.ds(first, 224), :] for w in windows], 1)
     here = pl.ds(pl.multiple_of(pl.program_id(0) * CHUNK, CHUNK), CHUNK)
     right = jnp.concatenate([p[:, here] for p in pieces], 0)
-    part = jnp.dot(left, right, preferred_element_type=F32)
-    if mine:
-        got, factor, out = rest
-        out[0, :, :] = (part + got[:, here].astype(F32)) * factor[0:1, 0:1]
-    else:
-        rest[0][...] = part.astype(BF16)
-
-
-def gram_work(windows, pieces, got=None, factor=None):
-    mine = got is not None
-    if mine:
-        out_shape = jax.ShapeDtypeStruct((1, 224, WIDTH), F32)
-        out_spec = pl.BlockSpec((1, 224, CHUNK), lambda n: (0, 0, n))
-    else:
-        out_shape = jax.ShapeDtypeStruct((224, WIDTH), BF16)
-        out_spec = pl.BlockSpec((224, CHUNK), lambda n: (0, n))
-    operands = (*windows, *pieces) + ((got, factor) if mine else ())
-    return pl.pallas_call(
-        functools.partial(gram_kernel, mine, len(windows)),
+    return jnp.dot(left, right, preferred_element_type=F32), here
+
+
+def gram_rows():
+    core = spot()[2]
+    _, shift = gram_start()
+    return shift + core * 224, shift + 224 - core * 224
+
+
+def gram_first_kernel(groups, *refs):
+    windows, pieces, (keep, send) = refs[:groups], refs[groups:-2], refs[-2:]
+    mine, other = gram_rows()
+    keep[...], _ = gram_part(windows, pieces, mine)
+    send[...], _ = gram_part(windows, pieces, other)
+
+
+def gram_send_kernel(groups, *refs):
+    windows, pieces, (held, send) = refs[:groups], refs[groups:-2], refs[-2:]
+    part, here = gram_part(windows, pieces, gram_rows()[1])
+    send[...] = (part + held[:, here]).astype(BF16)
+
+
+def gram_keep_kernel(groups, *refs):
+    windows, pieces, (held, got, factor, out) = refs[:groups], refs[groups:-4], refs[-4:]
+    part, here = gram_part(windows, pieces, gram_rows()[0])
+    out[0, :, :] = (part + held[:, here] + got[:, here].astype(F32)) * factor[0:1, 0:1]
+
+
+def gram_work(kernel, windows, pieces, others, outs):
+    operands = (*windows, *pieces, *others)
+    specs = [
+        pl.BlockSpec((224, CHUNK), lambda n: (0, n))
+        if len(out.shape) == 2
+        else pl.BlockSpec((1, 224, CHUNK), lambda n: (0, 0, n))
+        for out in outs
+    ]
+    depth = sum(p.shape[0] for p in pieces)
+    return pl.pallas_call(
+        functools.partial(kernel, len(windows)),
         grid=(WIDTH // CHUNK,),
-        out_shape=out_shape,
+        out_shape=outs,
         in_specs=[VMEM] * len(operands),
-        out_specs=out_spec,
+        out_specs=specs,
         compiler_params=params(10),
         cost_estimate=pl.CostEstimate(
-            flops=2 * 224 * WIDTH * 1024, bytes_accessed=24 << 20, transcendentals=0
+            flops=2 * 224 * WIDTH * depth, bytes_accessed=16 << 20, transcendentals=0
         ),
     )(*pinned(operands))
 
@@ -296,6 +312,7 @@
     for step in (1, 2, 3):
         parts.append(lax.ppermute(blocks[step], "expert", [(i, (i + step) % 4) for i in range(4)]))
     shard = jnp.concatenate(parts, 0)
+    shard, weights = after(shard, weights)
 
     up, down, up2, down2 = ring(shard, major)
     far = jnp.concatenate([up2, down2], 0)
@@ -303,19 +320,29 @@
     for origin, piece in zip(ORIGIN, (shard, up, down, far)):
         groups.append(((origin,), (piece,) + ring(piece, minor)))
     windows, counts, before = [], [], ()
-    for origins, pieces in groups:
-        spots = [(far, near) for near in ORIGIN for far in origins]
+    first = 0
+    for size in (1, 1, 2):
+        batch = groups[first : first + size]
+        first += size
+        spots = [(far, near) for origins, _ in batch for near in ORIGIN for far in origins]
+        pieces = [piece for _, group in batch for piece in group]
         hidden, window, count = hidden_work(spots, pieces, weights, before)
         before = (hidden,)
         windows.append(window)
         counts.append(count)
+        if len(windows) == 2:
+            early = [piece for _, group in groups[:first] for piece in group]
+            rows = jax.ShapeDtypeStruct((224, WIDTH), F32)
+            keep, send = gram_work(gram_first_kernel, windows, early, (), [rows, rows])
+            before, _ = after(before, (keep, send))
 
     z_down, y_down = along_z(hidden, -1), along_y(hidden, -1)
     y_up, z_far, y_far = along_y(hidden, 1), along_z(hidden, 2), along_y(hidden, 2)
     z_up = along_z(hidden, 1)
     hops = (z_up, z_down, z_far, y_up, y_down, y_far)
-    pieces = [piece for _, group in groups for piece in group]
-    send = gram_work(windows, pieces)
+    late = [piece for _, group in groups[2:] for piece in group]
+    rows = jax.ShapeDtypeStruct((224, WIDTH), BF16)
+    (send,) = gram_work(gram_send_kernel, windows[2:], late, (send,), [rows])
     hops, send = after(hops, send)
     down_keep, down_send = down_work(hidden, hops[:3], hops[3:], counts)
     down_got = sibling(down_send)
@@ -328,7 +355,8 @@
         along_z(sums[1], -1),
         along_z(sums[3], 2),
     ]
-    gram = gram_work(windows, pieces, got, factor)
+    rows = jax.ShapeDtypeStruct((1, 224, WIDTH), F32)
+    (gram,) = gram_work(gram_keep_kernel, windows[2:], late, (keep, got, factor), [rows])
     factor, gram = after(factor, gram)
     return gram, place(down_blocks, factor)
 

time: 144 us -> 141 us (0.979)
  starting transfers between devices: 55.3 us -> 50.2 us
  Pallas kernels: 19.3 us -> 21.9 us
    ppermute x4, starting transfers between devices: 12.9 us -> 6.37 us  [sibling(): return lax.ppermute(value, 'dp', [(i, i ^ 1) for i in range(2 * CHIPS)])]
    ppermute x16, starting transfers between devices: 21.6 us -> 16 us  [minor(): return lax.ppermute(value, 'dp', steps((0, step), (step, 0)))]
    ppermute x4, waiting for transfers between devices: 11.1 us -> 16.6 us  [major(): return lax.ppermute(value, 'dp', steps((step, 0), (0, step)))]
    ppermute x3, starting transfers between devices: 2.18 us -> 6.08 us  [along_y(): return lax.ppermute(value, 'dp', steps((step, 0), (step, 0)))]
    ppermute x6, starting transfers between devices: 6.42 us -> 9.5 us  [along_z(): return lax.ppermute(value, 'dp', steps((0, step), (0, step)))]
    pallas_call x2 -> x3, Pallas kernels: 11.1 us -> 13.9 us  [gram_work(): pl.pallas_call(functools.partial(kernel, len(windows)), grid=(WIDTH // CH...]
    ppermute x4, waiting for transfers between devices: 3.77 us -> 1.25 us  [sibling(): return lax.ppermute(value, 'dp', [(i, i ^ 1) for i in range(2 * CHIPS)])]
    ppermute x6, waiting for transfers between devices: 2.31 us -> 0.02 us  [along_z(): return lax.ppermute(value, 'dp', steps((0, step), (0, step)))]
  transfers between devices with their start and end apart: 36 -> 36, of which waited for: 21 -> 14; matrix products, arithmetic and copies ran while one was open for 0% -> 0% of each run, Pallas kernels for 10% -> 12%
where the time goes in v4:
time: 141 us
  waiting for transfers between devices  65.1 us (46%)
  starting transfers between devices  50.2 us (36%)
  Pallas kernels  21.9 us (16%)
  local copies, waits for them, and re-layouts  2.56 us (2%)
    ppermute x16, waiting for transfers between devices, minor(): return lax.ppermute(value, 'dp', steps((0, step), (step, 0)))  36.5 us
    ppermute x4, waiting for transfers between devices, major(): return lax.ppermute(value, 'dp', steps((step, 0), (0, step)))  16.6 us
    ppermute x16, starting transfers between devices, minor(): return lax.ppermute(value, 'dp', steps((0, step), (step, 0)))  16 us
    pallas_call x3, Pallas kernels, gram_work(): pl.pallas_call(functools.partial(kernel, len(windows)), grid=(WIDTH // CH...  13.9 us
    ppermute x6, starting transfers between devices, along_z(): return lax.ppermute(value, 'dp', steps((0, step), (0, step)))  9.5 us
    ppermute x3, waiting for transfers between devices, local(): lax.ppermute(blocks[step], 'expert', [(i, (i + step) % 4) for i in range(...  7.34 us
    ppermute x4, starting transfers between devices, major(): return lax.ppermute(value, 'dp', steps((step, 0), (0, step)))  6.57 us
    ppermute x4, starting transfers between devices, sibling(): return lax.ppermute(value, 'dp', [(i, i ^ 1) for i in range(2 * CHIPS)])  6.37 us
  transfers between devices with their start and end apart: 36, of which 14 were waited for; matrix products, arithmetic and copies ran while one was open for 0% of the time, Pallas kernels for 12%

profile of v4, /device:TPU:1, one launch (start us, length us, event | category | flops | bytes accessed | tf_op | source)
XLA Modules:
  0.0 140.8 jit_solution(2862187258487611916)
XLA Ops:
  0.7 2.2 %copy-done.2 = bf16[256,7168]{1,0:T(8,128)(2,1)S(1)} copy-done((bf16[256,7168]{1,0:T(8,128)(2,1)S(1)}, bf16[256,7168]{1,0:T(8,128)(2,1)}, u32[]{:S(2)}) %copy-start.2) | copy-done | bytes 3670040
  2.8 1.5 %shard_map.68 = (bf16[16,7296]{1,0:T(8,128)(2,1)S(1)}, bf16[16,7296]{1,0:T(8,128)(2,1)S(1)}, bf16[16,7296]{1,0:T(8,128)(2,1)S(1)}, bf16[16,7296]{1,0:T(8,128)(2,1)S(1)}) custom-call(s32[8,256]{1,0:T(8,128)} %bitcast.12, s32[8,256]{1,0:T(8,128)} %bitcast.13, bf16[256,7168]{1,0:T(8,128)(2,1)S(1)} %copy-done.2), custom_call_target="tpu_custom_call" | custom-call | tf_op jit(solution)/shard_map/pallas_call | solution.py:109
  4.3 2.1 %collective-permute-start = (bf16[16,7296]{1,0:T(8,128)(2,1)S(1)}, bf16[16,7296]{1,0:T(8,128)(2,1)S(1)}, u32[]{:S(2)}, u32[]{:S(2)}) collective-permute-start(bf16[16,7296]{1,0:T(8,128)(2,1)S(1)} %get-tuple-element.42), channel_id=1, source_target_pairs={{0,1},{1,2},{2,3},{3,0},{4,5},{5,6},{6,7},{7,4},{8,9},{9,10},{10,1... | collective-permute-start | bytes 700424 | tf_op jit(solution)/shard_map/ppermute | solution.py:313
  6.4 2.5 %collective-permute-start.1 = (bf16[16,7296]{1,0:T(8,128)(2,1)S(1)}, bf16[16,7296]{1,0:T(8,128)(2,1)S(1)}, u32[]{:S(2)}, u32[]{:S(2)}) collective-permute-start(bf16[16,7296]{1,0:T(8,128)(2,1)S(1)} %get-tuple-element.43), channel_id=1, source_target_pairs={{0,2},{1,3},{2,0},{3,1},{4,6},{5,7},{6,4},{7,5},{8,10},{9,11},{10,... | collective-permute-start | bytes 700424 | tf_op jit(solution)/shard_map/ppermute | solution.py:313
  10.0 1.5 %collective-permute-start.3 = (bf16[64,7168]{1,0:T(8,128)(2,1)S(1)}, bf16[64,7168]{1,0:T(8,128)(2,1)S(1)}, u32[]{:S(2)}, u32[]{:S(2)}) collective-permute-start(bf16[64,7168]{1,0:T(8,128)(2,1)S(1)} %bitcast.4), channel_id=1, source_target_pairs={{0,4},{4,0},{8,12},{12,8},{16,20},{20,16},{24,28},{28,24},{32,36},... | collective-permute-start | bytes 2752520 | tf_op jit(solution)/shard_map/ppermute | solution.py:77
  12.6 6.3 %collective-permute-done.1 = bf16[16,7296]{1,0:T(8,128)(2,1)S(1)} collective-permute-done((bf16[16,7296]{1,0:T(8,128)(2,1)S(1)}, bf16[16,7296]{1,0:T(8,128)(2,1)S(1)}, u32[]{:S(2)}, u32[]{:S(2)}) %collective-permute-start.1) | collective-permute-done | bytes 233504 | tf_op jit(solution)/shard_map/ppermute | solution.py:313
  19.0 1.7 %collective-permute-start.10 = (bf16[64,7296]{1,0:T(8,128)(2,1)S(1)}, bf16[64,7296]{1,0:T(8,128)(2,1)S(1)}, u32[]{:S(2)}, u32[]{:S(2)}) collective-permute-start(bf16[64,7296]{1,0:T(8,128)(2,1)S(1)} %pad_maximum_fusion.refs_0_.refs_2_), channel_id=1, source_target_pairs={{0,32},{4,12},{8,40},{12,20},{16,48},{20,28},{24,56},{28,4},{32,64... | collective-permute-start | bytes 2801672 | tf_op jit(solution)/shard_map/ppermute | solution.py:61
  20.8 2.2 %collective-permute-start.5 = (bf16[64,7296]{1,0:T(8,128)(2,1)S(1)}, bf16[64,7296]{1,0:T(8,128)(2,1)S(1)}, u32[]{:S(2)}, u32[]{:S(2)}) collective-permute-start(bf16[64,7296]{1,0:T(8,128)(2,1)S(1)} %pad_maximum_fusion.refs_0_.refs_2_), channel_id=1, source_target_pairs={{0,96},{4,28},{8,104},{12,4},{16,112},{20,12},{24,120},{28,20},{32... | collective-permute-start | bytes 2801672 | tf_op jit(solution)/shard_map/ppermute | solution.py:61
  23.0 11.2 %collective-permute-done.10.refs_0_.refs_7_ = bf16[64,7296]{1,0:T(8,128)(2,1)S(1)} collective-permute-done((bf16[64,7296]{1,0:T(8,128)(2,1)S(1)}, bf16[64,7296]{1,0:T(8,128)(2,1)S(1)}, u32[]{:S(2)}, u32[]{:S(2)}) %collective-permute-start.10) | collective-permute-done | bytes 933920 | tf_op jit(solution)/shard_map/ppermute | solution.py:61
  35.3 1.8 %collective-permute-start.22 = (bf16[64,7296]{1,0:T(8,128)(2,1)S(1)}, bf16[64,7296]{1,0:T(8,128)(2,1)S(1)}, u32[]{:S(2)}, u32[]{:S(2)}) collective-permute-start(bf16[64,7296]{1,0:T(8,128)(2,1)S(1)} %pad_maximum_fusion.refs_0_.refs_2_), channel_id=1, source_target_pairs={{0,24},{4,100},{8,0},{12,108},{16,8},{20,116},{24,16},{28,124},{32... | collective-permute-start | bytes 2801672 | tf_op jit(solution)/shard_map/ppermute | solution.py:65
  37.2 2.6 %collective-permute-start.12 = (bf16[32,7296]{1,0:T(8,128)(2,1)S(1)}, bf16[32,7296]{1,0:T(8,128)(2,1)S(1)}, u32[]{:S(2)}, u32[]{:S(2)}) collective-permute-start(bf16[32,7296]{1,0:T(8,128)(2,1)S(1)} %slice.43), channel_id=1, source_target_pairs={{0,96},{4,28},{8,104},{12,4},{16,112},{20,12},{24,120},{28,20},{32... | collective-permute-start | bytes 1400840 | tf_op jit(solution)/shard_map/ppermute | solution.py:61
  39.8 5.4 %collective-permute-done.11 = bf16[32,7296]{1,0:T(8,128)(2,1)S(1)} collective-permute-done((bf16[32,7296]{1,0:T(8,128)(2,1)S(1)}, bf16[32,7296]{1,0:T(8,128)(2,1)S(1)}, u32[]{:S(2)}, u32[]{:S(2)}) %collective-permute-start.11) | collective-permute-done | bytes 466976 | tf_op jit(solution)/shard_map/ppermute | solution.py:61
  45.1 2.9 %collective-permute-start.18 = (bf16[64,7296]{1,0:T(8,128)(2,1)S(1)}, bf16[64,7296]{1,0:T(8,128)(2,1)S(1)}, u32[]{:S(2)}, u32[]{:S(2)}) collective-permute-start(bf16[64,7296]{1,0:T(8,128)(2,1)S(1)} %collective-permute-done.10.refs_0_.refs_7_), channel_id=1, source_target_pairs={{0,24},{4,100},{8,0},{12,108},{16,8},{20,116},{24,16},{28,124},{32... | collective-permute-start | bytes 2801672 | tf_op jit(solution)/shard_map/ppermute | solution.py:65
  48.1 5.2 %collective-permute-done.21.refs_1_.refs_3_ = bf16[64,7296]{1,0:T(8,128)(2,1)S(1)} collective-permute-done((bf16[64,7296]{1,0:T(8,128)(2,1)S(1)}, bf16[64,7296]{1,0:T(8,128)(2,1)S(1)}, u32[]{:S(2)}, u32[]{:S(2)}) %collective-permute-start.21) | collective-permute-done | bytes 933920 | tf_op jit(solution)/shard_map/ppermute | solution.py:65
  53.3 2.7 %collective-permute-start.7 = (bf16[64,7296]{1,0:T(8,128)(2,1)S(1)}, bf16[64,7296]{1,0:T(8,128)(2,1)S(1)}, u32[]{:S(2)}, u32[]{:S(2)}) collective-permute-start(bf16[64,7296]{1,0:T(8,128)(2,1)S(1)} %collective-permute-done.5.refs_0_.refs_1_), channel_id=1, source_target_pairs={{0,24},{4,100},{8,0},{12,108},{16,8},{20,116},{24,16},{28,124},{32... | collective-permute-start | bytes 2801672 | tf_op jit(solution)/shard_map/ppermute | solution.py:65
  56.1 7.2 %collective-permute-done.17.refs_1_.refs_8_ = bf16[64,7296]{1,0:T(8,128)(2,1)S(1)} collective-permute-done((bf16[64,7296]{1,0:T(8,128)(2,1)S(1)}, bf16[64,7296]{1,0:T(8,128)(2,1)S(1)}, u32[]{:S(2)}, u32[]{:S(2)}) %collective-permute-start.17) | collective-permute-done | bytes 933920 | tf_op jit(solution)/shard_map/ppermute | solution.py:65
  63.3 1.5 %collective-permute-start.14 = (bf16[64,7296]{1,0:T(8,128)(2,1)S(1)}, bf16[64,7296]{1,0:T(8,128)(2,1)S(1)}, u32[]{:S(2)}, u32[]{:S(2)}) collective-permute-start(bf16[64,7296]{1,0:T(8,128)(2,1)S(1)} %constant_dynamic-update-slice_fusion.refs_5_.refs_6_), channel_id=1, source_target_pairs={{0,24},{4,100},{8,0},{12,108},{16,8},{20,116},{24,16},{28,124},{32... | collective-permute-start | bytes 2801672 | tf_op jit(solution)/shard_map/ppermute | solution.py:65
  65.0 8.3 %collective-permute-done.6.refs_1_.refs_2_ = bf16[64,7296]{1,0:T(8,128)(2,1)S(1)} collective-permute-done((bf16[64,7296]{1,0:T(8,128)(2,1)S(1)}, bf16[64,7296]{1,0:T(8,128)(2,1)S(1)}, u32[]{:S(2)}, u32[]{:S(2)}) %collective-permute-start.6) | collective-permute-done | bytes 933920 | tf_op jit(solution)/shard_map/ppermute | solution.py:65
  74.8 8.5 %collective-permute-done.13.refs_6_.refs_7_ = bf16[64,7296]{1,0:T(8,128)(2,1)S(1)} collective-permute-done((bf16[64,7296]{1,0:T(8,128)(2,1)S(1)}, bf16[64,7296]{1,0:T(8,128)(2,1)S(1)}, u32[]{:S(2)}, u32[]{:S(2)}) %collective-permute-start.13) | collective-permute-done | bytes 933920 | tf_op jit(solution)/shard_map/ppermute | solution.py:65
  85.0 3.3 %collective-permute-done.23.refs_3_.refs_5_ = bf16[32,7296]{1,0:T(8,128)(2,1)S(1)} collective-permute-done((bf16[32,7296]{1,0:T(8,128)(2,1)S(1)}, bf16[32,7296]{1,0:T(8,128)(2,1)S(1)}, u32[]{:S(2)}, u32[]{:S(2)}) %collective-permute-start.23) | collective-permute-done | bytes 466976 | tf_op jit(solution)/shard_map/ppermute | solution.py:65
  89.8 3.5 %collective-permute-done.19.refs_3_.refs_10_ = bf16[32,7296]{1,0:T(8,128)(2,1)S(1)} collective-permute-done((bf16[32,7296]{1,0:T(8,128)(2,1)S(1)}, bf16[32,7296]{1,0:T(8,128)(2,1)S(1)}, u32[]{:S(2)}, u32[]{:S(2)}) %collective-permute-start.19) | collective-permute-done | bytes 466976 | tf_op jit(solution)/shard_map/ppermute | solution.py:65
  93.3 1.5 %collective-permute-start.16 = (bf16[32,7296]{1,0:T(8,128)(2,1)S(1)}, bf16[32,7296]{1,0:T(8,128)(2,1)S(1)}, u32[]{:S(2)}, u32[]{:S(2)}) collective-permute-start(bf16[32,7296]{1,0:T(8,128)(2,1)S(1)} %slice.45), channel_id=1, source_target_pairs={{0,24},{4,100},{8,0},{12,108},{16,8},{20,116},{24,16},{28,124},{32... | collective-permute-start | bytes 1400840 | tf_op jit(solution)/shard_map/ppermute | solution.py:65
  97.4 5.5 %shard_map.71 = (f32[224,7168]{1,0:T(8,128)S(1)}, f32[224,7168]{1,0:T(8,128)S(1)}) custom-call(bf16[512,256]{1,0:T(8,128)(2,1)S(1)} %get-tuple-element.52.refs_0_, bf16[512,256]{1,0:T(8,128)(2,1)S(1)} %get-tuple-element.53.refs_1_, bf16[64,7296]{1,0:T(8,128)(2,1)S(1)} %pad_maximum_fusion.refs_0_.refs_2_, ...), custom_call_target="tpu_custom_call" | custom-call | flops 1644167168 | bytes 16777216 | tf_op jit(solution)/shard_map/pallas_call | solution.py:289
  103.2 2.2 %shard_map.72 = (bf16[1024,128]{1,0:T(8,128)(2,1)S(1)}, bf16[512,512]{1,0:T(8,128)(2,1)S(1)}, f32[16,128]{1,0:T(8,128)S(1)}) custom-call(bf16[64,7296]{1,0:T(8,128)(2,1)S(1)} %collective-permute-done.5.refs_0_.refs_1_, bf16[64,7296]{1,0:T(8,128)(2,1)S(1)} %collective-permute-done.6.refs_1_.refs_2_, ...), custom_call_target="tpu_custom_call" | custom-call | flops 1879048192 | bytes 8388608 | tf_op jit(solution)/shard_map/pallas_call | solution.py:150
  106.5 1.8 %collective-permute-start.26 = (bf16[1024,128]{1,0:T(8,128)(2,1)S(1)}, bf16[1024,128]{1,0:T(8,128)(2,1)S(1)}, u32[]{:S(2)}, u32[]{:S(2)}) collective-permute-start(bf16[1024,128]{1,0:T(8,128)(2,1)S(1)} %get-tuple-element.57.own), channel_id=1, source_target_pairs={{0,24},{4,28},{8,0},{12,4},{16,8},{20,12},{24,16},{28,20},{32,56},... | collective-permute-start | bytes 786440 | tf_op jit(solution)/shard_map/ppermute | solution.py:73
  112.3 3.4 %collective-permute-start.30 = (bf16[1024,128]{1,0:T(8,128)(2,1)S(1)}, bf16[1024,128]{1,0:T(8,128)(2,1)S(1)}, u32[]{:S(2)}, u32[]{:S(2)}) collective-permute-start(bf16[1024,128]{1,0:T(8,128)(2,1)S(1)} %get-tuple-element.57.own), channel_id=1, source_target_pairs={{0,64},{4,68},{8,72},{12,76},{16,80},{20,84},{24,88},{28,92},{32,9... | collective-permute-start | bytes 786440 | tf_op jit(solution)/shard_map/ppermute | solution.py:69
  115.7 3.1 %shard_map.73 = bf16[224,7168]{1,0:T(8,128)(2,1)S(1)} custom-call(bf16[512,512]{1,0:T(8,128)(2,1)S(1)} %get-tuple-element.58.refs_0_, bf16[64,7296]{1,0:T(8,128)(2,1)S(1)} %collective-permute-done.5.refs_0_.refs_1_, bf16[64,7296]{1,0:T(8,128)(2,1)S(1)} %collective-permute-done.6.refs_1_.refs_2_, bf16[64,7296]{1,0:T(8,128)(2,1)S(1)} %collective-permute-done.7.refs_2_.refs_3_, ...), custom_call_target="tpu_custom_call" | custom-call | flops 1644167168 | bytes 16777216 | tf_op jit(solution)/shard_map/pallas_call | solution.py:289
  118.9 3.5 %collective-permute-done.30.y2 = bf16[1024,128]{1,0:T(8,128)(2,1)S(1)} collective-permute-done((bf16[1024,128]{1,0:T(8,128)(2,1)S(1)}, bf16[1024,128]{1,0:T(8,128)(2,1)S(1)}, u32[]{:S(2)}, u32[]{:S(2)}) %collective-permute-start.30) | collective-permute-done | bytes 262176 | tf_op jit(solution)/shard_map/ppermute | solution.py:69
  123.2 4.4 %collective-permute-start.31 = (bf16[272,512]{1,0:T(8,128)(2,1)S(1)}, bf16[272,512]{1,0:T(8,128)(2,1)S(1)}, u32[]{:S(2)}, u32[]{:S(2)}) collective-permute-start(bf16[272,512]{1,0:T(8,128)(2,1)S(1)} %get-tuple-element.70), channel_id=1, source_target_pairs={{0,4},{4,0},{8,12},{12,8},{16,20},{20,16},{24,28},{28,24},{32,36},... | collective-permute-start | bytes 835592 | tf_op jit(solution)/shard_map/ppermute | solution.py:77
  129.6 2.4 %collective-permute-start.34 = (f32[64,512]{1,0:T(8,128)S(1)}, f32[64,512]{1,0:T(8,128)S(1)}, u32[]{:S(2)}, u32[]{:S(2)}) collective-permute-start(f32[64,512]{1,0:T(8,128)S(1)} %get-tuple-element.77), channel_id=1, source_target_pairs={{0,24},{4,28},{8,0},{12,4},{16,8},{20,12},{24,16},{28,20},{32,56},... | collective-permute-start | bytes 393224 | tf_op jit(solution)/shard_map/ppermute | solution.py:73
  132.0 2.5 %collective-permute-start.35 = (f32[64,512]{1,0:T(8,128)S(1)}, f32[64,512]{1,0:T(8,128)S(1)}, u32[]{:S(2)}, u32[]{:S(2)}) collective-permute-start(f32[64,512]{1,0:T(8,128)S(1)} %get-tuple-element.78), channel_id=1, source_target_pairs={{0,16},{4,20},{8,24},{12,28},{16,0},{20,4},{24,8},{28,12},{32,48},... | collective-permute-start | bytes 393224 | tf_op jit(solution)/shard_map/ppermute | solution.py:73
  134.6 5.3 %shard_map.76 = f32[1,224,7168]{2,1,0:T(8,128)} custom-call(bf16[512,512]{1,0:T(8,128)(2,1)S(1)} %get-tuple-element.58.refs_0_, bf16[64,7296]{1,0:T(8,128)(2,1)S(1)} %collective-permute-done.5.refs_0_.refs_1_, bf16[64,7296]{1,0:T(8,128)(2,1)S(1)} %collective-permute-done.6.refs_1_.refs_2_, bf16[64,7296]{1,0:T(8,128)(2,1)S(1)} %collective-permute-done.7.refs_2_.refs_3_, ...), custom_call_target="tpu_custom_call" | custom-call | flops 1644167168 | bytes 16777216 | tf_op jit(solution)/shard_map/pallas_call | solution.py:289
  (69 shorter events, 20.4 us)
Async XLA Ops:
  4.3 8.3 %collective-permute-start = (bf16[16,7296]{1,0:T(8,128)(2,1)S(1)}, bf16[16,7296]{1,0:T(8,128)(2,1)S(1)}, u32[]{:S(2)}, u32[]{:S(2)}) collective-permute-start(bf16[16,7296]{1,0:T(8,128)(2,1)S(1)} %get-tuple-element.42), channel_id=1, source_target_pairs={{0,1},{1,2},{2,3},{3,0},{4,5},{5,6},{6,7},{7,4},{8,9},{9,10},{10,1... | collective-permute-start | bytes 700424 | tf_op jit(solution)/shard_map/ppermute | solution.py:313
  6.4 12.5 %collective-permute-start.1 = (bf16[16,7296]{1,0:T(8,128)(2,1)S(1)}, bf16[16,7296]{1,0:T(8,128)(2,1)S(1)}, u32[]{:S(2)}, u32[]{:S(2)}) collective-permute-start(bf16[16,7296]{1,0:T(8,128)(2,1)S(1)} %get-tuple-element.43), channel_id=1, source_target_pairs={{0,2},{1,3},{2,0},{3,1},{4,6},{5,7},{6,4},{7,5},{8,10},{9,11},{10,... | collective-permute-start | bytes 700424 | tf_op jit(solution)/shard_map/ppermute | solution.py:313
  8.9 10.1 %collective-permute-start.2 = (bf16[16,7296]{1,0:T(8,128)(2,1)S(1)}, bf16[16,7296]{1,0:T(8,128)(2,1)S(1)}, u32[]{:S(2)}, u32[]{:S(2)}) collective-permute-start(bf16[16,7296]{1,0:T(8,128)(2,1)S(1)} %get-tuple-element.44), channel_id=1, source_target_pairs={{0,3},{1,0},{2,1},{3,2},{4,7},{5,4},{6,5},{7,6},{8,11},{9,8},{10,9... | collective-permute-start | bytes 700424 | tf_op jit(solution)/shard_map/ppermute | solution.py:313
  10.0 9.0 %collective-permute-start.3 = (bf16[64,7168]{1,0:T(8,128)(2,1)S(1)}, bf16[64,7168]{1,0:T(8,128)(2,1)S(1)}, u32[]{:S(2)}, u32[]{:S(2)}) collective-permute-start(bf16[64,7168]{1,0:T(8,128)(2,1)S(1)} %bitcast.4), channel_id=1, source_target_pairs={{0,4},{4,0},{8,12},{12,8},{16,20},{20,16},{24,28},{28,24},{32,36},... | collective-permute-start | bytes 2752520 | tf_op jit(solution)/shard_map/ppermute | solution.py:77
  19.0 15.1 %collective-permute-start.10 = (bf16[64,7296]{1,0:T(8,128)(2,1)S(1)}, bf16[64,7296]{1,0:T(8,128)(2,1)S(1)}, u32[]{:S(2)}, u32[]{:S(2)}) collective-permute-start(bf16[64,7296]{1,0:T(8,128)(2,1)S(1)} %pad_maximum_fusion.refs_0_.refs_2_), channel_id=1, source_target_pairs={{0,32},{4,12},{8,40},{12,20},{16,48},{20,28},{24,56},{28,4},{32,64... | collective-permute-start | bytes 2801672 | tf_op jit(solution)/shard_map/ppermute | solution.py:61
  20.8 16.4 %collective-permute-start.5 = (bf16[64,7296]{1,0:T(8,128)(2,1)S(1)}, bf16[64,7296]{1,0:T(8,128)(2,1)S(1)}, u32[]{:S(2)}, u32[]{:S(2)}) collective-permute-start(bf16[64,7296]{1,0:T(8,128)(2,1)S(1)} %pad_maximum_fusion.refs_0_.refs_2_), channel_id=1, source_target_pairs={{0,96},{4,28},{8,104},{12,4},{16,112},{20,12},{24,120},{28,20},{32... | collective-permute-start | bytes 2801672 | tf_op jit(solution)/shard_map/ppermute | solution.py:61
  34.2 11.0 %collective-permute-start.11 = (bf16[32,7296]{1,0:T(8,128)(2,1)S(1)}, bf16[32,7296]{1,0:T(8,128)(2,1)S(1)}, u32[]{:S(2)}, u32[]{:S(2)}) collective-permute-start(bf16[32,7296]{1,0:T(8,128)(2,1)S(1)} %slice.42), channel_id=1, source_target_pairs={{0,32},{4,12},{8,40},{12,20},{16,48},{20,28},{24,56},{28,4},{32,64... | collective-permute-start | bytes 1400840 | tf_op jit(solution)/shard_map/ppermute | solution.py:61
  34.2 19.1 %collective-permute-start.21 = (bf16[64,7296]{1,0:T(8,128)(2,1)S(1)}, bf16[64,7296]{1,0:T(8,128)(2,1)S(1)}, u32[]{:S(2)}, u32[]{:S(2)}) collective-permute-start(bf16[64,7296]{1,0:T(8,128)(2,1)S(1)} %pad_maximum_fusion.refs_0_.refs_2_), channel_id=1, source_target_pairs={{0,8},{4,36},{8,16},{12,44},{16,24},{20,52},{24,0},{28,60},{32,40}... | collective-permute-start | bytes 2801672 | tf_op jit(solution)/shard_map/ppermute | solution.py:65
  35.3 20.7 %collective-permute-start.22 = (bf16[64,7296]{1,0:T(8,128)(2,1)S(1)}, bf16[64,7296]{1,0:T(8,128)(2,1)S(1)}, u32[]{:S(2)}, u32[]{:S(2)}) collective-permute-start(bf16[64,7296]{1,0:T(8,128)(2,1)S(1)} %pad_maximum_fusion.refs_0_.refs_2_), channel_id=1, source_target_pairs={{0,24},{4,100},{8,0},{12,108},{16,8},{20,116},{24,16},{28,124},{32... | collective-permute-start | bytes 2801672 | tf_op jit(solution)/shard_map/ppermute | solution.py:65
  37.2 16.1 %collective-permute-start.12 = (bf16[32,7296]{1,0:T(8,128)(2,1)S(1)}, bf16[32,7296]{1,0:T(8,128)(2,1)S(1)}, u32[]{:S(2)}, u32[]{:S(2)}) collective-permute-start(bf16[32,7296]{1,0:T(8,128)(2,1)S(1)} %slice.43), channel_id=1, source_target_pairs={{0,96},{4,28},{8,104},{12,4},{16,112},{20,12},{24,120},{28,20},{32... | collective-permute-start | bytes 1400840 | tf_op jit(solution)/shard_map/ppermute | solution.py:61
  39.8 23.6 %collective-permute-start.17 = (bf16[64,7296]{1,0:T(8,128)(2,1)S(1)}, bf16[64,7296]{1,0:T(8,128)(2,1)S(1)}, u32[]{:S(2)}, u32[]{:S(2)}) collective-permute-start(bf16[64,7296]{1,0:T(8,128)(2,1)S(1)} %collective-permute-done.10.refs_0_.refs_7_), channel_id=1, source_target_pairs={{0,8},{4,36},{8,16},{12,44},{16,24},{20,52},{24,0},{28,60},{32,40}... | collective-permute-start | bytes 2801672 | tf_op jit(solution)/shard_map/ppermute | solution.py:65
  45.1 19.7 %collective-permute-start.18 = (bf16[64,7296]{1,0:T(8,128)(2,1)S(1)}, bf16[64,7296]{1,0:T(8,128)(2,1)S(1)}, u32[]{:S(2)}, u32[]{:S(2)}) collective-permute-start(bf16[64,7296]{1,0:T(8,128)(2,1)S(1)} %collective-permute-done.10.refs_0_.refs_7_), channel_id=1, source_target_pairs={{0,24},{4,100},{8,0},{12,108},{16,8},{20,116},{24,16},{28,124},{32... | collective-permute-start | bytes 2801672 | tf_op jit(solution)/shard_map/ppermute | solution.py:65
  53.3 20.0 %collective-permute-start.6 = (bf16[64,7296]{1,0:T(8,128)(2,1)S(1)}, bf16[64,7296]{1,0:T(8,128)(2,1)S(1)}, u32[]{:S(2)}, u32[]{:S(2)}) collective-permute-start(bf16[64,7296]{1,0:T(8,128)(2,1)S(1)} %collective-permute-done.5.refs_0_.refs_1_), channel_id=1, source_target_pairs={{0,8},{4,36},{8,16},{12,44},{16,24},{20,52},{24,0},{28,60},{32,40}... | collective-permute-start | bytes 2801672 | tf_op jit(solution)/shard_map/ppermute | solution.py:65
  53.3 21.5 %collective-permute-start.7 = (bf16[64,7296]{1,0:T(8,128)(2,1)S(1)}, bf16[64,7296]{1,0:T(8,128)(2,1)S(1)}, u32[]{:S(2)}, u32[]{:S(2)}) collective-permute-start(bf16[64,7296]{1,0:T(8,128)(2,1)S(1)} %collective-permute-done.5.refs_0_.refs_1_), channel_id=1, source_target_pairs={{0,24},{4,100},{8,0},{12,108},{16,8},{20,116},{24,16},{28,124},{32... | collective-permute-start | bytes 2801672 | tf_op jit(solution)/shard_map/ppermute | solution.py:65
  56.0 27.3 %collective-permute-start.13 = (bf16[64,7296]{1,0:T(8,128)(2,1)S(1)}, bf16[64,7296]{1,0:T(8,128)(2,1)S(1)}, u32[]{:S(2)}, u32[]{:S(2)}) collective-permute-start(bf16[64,7296]{1,0:T(8,128)(2,1)S(1)} %constant_dynamic-update-slice_fusion.refs_5_.refs_6_), channel_id=1, source_target_pairs={{0,8},{4,36},{8,16},{12,44},{16,24},{20,52},{24,0},{28,60},{32,40}... | collective-permute-start | bytes 2801672 | tf_op jit(solution)/shard_map/ppermute | solution.py:65
  63.3 21.6 %collective-permute-start.14 = (bf16[64,7296]{1,0:T(8,128)(2,1)S(1)}, bf16[64,7296]{1,0:T(8,128)(2,1)S(1)}, u32[]{:S(2)}, u32[]{:S(2)}) collective-permute-start(bf16[64,7296]{1,0:T(8,128)(2,1)S(1)} %constant_dynamic-update-slice_fusion.refs_5_.refs_6_), channel_id=1, source_target_pairs={{0,24},{4,100},{8,0},{12,108},{16,8},{20,116},{24,16},{28,124},{32... | collective-permute-start | bytes 2801672 | tf_op jit(solution)/shard_map/ppermute | solution.py:65
  64.9 23.4 %collective-permute-start.23 = (bf16[32,7296]{1,0:T(8,128)(2,1)S(1)}, bf16[32,7296]{1,0:T(8,128)(2,1)S(1)}, u32[]{:S(2)}, u32[]{:S(2)}) collective-permute-start(bf16[32,7296]{1,0:T(8,128)(2,1)S(1)} %slice.48), channel_id=1, source_target_pairs={{0,8},{4,36},{8,16},{12,44},{16,24},{20,52},{24,0},{28,60},{32,40}... | collective-permute-start | bytes 1400840 | tf_op jit(solution)/shard_map/ppermute | solution.py:65
  73.3 16.5 %collective-permute-start.24 = (bf16[32,7296]{1,0:T(8,128)(2,1)S(1)}, bf16[32,7296]{1,0:T(8,128)(2,1)S(1)}, u32[]{:S(2)}, u32[]{:S(2)}) collective-permute-start(bf16[32,7296]{1,0:T(8,128)(2,1)S(1)} %slice.49), channel_id=1, source_target_pairs={{0,24},{4,100},{8,0},{12,108},{16,8},{20,116},{24,16},{28,124},{32... | collective-permute-start | bytes 1400840 | tf_op jit(solution)/shard_map/ppermute | solution.py:65
  74.8 18.5 %collective-permute-start.19 = (bf16[32,7296]{1,0:T(8,128)(2,1)S(1)}, bf16[32,7296]{1,0:T(8,128)(2,1)S(1)}, u32[]{:S(2)}, u32[]{:S(2)}) collective-permute-start(bf16[32,7296]{1,0:T(8,128)(2,1)S(1)} %slice.46), channel_id=1, source_target_pairs={{0,8},{4,36},{8,16},{12,44},{16,24},{20,52},{24,0},{28,60},{32,40}... | collective-permute-start | bytes 1400840 | tf_op jit(solution)/shard_map/ppermute | solution.py:65
  83.3 12.7 %collective-permute-start.20 = (bf16[32,7296]{1,0:T(8,128)(2,1)S(1)}, bf16[32,7296]{1,0:T(8,128)(2,1)S(1)}, u32[]{:S(2)}, u32[]{:S(2)}) collective-permute-start(bf16[32,7296]{1,0:T(8,128)(2,1)S(1)} %slice.47), channel_id=1, source_target_pairs={{0,24},{4,100},{8,0},{12,108},{16,8},{20,116},{24,16},{28,124},{32... | collective-permute-start | bytes 1400840 | tf_op jit(solution)/shard_map/ppermute | solution.py:65
  84.9 17.9 %collective-permute-start.8 = (bf16[32,7296]{1,0:T(8,128)(2,1)S(1)}, bf16[32,7296]{1,0:T(8,128)(2,1)S(1)}, u32[]{:S(2)}, u32[]{:S(2)}) collective-permute-start(bf16[32,7296]{1,0:T(8,128)(2,1)S(1)} %slice.40), channel_id=1, source_target_pairs={{0,8},{4,36},{8,16},{12,44},{16,24},{20,52},{24,0},{28,60},{32,40}... | collective-permute-start | bytes 1400840 | tf_op jit(solution)/shard_map/ppermute | solution.py:65
  88.3 14.5 %collective-permute-start.9 = (bf16[32,7296]{1,0:T(8,128)(2,1)S(1)}, bf16[32,7296]{1,0:T(8,128)(2,1)S(1)}, u32[]{:S(2)}, u32[]{:S(2)}) collective-permute-start(bf16[32,7296]{1,0:T(8,128)(2,1)S(1)} %slice.41), channel_id=1, source_target_pairs={{0,24},{4,100},{8,0},{12,108},{16,8},{20,116},{24,16},{28,124},{32... | collective-permute-start | bytes 1400840 | tf_op jit(solution)/shard_map/ppermute | solution.py:65
  89.8 13.4 %collective-permute-start.15 = (bf16[32,7296]{1,0:T(8,128)(2,1)S(1)}, bf16[32,7296]{1,0:T(8,128)(2,1)S(1)}, u32[]{:S(2)}, u32[]{:S(2)}) collective-permute-start(bf16[32,7296]{1,0:T(8,128)(2,1)S(1)} %slice.44), channel_id=1, source_target_pairs={{0,8},{4,36},{8,16},{12,44},{16,24},{20,52},{24,0},{28,60},{32,40}... | collective-permute-start | bytes 1400840 | tf_op jit(solution)/shard_map/ppermute | solution.py:65
  93.3 9.9 %collective-permute-start.16 = (bf16[32,7296]{1,0:T(8,128)(2,1)S(1)}, bf16[32,7296]{1,0:T(8,128)(2,1)S(1)}, u32[]{:S(2)}, u32[]{:S(2)}) collective-permute-start(bf16[32,7296]{1,0:T(8,128)(2,1)S(1)} %slice.45), channel_id=1, source_target_pairs={{0,24},{4,100},{8,0},{12,108},{16,8},{20,116},{24,16},{28,124},{32... | collective-permute-start | bytes 1400840 | tf_op jit(solution)/shard_map/ppermute | solution.py:65
  106.5 12.3 %collective-permute-start.26 = (bf16[1024,128]{1,0:T(8,128)(2,1)S(1)}, bf16[1024,128]{1,0:T(8,128)(2,1)S(1)}, u32[]{:S(2)}, u32[]{:S(2)}) collective-permute-start(bf16[1024,128]{1,0:T(8,128)(2,1)S(1)} %get-tuple-element.57.own), channel_id=1, source_target_pairs={{0,24},{4,28},{8,0},{12,4},{16,8},{20,12},{24,16},{28,20},{32,56},... | collective-permute-start | bytes 786440 | tf_op jit(solution)/shard_map/ppermute | solution.py:73
  108.3 10.6 %collective-permute-start.27 = (bf16[1024,128]{1,0:T(8,128)(2,1)S(1)}, bf16[1024,128]{1,0:T(8,128)(2,1)S(1)}, u32[]{:S(2)}, u32[]{:S(2)}) collective-permute-start(bf16[1024,128]{1,0:T(8,128)(2,1)S(1)} %get-tuple-element.57.own), channel_id=1, source_target_pairs={{0,16},{4,20},{8,24},{12,28},{16,0},{20,4},{24,8},{28,12},{32,48},... | collective-permute-start | bytes 786440 | tf_op jit(solution)/shard_map/ppermute | solution.py:73
  109.7 9.2 %collective-permute-start.28 = (bf16[1024,128]{1,0:T(8,128)(2,1)S(1)}, bf16[1024,128]{1,0:T(8,128)(2,1)S(1)}, u32[]{:S(2)}, u32[]{:S(2)}) collective-permute-start(bf16[1024,128]{1,0:T(8,128)(2,1)S(1)} %get-tuple-element.57.own), channel_id=1, source_target_pairs={{0,32},{4,36},{8,40},{12,44},{16,48},{20,52},{24,56},{28,60},{32,6... | collective-permute-start | bytes 786440 | tf_op jit(solution)/shard_map/ppermute | solution.py:69
  111.0 7.9 %collective-permute-start.29 = (bf16[1024,128]{1,0:T(8,128)(2,1)S(1)}, bf16[1024,128]{1,0:T(8,128)(2,1)S(1)}, u32[]{:S(2)}, u32[]{:S(2)}) collective-permute-start(bf16[1024,128]{1,0:T(8,128)(2,1)S(1)} %get-tuple-element.57.own), channel_id=1, source_target_pairs={{0,96},{4,100},{8,104},{12,108},{16,112},{20,116},{24,120},{28,124... | collective-permute-start | bytes 786440 | tf_op jit(solution)/shard_map/ppermute | solution.py:69
  112.3 10.0 %collective-permute-start.30 = (bf16[1024,128]{1,0:T(8,128)(2,1)S(1)}, bf16[1024,128]{1,0:T(8,128)(2,1)S(1)}, u32[]{:S(2)}, u32[]{:S(2)}) collective-permute-start(bf16[1024,128]{1,0:T(8,128)(2,1)S(1)} %get-tuple-element.57.own), channel_id=1, source_target_pairs={{0,64},{4,68},{8,72},{12,76},{16,80},{20,84},{24,88},{28,92},{32,9... | collective-permute-start | bytes 786440 | tf_op jit(solution)/shard_map/ppermute | solution.py:69
  129.2 10.6 %collective-permute-start.33 = (f32[64,512]{1,0:T(8,128)S(1)}, f32[64,512]{1,0:T(8,128)S(1)}, u32[]{:S(2)}, u32[]{:S(2)}) collective-permute-start(f32[64,512]{1,0:T(8,128)S(1)} %get-tuple-element.76), channel_id=1, source_target_pairs={{0,8},{4,12},{8,16},{12,20},{16,24},{20,28},{24,0},{28,4},{32,40},... | collective-permute-start | bytes 393224 | tf_op jit(solution)/shard_map/ppermute | solution.py:73
  129.6 10.3 %collective-permute-start.34 = (f32[64,512]{1,0:T(8,128)S(1)}, f32[64,512]{1,0:T(8,128)S(1)}, u32[]{:S(2)}, u32[]{:S(2)}) collective-permute-start(f32[64,512]{1,0:T(8,128)S(1)} %get-tuple-element.77), channel_id=1, source_target_pairs={{0,24},{4,28},{8,0},{12,4},{16,8},{20,12},{24,16},{28,20},{32,56},... | collective-permute-start | bytes 393224 | tf_op jit(solution)/shard_map/ppermute | solution.py:73
  132.0 7.9 %collective-permute-start.35 = (f32[64,512]{1,0:T(8,128)S(1)}, f32[64,512]{1,0:T(8,128)S(1)}, u32[]{:S(2)}, u32[]{:S(2)}) collective-permute-start(f32[64,512]{1,0:T(8,128)S(1)} %get-tuple-element.78), channel_id=1, source_target_pairs={{0,16},{4,20},{8,24},{12,28},{16,0},{20,4},{24,8},{28,12},{32,48},... | collective-permute-start | bytes 393224 | tf_op jit(solution)/shard_map/ppermute | solution.py:73
  (7 other events, 48.2 us)

commit v5 on v4

--- a/solution.py
+++ b/solution.py
@@ -84,35 +84,48 @@
     return (up, down, move(up[:half], 1), move(down[half:], -1))
 
 
-def dispatch_kernel(routes, slots, tokens, *outs):
+def one_hot_kernel(routes, slots, out, flag):
     wanted = jnp.where(routes[...] < 4, routes[...] * CAP + slots[...], -1)
     lane = lax.broadcasted_iota(jnp.int32, (4 * CAP, 1), 0)
     target = ((lane // CAP + lax.axis_index("expert")) % 4) * CAP + lane % CAP
     hit = wanted[0:1, :] == target
     for k in range(1, 8):
         hit = hit | (wanted[k : k + 1, :] == target)
-    one_hot = hit.astype(F32).astype(BF16)
-    flag = jnp.max(hit.astype(F32), axis=1, keepdims=True)
-    flag = jnp.broadcast_to(flag, (4 * CAP, FLAG)).astype(BF16)
+    hit = hit.astype(F32)
+    out[...] = hit.astype(BF16)
+    flag[...] = jnp.broadcast_to(jnp.max(hit, axis=1, keepdims=True), (4 * CAP, FLAG)).astype(BF16)
+
+
+def dispatch_kernel(one_hot, flag, tokens, *outs):
     for start in range(0, WIDTH, 1024):
         rows = jnp.dot(
-            one_hot, tokens[:, start : start + 1024], preferred_element_type=F32
+            one_hot[...], tokens[:, start : start + 1024], preferred_element_type=F32
         ).astype(BF16)
         for j, out in enumerate(outs):
             out[:, start : start + 1024] = rows[j * CAP : (j + 1) * CAP]
     for j, out in enumerate(outs):
-        out[:, WIDTH:] = flag[j * CAP : (j + 1) * CAP]
+        out[:, WIDTH:] = flag[j * CAP : (j + 1) * CAP, :]
 
 
 def dispatch(routes, slots, tokens):
     in_hbm = [pltpu.with_memory_space_constraint(v.T, pltpu.HBM) for v in (routes, slots)]
+    one_hot, flag = pl.pallas_call(
+        one_hot_kernel,
+        out_shape=[
+            jax.ShapeDtypeStruct((4 * CAP, 256), BF16),
+            jax.ShapeDtypeStruct((4 * CAP, FLAG), BF16),
+        ],
+        in_specs=[VMEM] * 2,
+        out_specs=[VMEM] * 2,
+        compiler_params=params(4),
+    )(*in_hbm)
     return pl.pallas_call(
         dispatch_kernel,
         out_shape=[jax.ShapeDtypeStruct((CAP, SENT), BF16)] * 4,
         in_specs=[VMEM] * 3,
         out_specs=[VMEM] * 4,
         compiler_params=params(32),
-    )(*in_hbm, *pinned([tokens]))
+    )(*pinned((one_hot, flag, tokens)))
 
 
 def hidden_kernel(spots, first, *refs):

time: 141 us -> 141 us (level)
  no operation moved by 1% of the time
where the time goes in v5:
time: 141 us
  waiting for transfers between devices  65.1 us (46%)
  starting transfers between devices  50.2 us (36%)
  Pallas kernels  22 us (16%)
  local copies, waits for them, and re-layouts  2.57 us (2%)
    ppermute x16, waiting for transfers between devices, minor(): return lax.ppermute(value, 'dp', steps((0, step), (step, 0)))  36.5 us
    ppermute x4, waiting for transfers between devices, major(): return lax.ppermute(value, 'dp', steps((step, 0), (0, step)))  16.6 us
    ppermute x16, starting transfers between devices, minor(): return lax.ppermute(value, 'dp', steps((0, step), (step, 0)))  16 us
    pallas_call x3, Pallas kernels, gram_work(): pl.pallas_call(functools.partial(kernel, len(windows)), grid=(WIDTH // CH...  13.9 us
    ppermute x6, starting transfers between devices, along_z(): return lax.ppermute(value, 'dp', steps((0, step), (0, step)))  9.51 us
    ppermute x3, waiting for transfers between devices, local(): lax.ppermute(blocks[step], 'expert', [(i, (i + step) % 4) for i in range(...  7.34 us
    ppermute x4, starting transfers between devices, major(): return lax.ppermute(value, 'dp', steps((step, 0), (0, step)))  6.56 us
    ppermute x4, starting transfers between devices, sibling(): return lax.ppermute(value, 'dp', [(i, i ^ 1) for i in range(2 * CHIPS)])  6.38 us
  transfers between devices with their start and end apart: 36, of which 14 were waited for; matrix products, arithmetic and copies ran while one was open for 0% of the time, Pallas kernels for 12%

profile of v5, /device:TPU:1, one launch (start us, length us, event | category | flops | bytes accessed | tf_op | source)
XLA Modules:
  0.0 140.9 jit_solution(13053388005331804518)
XLA Ops:
  1.5 2.2 %copy-done.2 = bf16[256,7168]{1,0:T(8,128)(2,1)S(1)} copy-done((bf16[256,7168]{1,0:T(8,128)(2,1)S(1)}, bf16[256,7168]{1,0:T(8,128)(2,1)}, u32[]{:S(2)}) %copy-start.2) | copy-done | bytes 3670040
  4.4 2.1 %collective-permute-start = (bf16[16,7296]{1,0:T(8,128)(2,1)S(1)}, bf16[16,7296]{1,0:T(8,128)(2,1)S(1)}, u32[]{:S(2)}, u32[]{:S(2)}) collective-permute-start(bf16[16,7296]{1,0:T(8,128)(2,1)S(1)} %get-tuple-element.46), channel_id=1, source_target_pairs={{0,1},{1,2},{2,3},{3,0},{4,5},{5,6},{6,7},{7,4},{8,9},{9,10},{10,1... | collective-permute-start | bytes 700424 | tf_op jit(solution)/shard_map/ppermute | solution.py:326
  6.5 2.4 %collective-permute-start.1 = (bf16[16,7296]{1,0:T(8,128)(2,1)S(1)}, bf16[16,7296]{1,0:T(8,128)(2,1)S(1)}, u32[]{:S(2)}, u32[]{:S(2)}) collective-permute-start(bf16[16,7296]{1,0:T(8,128)(2,1)S(1)} %get-tuple-element.47), channel_id=1, source_target_pairs={{0,2},{1,3},{2,0},{3,1},{4,6},{5,7},{6,4},{7,5},{8,10},{9,11},{10,... | collective-permute-start | bytes 700424 | tf_op jit(solution)/shard_map/ppermute | solution.py:326
  10.2 1.5 %collective-permute-start.3 = (bf16[64,7168]{1,0:T(8,128)(2,1)S(1)}, bf16[64,7168]{1,0:T(8,128)(2,1)S(1)}, u32[]{:S(2)}, u32[]{:S(2)}) collective-permute-start(bf16[64,7168]{1,0:T(8,128)(2,1)S(1)} %bitcast.4), channel_id=1, source_target_pairs={{0,4},{4,0},{8,12},{12,8},{16,20},{20,16},{24,28},{28,24},{32,36},... | collective-permute-start | bytes 2752520 | tf_op jit(solution)/shard_map/ppermute | solution.py:77
  12.8 6.3 %collective-permute-done.1 = bf16[16,7296]{1,0:T(8,128)(2,1)S(1)} collective-permute-done((bf16[16,7296]{1,0:T(8,128)(2,1)S(1)}, bf16[16,7296]{1,0:T(8,128)(2,1)S(1)}, u32[]{:S(2)}, u32[]{:S(2)}) %collective-permute-start.1) | collective-permute-done | bytes 233504 | tf_op jit(solution)/shard_map/ppermute | solution.py:326
  19.2 1.7 %collective-permute-start.10 = (bf16[64,7296]{1,0:T(8,128)(2,1)S(1)}, bf16[64,7296]{1,0:T(8,128)(2,1)S(1)}, u32[]{:S(2)}, u32[]{:S(2)}) collective-permute-start(bf16[64,7296]{1,0:T(8,128)(2,1)S(1)} %pad_maximum_fusion.refs_0_.refs_2_), channel_id=1, source_target_pairs={{0,32},{4,12},{8,40},{12,20},{16,48},{20,28},{24,56},{28,4},{32,64... | collective-permute-start | bytes 2801672 | tf_op jit(solution)/shard_map/ppermute | solution.py:61
  20.9 2.2 %collective-permute-start.5 = (bf16[64,7296]{1,0:T(8,128)(2,1)S(1)}, bf16[64,7296]{1,0:T(8,128)(2,1)S(1)}, u32[]{:S(2)}, u32[]{:S(2)}) collective-permute-start(bf16[64,7296]{1,0:T(8,128)(2,1)S(1)} %pad_maximum_fusion.refs_0_.refs_2_), channel_id=1, source_target_pairs={{0,96},{4,28},{8,104},{12,4},{16,112},{20,12},{24,120},{28,20},{32... | collective-permute-start | bytes 2801672 | tf_op jit(solution)/shard_map/ppermute | solution.py:61
  23.1 11.2 %collective-permute-done.10.refs_0_.refs_7_ = bf16[64,7296]{1,0:T(8,128)(2,1)S(1)} collective-permute-done((bf16[64,7296]{1,0:T(8,128)(2,1)S(1)}, bf16[64,7296]{1,0:T(8,128)(2,1)S(1)}, u32[]{:S(2)}, u32[]{:S(2)}) %collective-permute-start.10) | collective-permute-done | bytes 933920 | tf_op jit(solution)/shard_map/ppermute | solution.py:61
  35.5 1.8 %collective-permute-start.22 = (bf16[64,7296]{1,0:T(8,128)(2,1)S(1)}, bf16[64,7296]{1,0:T(8,128)(2,1)S(1)}, u32[]{:S(2)}, u32[]{:S(2)}) collective-permute-start(bf16[64,7296]{1,0:T(8,128)(2,1)S(1)} %pad_maximum_fusion.refs_0_.refs_2_), channel_id=1, source_target_pairs={{0,24},{4,100},{8,0},{12,108},{16,8},{20,116},{24,16},{28,124},{32... | collective-permute-start | bytes 2801672 | tf_op jit(solution)/shard_map/ppermute | solution.py:65
  37.3 2.6 %collective-permute-start.12 = (bf16[32,7296]{1,0:T(8,128)(2,1)S(1)}, bf16[32,7296]{1,0:T(8,128)(2,1)S(1)}, u32[]{:S(2)}, u32[]{:S(2)}) collective-permute-start(bf16[32,7296]{1,0:T(8,128)(2,1)S(1)} %slice.43), channel_id=1, source_target_pairs={{0,96},{4,28},{8,104},{12,4},{16,112},{20,12},{24,120},{28,20},{32... | collective-permute-start | bytes 1400840 | tf_op jit(solution)/shard_map/ppermute | solution.py:61
  39.9 5.4 %collective-permute-done.11 = bf16[32,7296]{1,0:T(8,128)(2,1)S(1)} collective-permute-done((bf16[32,7296]{1,0:T(8,128)(2,1)S(1)}, bf16[32,7296]{1,0:T(8,128)(2,1)S(1)}, u32[]{:S(2)}, u32[]{:S(2)}) %collective-permute-start.11) | collective-permute-done | bytes 466976 | tf_op jit(solution)/shard_map/ppermute | solution.py:61
  45.3 2.9 %collective-permute-start.18 = (bf16[64,7296]{1,0:T(8,128)(2,1)S(1)}, bf16[64,7296]{1,0:T(8,128)(2,1)S(1)}, u32[]{:S(2)}, u32[]{:S(2)}) collective-permute-start(bf16[64,7296]{1,0:T(8,128)(2,1)S(1)} %collective-permute-done.10.refs_0_.refs_7_), channel_id=1, source_target_pairs={{0,24},{4,100},{8,0},{12,108},{16,8},{20,116},{24,16},{28,124},{32... | collective-permute-start | bytes 2801672 | tf_op jit(solution)/shard_map/ppermute | solution.py:65
  48.2 5.2 %collective-permute-done.21.refs_1_.refs_3_ = bf16[64,7296]{1,0:T(8,128)(2,1)S(1)} collective-permute-done((bf16[64,7296]{1,0:T(8,128)(2,1)S(1)}, bf16[64,7296]{1,0:T(8,128)(2,1)S(1)}, u32[]{:S(2)}, u32[]{:S(2)}) %collective-permute-start.21) | collective-permute-done | bytes 933920 | tf_op jit(solution)/shard_map/ppermute | solution.py:65
  53.5 2.7 %collective-permute-start.7 = (bf16[64,7296]{1,0:T(8,128)(2,1)S(1)}, bf16[64,7296]{1,0:T(8,128)(2,1)S(1)}, u32[]{:S(2)}, u32[]{:S(2)}) collective-permute-start(bf16[64,7296]{1,0:T(8,128)(2,1)S(1)} %collective-permute-done.5.refs_0_.refs_1_), channel_id=1, source_target_pairs={{0,24},{4,100},{8,0},{12,108},{16,8},{20,116},{24,16},{28,124},{32... | collective-permute-start | bytes 2801672 | tf_op jit(solution)/shard_map/ppermute | solution.py:65
  56.3 7.2 %collective-permute-done.17.refs_1_.refs_8_ = bf16[64,7296]{1,0:T(8,128)(2,1)S(1)} collective-permute-done((bf16[64,7296]{1,0:T(8,128)(2,1)S(1)}, bf16[64,7296]{1,0:T(8,128)(2,1)S(1)}, u32[]{:S(2)}, u32[]{:S(2)}) %collective-permute-start.17) | collective-permute-done | bytes 933920 | tf_op jit(solution)/shard_map/ppermute | solution.py:65
  63.5 1.5 %collective-permute-start.14 = (bf16[64,7296]{1,0:T(8,128)(2,1)S(1)}, bf16[64,7296]{1,0:T(8,128)(2,1)S(1)}, u32[]{:S(2)}, u32[]{:S(2)}) collective-permute-start(bf16[64,7296]{1,0:T(8,128)(2,1)S(1)} %constant_dynamic-update-slice_fusion.refs_5_.refs_6_), channel_id=1, source_target_pairs={{0,24},{4,100},{8,0},{12,108},{16,8},{20,116},{24,16},{28,124},{32... | collective-permute-start | bytes 2801672 | tf_op jit(solution)/shard_map/ppermute | solution.py:65
  65.1 8.3 %collective-permute-done.6.refs_1_.refs_2_ = bf16[64,7296]{1,0:T(8,128)(2,1)S(1)} collective-permute-done((bf16[64,7296]{1,0:T(8,128)(2,1)S(1)}, bf16[64,7296]{1,0:T(8,128)(2,1)S(1)}, u32[]{:S(2)}, u32[]{:S(2)}) %collective-permute-start.6) | collective-permute-done | bytes 933920 | tf_op jit(solution)/shard_map/ppermute | solution.py:65
  73.5 1.5 %collective-permute-start.24 = (bf16[32,7296]{1,0:T(8,128)(2,1)S(1)}, bf16[32,7296]{1,0:T(8,128)(2,1)S(1)}, u32[]{:S(2)}, u32[]{:S(2)}) collective-permute-start(bf16[32,7296]{1,0:T(8,128)(2,1)S(1)} %slice.49), channel_id=1, source_target_pairs={{0,24},{4,100},{8,0},{12,108},{16,8},{20,116},{24,16},{28,124},{32... | collective-permute-start | bytes 1400840 | tf_op jit(solution)/shard_map/ppermute | solution.py:65
  75.0 8.5 %collective-permute-done.13.refs_6_.refs_7_ = bf16[64,7296]{1,0:T(8,128)(2,1)S(1)} collective-permute-done((bf16[64,7296]{1,0:T(8,128)(2,1)S(1)}, bf16[64,7296]{1,0:T(8,128)(2,1)S(1)}, u32[]{:S(2)}, u32[]{:S(2)}) %collective-permute-start.13) | collective-permute-done | bytes 933920 | tf_op jit(solution)/shard_map/ppermute | solution.py:65
  85.2 3.3 %collective-permute-done.23.refs_3_.refs_5_ = bf16[32,7296]{1,0:T(8,128)(2,1)S(1)} collective-permute-done((bf16[32,7296]{1,0:T(8,128)(2,1)S(1)}, bf16[32,7296]{1,0:T(8,128)(2,1)S(1)}, u32[]{:S(2)}, u32[]{:S(2)}) %collective-permute-start.23) | collective-permute-done | bytes 466976 | tf_op jit(solution)/shard_map/ppermute | solution.py:65
  89.9 3.5 %collective-permute-done.19.refs_3_.refs_10_ = bf16[32,7296]{1,0:T(8,128)(2,1)S(1)} collective-permute-done((bf16[32,7296]{1,0:T(8,128)(2,1)S(1)}, bf16[32,7296]{1,0:T(8,128)(2,1)S(1)}, u32[]{:S(2)}, u32[]{:S(2)}) %collective-permute-start.19) | collective-permute-done | bytes 466976 | tf_op jit(solution)/shard_map/ppermute | solution.py:65
  93.5 1.5 %collective-permute-start.16 = (bf16[32,7296]{1,0:T(8,128)(2,1)S(1)}, bf16[32,7296]{1,0:T(8,128)(2,1)S(1)}, u32[]{:S(2)}, u32[]{:S(2)}) collective-permute-start(bf16[32,7296]{1,0:T(8,128)(2,1)S(1)} %slice.45), channel_id=1, source_target_pairs={{0,24},{4,100},{8,0},{12,108},{16,8},{20,116},{24,16},{28,124},{32... | collective-permute-start | bytes 1400840 | tf_op jit(solution)/shard_map/ppermute | solution.py:65
  97.5 5.5 %shard_map.72 = (f32[224,7168]{1,0:T(8,128)S(1)}, f32[224,7168]{1,0:T(8,128)S(1)}) custom-call(bf16[512,256]{1,0:T(8,128)(2,1)S(1)} %get-tuple-element.56.refs_0_, bf16[512,256]{1,0:T(8,128)(2,1)S(1)} %get-tuple-element.57.refs_1_, bf16[64,7296]{1,0:T(8,128)(2,1)S(1)} %pad_maximum_fusion.refs_0_.refs_2_, ...), custom_call_target="tpu_custom_call" | custom-call | flops 1644167168 | bytes 16777216 | tf_op jit(solution)/shard_map/pallas_call | solution.py:302
  103.3 2.2 %shard_map.73 = (bf16[1024,128]{1,0:T(8,128)(2,1)S(1)}, bf16[512,512]{1,0:T(8,128)(2,1)S(1)}, f32[16,128]{1,0:T(8,128)S(1)}) custom-call(bf16[64,7296]{1,0:T(8,128)(2,1)S(1)} %collective-permute-done.5.refs_0_.refs_1_, bf16[64,7296]{1,0:T(8,128)(2,1)S(1)} %collective-permute-done.6.refs_1_.refs_2_, ...), custom_call_target="tpu_custom_call" | custom-call | flops 1879048192 | bytes 8388608 | tf_op jit(solution)/shard_map/pallas_call | solution.py:163
  106.7 1.8 %collective-permute-start.26 = (bf16[1024,128]{1,0:T(8,128)(2,1)S(1)}, bf16[1024,128]{1,0:T(8,128)(2,1)S(1)}, u32[]{:S(2)}, u32[]{:S(2)}) collective-permute-start(bf16[1024,128]{1,0:T(8,128)(2,1)S(1)} %get-tuple-element.61.own), channel_id=1, source_target_pairs={{0,24},{4,28},{8,0},{12,4},{16,8},{20,12},{24,16},{28,20},{32,56},... | collective-permute-start | bytes 786440 | tf_op jit(solution)/shard_map/ppermute | solution.py:73
  112.5 3.4 %collective-permute-start.30 = (bf16[1024,128]{1,0:T(8,128)(2,1)S(1)}, bf16[1024,128]{1,0:T(8,128)(2,1)S(1)}, u32[]{:S(2)}, u32[]{:S(2)}) collective-permute-start(bf16[1024,128]{1,0:T(8,128)(2,1)S(1)} %get-tuple-element.61.own), channel_id=1, source_target_pairs={{0,64},{4,68},{8,72},{12,76},{16,80},{20,84},{24,88},{28,92},{32,9... | collective-permute-start | bytes 786440 | tf_op jit(solution)/shard_map/ppermute | solution.py:69
  115.9 3.1 %shard_map.74 = bf16[224,7168]{1,0:T(8,128)(2,1)S(1)} custom-call(bf16[512,512]{1,0:T(8,128)(2,1)S(1)} %get-tuple-element.62.refs_0_, bf16[64,7296]{1,0:T(8,128)(2,1)S(1)} %collective-permute-done.5.refs_0_.refs_1_, bf16[64,7296]{1,0:T(8,128)(2,1)S(1)} %collective-permute-done.6.refs_1_.refs_2_, bf16[64,7296]{1,0:T(8,128)(2,1)S(1)} %collective-permute-done.7.refs_2_.refs_3_, ...), custom_call_target="tpu_custom_call" | custom-call | flops 1644167168 | bytes 16777216 | tf_op jit(solution)/shard_map/pallas_call | solution.py:302
  119.0 3.5 %collective-permute-done.30.y2 = bf16[1024,128]{1,0:T(8,128)(2,1)S(1)} collective-permute-done((bf16[1024,128]{1,0:T(8,128)(2,1)S(1)}, bf16[1024,128]{1,0:T(8,128)(2,1)S(1)}, u32[]{:S(2)}, u32[]{:S(2)}) %collective-permute-start.30) | collective-permute-done | bytes 262176 | tf_op jit(solution)/shard_map/ppermute | solution.py:69
  123.3 4.4 %collective-permute-start.31 = (bf16[272,512]{1,0:T(8,128)(2,1)S(1)}, bf16[272,512]{1,0:T(8,128)(2,1)S(1)}, u32[]{:S(2)}, u32[]{:S(2)}) collective-permute-start(bf16[272,512]{1,0:T(8,128)(2,1)S(1)} %get-tuple-element.74), channel_id=1, source_target_pairs={{0,4},{4,0},{8,12},{12,8},{16,20},{20,16},{24,28},{28,24},{32,36},... | collective-permute-start | bytes 835592 | tf_op jit(solution)/shard_map/ppermute | solution.py:77
  129.7 2.4 %collective-permute-start.34 = (f32[64,512]{1,0:T(8,128)S(1)}, f32[64,512]{1,0:T(8,128)S(1)}, u32[]{:S(2)}, u32[]{:S(2)}) collective-permute-start(f32[64,512]{1,0:T(8,128)S(1)} %get-tuple-element.81), channel_id=1, source_target_pairs={{0,24},{4,28},{8,0},{12,4},{16,8},{20,12},{24,16},{28,20},{32,56},... | collective-permute-start | bytes 393224 | tf_op jit(solution)/shard_map/ppermute | solution.py:73
  132.1 2.5 %collective-permute-start.35 = (f32[64,512]{1,0:T(8,128)S(1)}, f32[64,512]{1,0:T(8,128)S(1)}, u32[]{:S(2)}, u32[]{:S(2)}) collective-permute-start(f32[64,512]{1,0:T(8,128)S(1)} %get-tuple-element.82), channel_id=1, source_target_pairs={{0,16},{4,20},{8,24},{12,28},{16,0},{20,4},{24,8},{28,12},{32,48},... | collective-permute-start | bytes 393224 | tf_op jit(solution)/shard_map/ppermute | solution.py:73
  134.7 5.3 %shard_map.77 = f32[1,224,7168]{2,1,0:T(8,128)} custom-call(bf16[512,512]{1,0:T(8,128)(2,1)S(1)} %get-tuple-element.62.refs_0_, bf16[64,7296]{1,0:T(8,128)(2,1)S(1)} %collective-permute-done.5.refs_0_.refs_1_, bf16[64,7296]{1,0:T(8,128)(2,1)S(1)} %collective-permute-done.6.refs_1_.refs_2_, bf16[64,7296]{1,0:T(8,128)(2,1)S(1)} %collective-permute-done.7.refs_2_.refs_3_, ...), custom_call_target="tpu_custom_call" | custom-call | flops 1644167168 | bytes 16777216 | tf_op jit(solution)/shard_map/pallas_call | solution.py:302
  (70 shorter events, 20.6 us)
Async XLA Ops:
  4.4 8.3 %collective-permute-start = (bf16[16,7296]{1,0:T(8,128)(2,1)S(1)}, bf16[16,7296]{1,0:T(8,128)(2,1)S(1)}, u32[]{:S(2)}, u32[]{:S(2)}) collective-permute-start(bf16[16,7296]{1,0:T(8,128)(2,1)S(1)} %get-tuple-element.46), channel_id=1, source_target_pairs={{0,1},{1,2},{2,3},{3,0},{4,5},{5,6},{6,7},{7,4},{8,9},{9,10},{10,1... | collective-permute-start | bytes 700424 | tf_op jit(solution)/shard_map/ppermute | solution.py:326
  6.5 12.5 %collective-permute-start.1 = (bf16[16,7296]{1,0:T(8,128)(2,1)S(1)}, bf16[16,7296]{1,0:T(8,128)(2,1)S(1)}, u32[]{:S(2)}, u32[]{:S(2)}) collective-permute-start(bf16[16,7296]{1,0:T(8,128)(2,1)S(1)} %get-tuple-element.47), channel_id=1, source_target_pairs={{0,2},{1,3},{2,0},{3,1},{4,6},{5,7},{6,4},{7,5},{8,10},{9,11},{10,... | collective-permute-start | bytes 700424 | tf_op jit(solution)/shard_map/ppermute | solution.py:326
  9.0 10.1 %collective-permute-start.2 = (bf16[16,7296]{1,0:T(8,128)(2,1)S(1)}, bf16[16,7296]{1,0:T(8,128)(2,1)S(1)}, u32[]{:S(2)}, u32[]{:S(2)}) collective-permute-start(bf16[16,7296]{1,0:T(8,128)(2,1)S(1)} %get-tuple-element.48), channel_id=1, source_target_pairs={{0,3},{1,0},{2,1},{3,2},{4,7},{5,4},{6,5},{7,6},{8,11},{9,8},{10,9... | collective-permute-start | bytes 700424 | tf_op jit(solution)/shard_map/ppermute | solution.py:326
  10.2 9.0 %collective-permute-start.3 = (bf16[64,7168]{1,0:T(8,128)(2,1)S(1)}, bf16[64,7168]{1,0:T(8,128)(2,1)S(1)}, u32[]{:S(2)}, u32[]{:S(2)}) collective-permute-start(bf16[64,7168]{1,0:T(8,128)(2,1)S(1)} %bitcast.4), channel_id=1, source_target_pairs={{0,4},{4,0},{8,12},{12,8},{16,20},{20,16},{24,28},{28,24},{32,36},... | collective-permute-start | bytes 2752520 | tf_op jit(solution)/shard_map/ppermute | solution.py:77
  19.2 15.1 %collective-permute-start.10 = (bf16[64,7296]{1,0:T(8,128)(2,1)S(1)}, bf16[64,7296]{1,0:T(8,128)(2,1)S(1)}, u32[]{:S(2)}, u32[]{:S(2)}) collective-permute-start(bf16[64,7296]{1,0:T(8,128)(2,1)S(1)} %pad_maximum_fusion.refs_0_.refs_2_), channel_id=1, source_target_pairs={{0,32},{4,12},{8,40},{12,20},{16,48},{20,28},{24,56},{28,4},{32,64... | collective-permute-start | bytes 2801672 | tf_op jit(solution)/shard_map/ppermute | solution.py:61
  20.9 16.4 %collective-permute-start.5 = (bf16[64,7296]{1,0:T(8,128)(2,1)S(1)}, bf16[64,7296]{1,0:T(8,128)(2,1)S(1)}, u32[]{:S(2)}, u32[]{:S(2)}) collective-permute-start(bf16[64,7296]{1,0:T(8,128)(2,1)S(1)} %pad_maximum_fusion.refs_0_.refs_2_), channel_id=1, source_target_pairs={{0,96},{4,28},{8,104},{12,4},{16,112},{20,12},{24,120},{28,20},{32... | collective-permute-start | bytes 2801672 | tf_op jit(solution)/shard_map/ppermute | solution.py:61
  34.3 11.0 %collective-permute-start.11 = (bf16[32,7296]{1,0:T(8,128)(2,1)S(1)}, bf16[32,7296]{1,0:T(8,128)(2,1)S(1)}, u32[]{:S(2)}, u32[]{:S(2)}) collective-permute-start(bf16[32,7296]{1,0:T(8,128)(2,1)S(1)} %slice.42), channel_id=1, source_target_pairs={{0,32},{4,12},{8,40},{12,20},{16,48},{20,28},{24,56},{28,4},{32,64... | collective-permute-start | bytes 1400840 | tf_op jit(solution)/shard_map/ppermute | solution.py:61
  34.4 19.1 %collective-permute-start.21 = (bf16[64,7296]{1,0:T(8,128)(2,1)S(1)}, bf16[64,7296]{1,0:T(8,128)(2,1)S(1)}, u32[]{:S(2)}, u32[]{:S(2)}) collective-permute-start(bf16[64,7296]{1,0:T(8,128)(2,1)S(1)} %pad_maximum_fusion.refs_0_.refs_2_), channel_id=1, source_target_pairs={{0,8},{4,36},{8,16},{12,44},{16,24},{20,52},{24,0},{28,60},{32,40}... | collective-permute-start | bytes 2801672 | tf_op jit(solution)/shard_map/ppermute | solution.py:65
  35.5 20.7 %collective-permute-start.22 = (bf16[64,7296]{1,0:T(8,128)(2,1)S(1)}, bf16[64,7296]{1,0:T(8,128)(2,1)S(1)}, u32[]{:S(2)}, u32[]{:S(2)}) collective-permute-start(bf16[64,7296]{1,0:T(8,128)(2,1)S(1)} %pad_maximum_fusion.refs_0_.refs_2_), channel_id=1, source_target_pairs={{0,24},{4,100},{8,0},{12,108},{16,8},{20,116},{24,16},{28,124},{32... | collective-permute-start | bytes 2801672 | tf_op jit(solution)/shard_map/ppermute | solution.py:65
  37.3 16.1 %collective-permute-start.12 = (bf16[32,7296]{1,0:T(8,128)(2,1)S(1)}, bf16[32,7296]{1,0:T(8,128)(2,1)S(1)}, u32[]{:S(2)}, u32[]{:S(2)}) collective-permute-start(bf16[32,7296]{1,0:T(8,128)(2,1)S(1)} %slice.43), channel_id=1, source_target_pairs={{0,96},{4,28},{8,104},{12,4},{16,112},{20,12},{24,120},{28,20},{32... | collective-permute-start | bytes 1400840 | tf_op jit(solution)/shard_map/ppermute | solution.py:61
  39.9 23.6 %collective-permute-start.17 = (bf16[64,7296]{1,0:T(8,128)(2,1)S(1)}, bf16[64,7296]{1,0:T(8,128)(2,1)S(1)}, u32[]{:S(2)}, u32[]{:S(2)}) collective-permute-start(bf16[64,7296]{1,0:T(8,128)(2,1)S(1)} %collective-permute-done.10.refs_0_.refs_7_), channel_id=1, source_target_pairs={{0,8},{4,36},{8,16},{12,44},{16,24},{20,52},{24,0},{28,60},{32,40}... | collective-permute-start | bytes 2801672 | tf_op jit(solution)/shard_map/ppermute | solution.py:65
  45.3 19.8 %collective-permute-start.18 = (bf16[64,7296]{1,0:T(8,128)(2,1)S(1)}, bf16[64,7296]{1,0:T(8,128)(2,1)S(1)}, u32[]{:S(2)}, u32[]{:S(2)}) collective-permute-start(bf16[64,7296]{1,0:T(8,128)(2,1)S(1)} %collective-permute-done.10.refs_0_.refs_7_), channel_id=1, source_target_pairs={{0,24},{4,100},{8,0},{12,108},{16,8},{20,116},{24,16},{28,124},{32... | collective-permute-start | bytes 2801672 | tf_op jit(solution)/shard_map/ppermute | solution.py:65
  53.5 20.0 %collective-permute-start.6 = (bf16[64,7296]{1,0:T(8,128)(2,1)S(1)}, bf16[64,7296]{1,0:T(8,128)(2,1)S(1)}, u32[]{:S(2)}, u32[]{:S(2)}) collective-permute-start(bf16[64,7296]{1,0:T(8,128)(2,1)S(1)} %collective-permute-done.5.refs_0_.refs_1_), channel_id=1, source_target_pairs={{0,8},{4,36},{8,16},{12,44},{16,24},{20,52},{24,0},{28,60},{32,40}... | collective-permute-start | bytes 2801672 | tf_op jit(solution)/shard_map/ppermute | solution.py:65
  53.5 21.5 %collective-permute-start.7 = (bf16[64,7296]{1,0:T(8,128)(2,1)S(1)}, bf16[64,7296]{1,0:T(8,128)(2,1)S(1)}, u32[]{:S(2)}, u32[]{:S(2)}) collective-permute-start(bf16[64,7296]{1,0:T(8,128)(2,1)S(1)} %collective-permute-done.5.refs_0_.refs_1_), channel_id=1, source_target_pairs={{0,24},{4,100},{8,0},{12,108},{16,8},{20,116},{24,16},{28,124},{32... | collective-permute-start | bytes 2801672 | tf_op jit(solution)/shard_map/ppermute | solution.py:65
  56.2 27.3 %collective-permute-start.13 = (bf16[64,7296]{1,0:T(8,128)(2,1)S(1)}, bf16[64,7296]{1,0:T(8,128)(2,1)S(1)}, u32[]{:S(2)}, u32[]{:S(2)}) collective-permute-start(bf16[64,7296]{1,0:T(8,128)(2,1)S(1)} %constant_dynamic-update-slice_fusion.refs_5_.refs_6_), channel_id=1, source_target_pairs={{0,8},{4,36},{8,16},{12,44},{16,24},{20,52},{24,0},{28,60},{32,40}... | collective-permute-start | bytes 2801672 | tf_op jit(solution)/shard_map/ppermute | solution.py:65
  63.5 21.6 %collective-permute-start.14 = (bf16[64,7296]{1,0:T(8,128)(2,1)S(1)}, bf16[64,7296]{1,0:T(8,128)(2,1)S(1)}, u32[]{:S(2)}, u32[]{:S(2)}) collective-permute-start(bf16[64,7296]{1,0:T(8,128)(2,1)S(1)} %constant_dynamic-update-slice_fusion.refs_5_.refs_6_), channel_id=1, source_target_pairs={{0,24},{4,100},{8,0},{12,108},{16,8},{20,116},{24,16},{28,124},{32... | collective-permute-start | bytes 2801672 | tf_op jit(solution)/shard_map/ppermute | solution.py:65
  65.0 23.4 %collective-permute-start.23 = (bf16[32,7296]{1,0:T(8,128)(2,1)S(1)}, bf16[32,7296]{1,0:T(8,128)(2,1)S(1)}, u32[]{:S(2)}, u32[]{:S(2)}) collective-permute-start(bf16[32,7296]{1,0:T(8,128)(2,1)S(1)} %slice.48), channel_id=1, source_target_pairs={{0,8},{4,36},{8,16},{12,44},{16,24},{20,52},{24,0},{28,60},{32,40}... | collective-permute-start | bytes 1400840 | tf_op jit(solution)/shard_map/ppermute | solution.py:65
  73.5 16.5 %collective-permute-start.24 = (bf16[32,7296]{1,0:T(8,128)(2,1)S(1)}, bf16[32,7296]{1,0:T(8,128)(2,1)S(1)}, u32[]{:S(2)}, u32[]{:S(2)}) collective-permute-start(bf16[32,7296]{1,0:T(8,128)(2,1)S(1)} %slice.49), channel_id=1, source_target_pairs={{0,24},{4,100},{8,0},{12,108},{16,8},{20,116},{24,16},{28,124},{32... | collective-permute-start | bytes 1400840 | tf_op jit(solution)/shard_map/ppermute | solution.py:65
  74.9 18.5 %collective-permute-start.19 = (bf16[32,7296]{1,0:T(8,128)(2,1)S(1)}, bf16[32,7296]{1,0:T(8,128)(2,1)S(1)}, u32[]{:S(2)}, u32[]{:S(2)}) collective-permute-start(bf16[32,7296]{1,0:T(8,128)(2,1)S(1)} %slice.46), channel_id=1, source_target_pairs={{0,8},{4,36},{8,16},{12,44},{16,24},{20,52},{24,0},{28,60},{32,40}... | collective-permute-start | bytes 1400840 | tf_op jit(solution)/shard_map/ppermute | solution.py:65
  83.5 12.7 %collective-permute-start.20 = (bf16[32,7296]{1,0:T(8,128)(2,1)S(1)}, bf16[32,7296]{1,0:T(8,128)(2,1)S(1)}, u32[]{:S(2)}, u32[]{:S(2)}) collective-permute-start(bf16[32,7296]{1,0:T(8,128)(2,1)S(1)} %slice.47), channel_id=1, source_target_pairs={{0,24},{4,100},{8,0},{12,108},{16,8},{20,116},{24,16},{28,124},{32... | collective-permute-start | bytes 1400840 | tf_op jit(solution)/shard_map/ppermute | solution.py:65
  85.1 17.9 %collective-permute-start.8 = (bf16[32,7296]{1,0:T(8,128)(2,1)S(1)}, bf16[32,7296]{1,0:T(8,128)(2,1)S(1)}, u32[]{:S(2)}, u32[]{:S(2)}) collective-permute-start(bf16[32,7296]{1,0:T(8,128)(2,1)S(1)} %slice.40), channel_id=1, source_target_pairs={{0,8},{4,36},{8,16},{12,44},{16,24},{20,52},{24,0},{28,60},{32,40}... | collective-permute-start | bytes 1400840 | tf_op jit(solution)/shard_map/ppermute | solution.py:65
  88.5 14.5 %collective-permute-start.9 = (bf16[32,7296]{1,0:T(8,128)(2,1)S(1)}, bf16[32,7296]{1,0:T(8,128)(2,1)S(1)}, u32[]{:S(2)}, u32[]{:S(2)}) collective-permute-start(bf16[32,7296]{1,0:T(8,128)(2,1)S(1)} %slice.41), channel_id=1, source_target_pairs={{0,24},{4,100},{8,0},{12,108},{16,8},{20,116},{24,16},{28,124},{32... | collective-permute-start | bytes 1400840 | tf_op jit(solution)/shard_map/ppermute | solution.py:65
  89.9 13.4 %collective-permute-start.15 = (bf16[32,7296]{1,0:T(8,128)(2,1)S(1)}, bf16[32,7296]{1,0:T(8,128)(2,1)S(1)}, u32[]{:S(2)}, u32[]{:S(2)}) collective-permute-start(bf16[32,7296]{1,0:T(8,128)(2,1)S(1)} %slice.44), channel_id=1, source_target_pairs={{0,8},{4,36},{8,16},{12,44},{16,24},{20,52},{24,0},{28,60},{32,40}... | collective-permute-start | bytes 1400840 | tf_op jit(solution)/shard_map/ppermute | solution.py:65
  93.5 9.9 %collective-permute-start.16 = (bf16[32,7296]{1,0:T(8,128)(2,1)S(1)}, bf16[32,7296]{1,0:T(8,128)(2,1)S(1)}, u32[]{:S(2)}, u32[]{:S(2)}) collective-permute-start(bf16[32,7296]{1,0:T(8,128)(2,1)S(1)} %slice.45), channel_id=1, source_target_pairs={{0,24},{4,100},{8,0},{12,108},{16,8},{20,116},{24,16},{28,124},{32... | collective-permute-start | bytes 1400840 | tf_op jit(solution)/shard_map/ppermute | solution.py:65
  106.7 12.3 %collective-permute-start.26 = (bf16[1024,128]{1,0:T(8,128)(2,1)S(1)}, bf16[1024,128]{1,0:T(8,128)(2,1)S(1)}, u32[]{:S(2)}, u32[]{:S(2)}) collective-permute-start(bf16[1024,128]{1,0:T(8,128)(2,1)S(1)} %get-tuple-element.61.own), channel_id=1, source_target_pairs={{0,24},{4,28},{8,0},{12,4},{16,8},{20,12},{24,16},{28,20},{32,56},... | collective-permute-start | bytes 786440 | tf_op jit(solution)/shard_map/ppermute | solution.py:73
  108.4 10.6 %collective-permute-start.27 = (bf16[1024,128]{1,0:T(8,128)(2,1)S(1)}, bf16[1024,128]{1,0:T(8,128)(2,1)S(1)}, u32[]{:S(2)}, u32[]{:S(2)}) collective-permute-start(bf16[1024,128]{1,0:T(8,128)(2,1)S(1)} %get-tuple-element.61.own), channel_id=1, source_target_pairs={{0,16},{4,20},{8,24},{12,28},{16,0},{20,4},{24,8},{28,12},{32,48},... | collective-permute-start | bytes 786440 | tf_op jit(solution)/shard_map/ppermute | solution.py:73
  109.8 9.2 %collective-permute-start.28 = (bf16[1024,128]{1,0:T(8,128)(2,1)S(1)}, bf16[1024,128]{1,0:T(8,128)(2,1)S(1)}, u32[]{:S(2)}, u32[]{:S(2)}) collective-permute-start(bf16[1024,128]{1,0:T(8,128)(2,1)S(1)} %get-tuple-element.61.own), channel_id=1, source_target_pairs={{0,32},{4,36},{8,40},{12,44},{16,48},{20,52},{24,56},{28,60},{32,6... | collective-permute-start | bytes 786440 | tf_op jit(solution)/shard_map/ppermute | solution.py:69
  111.1 7.9 %collective-permute-start.29 = (bf16[1024,128]{1,0:T(8,128)(2,1)S(1)}, bf16[1024,128]{1,0:T(8,128)(2,1)S(1)}, u32[]{:S(2)}, u32[]{:S(2)}) collective-permute-start(bf16[1024,128]{1,0:T(8,128)(2,1)S(1)} %get-tuple-element.61.own), channel_id=1, source_target_pairs={{0,96},{4,100},{8,104},{12,108},{16,112},{20,116},{24,120},{28,124... | collective-permute-start | bytes 786440 | tf_op jit(solution)/shard_map/ppermute | solution.py:69
  112.5 10.0 %collective-permute-start.30 = (bf16[1024,128]{1,0:T(8,128)(2,1)S(1)}, bf16[1024,128]{1,0:T(8,128)(2,1)S(1)}, u32[]{:S(2)}, u32[]{:S(2)}) collective-permute-start(bf16[1024,128]{1,0:T(8,128)(2,1)S(1)} %get-tuple-element.61.own), channel_id=1, source_target_pairs={{0,64},{4,68},{8,72},{12,76},{16,80},{20,84},{24,88},{28,92},{32,9... | collective-permute-start | bytes 786440 | tf_op jit(solution)/shard_map/ppermute | solution.py:69
  129.4 10.6 %collective-permute-start.33 = (f32[64,512]{1,0:T(8,128)S(1)}, f32[64,512]{1,0:T(8,128)S(1)}, u32[]{:S(2)}, u32[]{:S(2)}) collective-permute-start(f32[64,512]{1,0:T(8,128)S(1)} %get-tuple-element.80), channel_id=1, source_target_pairs={{0,8},{4,12},{8,16},{12,20},{16,24},{20,28},{24,0},{28,4},{32,40},... | collective-permute-start | bytes 393224 | tf_op jit(solution)/shard_map/ppermute | solution.py:73
  129.7 10.3 %collective-permute-start.34 = (f32[64,512]{1,0:T(8,128)S(1)}, f32[64,512]{1,0:T(8,128)S(1)}, u32[]{:S(2)}, u32[]{:S(2)}) collective-permute-start(f32[64,512]{1,0:T(8,128)S(1)} %get-tuple-element.81), channel_id=1, source_target_pairs={{0,24},{4,28},{8,0},{12,4},{16,8},{20,12},{24,16},{28,20},{32,56},... | collective-permute-start | bytes 393224 | tf_op jit(solution)/shard_map/ppermute | solution.py:73
  132.1 7.9 %collective-permute-start.35 = (f32[64,512]{1,0:T(8,128)S(1)}, f32[64,512]{1,0:T(8,128)S(1)}, u32[]{:S(2)}, u32[]{:S(2)}) collective-permute-start(f32[64,512]{1,0:T(8,128)S(1)} %get-tuple-element.82), channel_id=1, source_target_pairs={{0,16},{4,20},{8,24},{12,28},{16,0},{20,4},{24,8},{28,12},{32,48},... | collective-permute-start | bytes 393224 | tf_op jit(solution)/shard_map/ppermute | solution.py:73
  (7 other events, 46.9 us)
